TPU v7x, 32 devices: a whole 2x2x4 slice. The times are simulated.
32 devices in a mesh: grp: 2 (over y), field: 4 (over z), pair: 4 (over x, core).
Axes of the slice: x: 2, y: 2, z: 4, core: 2. Of those that a mesh axis runs over, the one named last changes fastest.
Arguments:
- cholesky_tensor: float32 [1536, 9216], P(('grp', 'field'), 'pair'), parts along dimension 0, may hold values from -0.0625 to 0.0625
- green_function: float32 [2, 8192, 9216], P(None, ('grp', 'field'), 'pair'), parts along dimension 1, may hold values from -6 to 6
- mean_field: float32 [2, 1536], P(None, 'grp'), parts along dimension 1, may hold values from -6 to 6
- field_noise: float32 [8192, 768], P(('grp', 'field')), parts along dimension 0, may hold values from -6 to 6
Outputs:
- capped_bias: float32 [2, 8192, 768], P(None, ('grp', 'field', 'pair')), parts along dimension 1
- one_body: float32 [8192, 2, 9216], P(('grp', 'field'), None, 'pair'), parts along dimension 0
There are 2 independent parts, one for each index of `grp`. A program takes and returns all parts, laid end to end along the dimension named above; each array names one. Nothing has to cross between parts.
All inputs are finite; a program needn't handle non-finite values.
Results may differ from a plain program's by a relative error of at most 0.000059.
Values sent between devices are 32-bit elements; how exact they have to be, the bound alone decides.
No kernel may reach another device: no remote copies, remote signals or barrier semaphores. Data moves between devices by JAX's collectives and lax.ppermute only.
A program may use at most 128 MiB of HBM per device.

v0:
```python
import math

import jax
import jax.numpy as jnp
from jax import lax
from jax.sharding import PartitionSpec as P

NF = 768
NP = 9216


def per_device(cholesky_tensor, green_function, mean_field, field_noise):
    operator_scale = math.sqrt(NP / NF)
    partial_bias = jnp.einsum(
        "cwp,fp->cwf",
        green_function,
        lax.all_gather(cholesky_tensor, "field", axis=0, tiled=True),
        precision=lax.Precision.HIGHEST,
    )
    mean_shift = mean_field[:, None, :]
    walker_part = lax.psum_scatter(partial_bias, "pair", scatter_dimension=1, tiled=True)
    capped_share = 2.0 * jnp.tanh((walker_part - mean_shift) / 2.0)
    capped_all = lax.all_gather(capped_share, "pair", axis=1, tiled=True)
    fields = jnp.stack([field_noise - capped_all[0], -capped_all[1]], axis=1)
    summed_operator = jnp.einsum(
        "wcf,fp->wcp",
        fields,
        lax.all_gather(cholesky_tensor, "field", axis=0, tiled=True),
        precision=lax.Precision.HIGHEST,
    )
    one_body = operator_scale * summed_operator
    return (capped_share, one_body)


def solution(mesh):
    return jax.shard_map(
        per_device,
        mesh=mesh,
        in_specs=(
            P(("grp", "field"), "pair"),
            P(None, ("grp", "field"), "pair"),
            P(None, "grp"),
            P(("grp", "field"), None),
        ),
        out_specs=(P(None, ("grp", "field", "pair"), None), P(("grp", "field"), None, "pair")),
        check_vma=False,
    )
```

profile of v0, /device:TPU:0, one launch (start us, length us, event | category | flops | bytes accessed | tf_op | source)
XLA Modules:
  0.0 419.4 jit_solution(8350141060765599660)
XLA Ops:
  7.2 0.0 all-gather.3.cloned.1.call-start
  7.2 0.7 all-gather.3.cloned.1.call-update
  7.9 0.0 reduce-scatter.2.cloned.1.call-start
  7.9 132.6 %all-gather.3.cloned.1.call-done = f32[768,2304]{1,0:T(8,128)} async-done(((f32[192,2304]{1,0:T(8,128)}), f32[768,2304]{1,0:T(8,128)}) %all-gather.3.cloned.1.call-update) | async-done | bytes 7077904 | tf_op jit(solution)/shard_map/all_gather | solution.py:17
  140.5 52.7 %fusion.1 = f32[2,1024,768]{2,1,0:T(8,128)} fusion(f32[2,1024,2304]{2,1,0:T(8,128)} %param.5, f32[768,2304]{1,0:T(8,128)} %all-gather.3.cloned.1.call-done), kind=kOutput, calls=%fused_computation.2 | convolution fusion | flops 43486543872 | bytes 32243712 | tf_op jit(solution)/shard_map/cwp,fp->cwf/dot_general | solution.py:14
  193.2 0.0 copy-start.2
  193.2 0.0 reduce-scatter.2.cloned.1.call-update
  193.2 0.0 copy-start.1
  193.2 0.0 all-gather.5.cloned.1.call-start
  193.3 56.7 %reduce-scatter.2.cloned.1.call-done = f32[2,256,768]{2,1,0:T(8,128)} async-done(((f32[2,1024,768]{2,1,0:T(8,128)}), f32[2,256,768]{2,1,0:T(8,128)}) %reduce-scatter.2.cloned.1.call-update) | async-done | bytes 1572880 | tf_op jit(solution)/shard_map/reduce_scatter | solution.py:21
  249.9 0.0 copy-done.2
  249.9 2.8 tanh_multiply_fusion
  252.7 0.0 all-gather.5.cloned.1.call-update
  252.7 46.5 %all-gather.5.cloned.1.call-done = f32[2,1024,768]{2,1,0:T(8,128)} async-done(((f32[2,256,768]{2,1,0:T(8,128)}), f32[2,1024,768]{2,1,0:T(8,128)}) %all-gather.5.cloned.1.call-update) | async-done | bytes 6291472 | tf_op jit(solution)/shard_map/all_gather | solution.py:23
  299.3 0.0 copy-start
  299.3 2.2 fusion.6
  301.5 0.0 copy-done.1
  301.5 1.5 copy-done
  303.0 0.6 fusion.8
  303.6 52.0 %convolution_multiply_fusion = f32[1024,2,2304]{2,0,1:T(8,128)S(1)} fusion(f32[768,2304]{1,0:T(8,128)} %all-gather.3.cloned.1.call-done, f32[1024,1,768]{2,0,1:T(8,128)S(1)} %fusion.6, f32[1024,1,768]{2,0,1:T(8,128)S(1)} %fusion.8), kind=kOutput, calls=%fused_computation | convolution fusion | flops 43492835328 | bytes 32243712 | tf_op jit(solution)/shard_map/wcf,fp->wcp/dot_general | solution.py:25
  355.6 57.3 %copy.6 = f32[1024,2,2304]{2,1,0:T(2,128)} copy(f32[1024,2,2304]{2,0,1:T(8,128)S(1)} %convolution_multiply_fusion) | data formatting | bytes 37748736
Async XLA Ops:
  7.2 133.3 %all-gather.3.cloned.1.call-start = ((), (), s32[]{:S(2)}) async-start(), calls=%async_computation.1 | async-start | bytes 8847360 | tf_op jit(solution)/shard_map/all_gather | solution.py:17
  7.9 242.0 %reduce-scatter.2.cloned.1.call-start = ((), (), s32[]{:S(2)}) async-start(), calls=%async_computation.2 | async-start | bytes 7864320 | tf_op jit(solution)/shard_map/reduce_scatter | solution.py:21
  193.2 56.7 %copy-start.2 = (f32[2,768]{1,0:T(2,128)S(1)}, f32[2,768]{1,0:T(2,128)}, u32[]{:S(2)}) copy-start(f32[2,768]{1,0:T(2,128)} %param.6) | copy-start | bytes 18436
  193.2 108.3 %copy-start.1 = (f32[1024,768]{1,0:T(8,128)S(1)}, f32[1024,768]{1,0:T(8,128)}, u32[]{:S(2)}) copy-start(f32[1024,768]{1,0:T(8,128)} %param.7) | copy-start | bytes 9437188
  193.2 106.0 %all-gather.5.cloned.1.call-start = ((), (), s32[]{:S(2)}) async-start(), calls=%async_computation.3 | async-start | bytes 7864320 | tf_op jit(solution)/shard_map/all_gather | solution.py:23
  299.3 3.7 copy-start
Sparse Core Ops, SparseCore 0:
  9.6 130.8 all-gather.2
  193.3 56.5 reduce-scatter.1
  252.8 46.3 all-gather.4
where the time goes:
time: 420 us; the launch traced here: 419 us
  waiting for transfers between devices  236 us (56%)
  matrix products  105 us (25%)
  local copies, waits for them, and re-layouts  58.8 us (14%)
  between operations  13.8 us (3%)
  other arithmetic  5.65 us (1%)
    all_gather x1, waiting for transfers between devices, per_device(): lax.all_gather(cholesky_tensor, 'field', axis=0, tiled=True)  133 us
    unnamed x7, local copies, waits for them, and re-layouts  58.8 us
    reduce_scatter x1, waiting for transfers between devices, per_device(): lax.psum_scatter(partial_bias, 'pair', scatter_dimension=1, tiled=True)  56.7 us
    dot_general x1, matrix products, per_device(): jnp.einsum('cwp,fp->cwf', green_function, lax.all_gather(cholesky_tensor,...  52.7 us
    dot_general x1, matrix products, per_device(): jnp.einsum('wcf,fp->wcp', fields, lax.all_gather(cholesky_tensor, 'field'...  52 us
    all_gather x1, waiting for transfers between devices, per_device(): capped_all = lax.all_gather(capped_share, 'pair', axis=1, tiled=True)  46.5 us
  transfers between devices with their start and end apart: 3, of which 3 were waited for; matrix products, arithmetic and copies ran while one was open for 0% of the time, Pallas kernels for 0%

commit v1 on v0

v1 whole, which is shorter than its diff:
```python
import functools
import math

import jax
import jax.numpy as jnp
from jax import lax
from jax.experimental import pallas as pl
from jax.experimental.pallas import tpu as pltpu
from jax.sharding import PartitionSpec as P

CORES = 2
KERNEL_VMEM = 24 * 1024 * 1024
ROWS_DOT = (((1,), (1,)), ((), ()))
DOT = (((1,), (0,)), ((), ()))
WHOLE = pl.BlockSpec(memory_space=pltpu.VMEM)


def split(x):
    high = x.astype(jnp.bfloat16)
    return high, (x - high.astype(jnp.float32)).astype(jnp.bfloat16)


def params():
    return pltpu.CompilerParams(vmem_limit_bytes=KERNEL_VMEM)


def stacked(parts):
    return parts[0] if len(parts) == 1 else jnp.concatenate(parts, 0)


def split_green_kernel(green_ref, high_ref, low_ref):
    at = (pl.program_id(0), pl.program_id(1), pl.program_id(2))
    high_ref[at], low_ref[at] = split(green_ref[0, 0, 0])


def split_green(green):
    channels, across, cores, rows, pairs = green.shape
    return pl.pallas_call(
        split_green_kernel,
        out_shape=[pltpu.VMEM(green.shape, jnp.bfloat16)] * 2,
        grid=(channels, across, cores),
        in_specs=[pl.BlockSpec((1, 1, 1, rows, pairs), lambda c, x, h: (c, x, h, 0, 0))],
        out_specs=[WHOLE, WHOLE],
        compiler_params=params(),
        cost_estimate=pl.CostEstimate(flops=3 * green.size, bytes_accessed=4 * green.size, transcendentals=0),
        name="split_green",
    )(green)


def bias_kernel(n, half_ref, high_ref, low_ref, *refs):
    parts, out_ref, chol = refs[:n], refs[n], refs[n + 1]
    fields = chol.shape[0] // 2
    chol[:fields], chol[fields:] = split(stacked([part[...] for part in parts]))
    channels, across = high_ref.shape[:2]
    half = half_ref[0]
    for c in range(channels):
        for x in range(across):
            both = lax.dot_general(chol[...], high_ref[c, x, half], ROWS_DOT, preferred_element_type=jnp.float32)
            cross = lax.dot_general(chol[:fields], low_ref[c, x, half], ROWS_DOT, preferred_element_type=jnp.float32)
            out_ref[c, x] = both[:fields] + (both[fields:] + cross)


def bias_of(high, low, parts, half):
    channels, across, _, rows, pairs = high.shape
    fields = sum(part.shape[0] for part in parts)
    return pl.pallas_call(
        functools.partial(bias_kernel, len(parts)),
        out_shape=jax.ShapeDtypeStruct((channels, across, fields, rows), jnp.float32),
        in_specs=[pl.BlockSpec(memory_space=pltpu.SMEM)] + [WHOLE] * (2 + len(parts)),
        out_specs=WHOLE,
        scratch_shapes=[pltpu.VMEM((2 * fields, pairs), jnp.bfloat16)],
        compiler_params=params(),
        cost_estimate=pl.CostEstimate(
            flops=6 * channels * across * rows * pairs * fields, bytes_accessed=4 * fields * pairs, transcendentals=0
        ),
        name="bias",
    )(half, high, low, *parts)


def stack_chol(out, parts):
    high, low = split(stacked([part[...] for part in parts]))
    depth = high.shape[0]
    out[:depth] = high
    out[depth : 2 * depth] = high
    out[2 * depth :] = low


def stack_fields(capped, noise):
    first = stacked(noise) - stacked([c[0] for c in capped])
    second = -stacked([c[1] for c in capped])
    high, low = split(jnp.concatenate([first, second], 1))
    return jnp.concatenate([high, low, high], 0).T


def noise_specs(unit, lanes, at):
    def spec(step, shard):
        return pl.BlockSpec((1, 1, shard, lanes), lambda x, b, s: (s[1 + step], *at(x, b, s)))

    return [spec(step, shard) for step, _, _, shard in unit]


def noise_pieces(refs, unit):
    return [ref[0, 0, start : start + rows] for ref, (_, start, rows, _) in zip(refs, unit)]


def accumulate_kernel(n, m, unit, old, s_ref, *refs):
    mine, other, noise, chol = refs[:n], refs[n : 2 * n], refs[2 * n : 2 * n + m], refs[2 * n + m : 2 * n + 2 * m]
    out_ref, stack = refs[-2], refs[-1]
    x, core = pl.program_id(0), pl.program_id(1)

    @pl.when((x == 0) & (core == 0))
    def _():
        stack_chol(stack, chol)

    own = core == s_ref[0]
    capped = [jnp.where(own, a[:, 0], b[:, 0]) for a, b in zip(mine, other)]
    sums = lax.dot_general(
        stack_fields(capped, noise_pieces(noise, unit)), stack[...], DOT, preferred_element_type=jnp.float32
    )
    rows = sums.shape[0] // 2
    for c in range(2):
        term = sums[c * rows : (c + 1) * rows]
        out_ref[c, x, core] = term + refs[-3][c, x, core] if old else term


def accumulate(mine, other, noise, chol, unit, scalars, prior, sizes):
    across, rows, pairs = sizes
    depth = sum(part.shape[0] for part in chol)
    in_specs = [pl.BlockSpec((2, 1, *part.shape[2:]), lambda x, b, s: (0, x, 0, 0)) for part in (*mine, *other)]
    in_specs += noise_specs(unit, rows, lambda x, b, s: (x * CORES + b, 0, 0))
    in_specs += [pl.BlockSpec(part.shape, lambda x, b, s: (0, 0)) for part in chol]
    operands = [scalars, *mine, *other, *([noise] * len(unit)), *chol]
    aliases = {}
    if prior is not None:
        in_specs.append(WHOLE)
        aliases = {len(operands): 0}
        operands.append(prior)
    return pl.pallas_call(
        functools.partial(accumulate_kernel, len(mine), len(unit), unit, prior is not None),
        out_shape=pltpu.VMEM((2, across, CORES, rows, pairs), jnp.float32),
        grid_spec=pltpu.PrefetchScalarGridSpec(
            num_scalar_prefetch=1,
            grid=(across, CORES),
            in_specs=in_specs,
            out_specs=WHOLE,
            scratch_shapes=[pltpu.VMEM((3 * depth, pairs), jnp.bfloat16)],
        ),
        input_output_aliases=aliases,
        compiler_params=params(),
        cost_estimate=pl.CostEstimate(
            flops=12 * across * CORES * rows * pairs * depth, bytes_accessed=4 * depth * pairs, transcendentals=0
        ),
        name="accumulate",
    )(*operands)


def stack_kernel(*refs):
    stack_chol(refs[-1], refs[:-1])


def stack_of(chol):
    depth = sum(part.shape[0] for part in chol)
    return pl.pallas_call(
        stack_kernel,
        out_shape=pltpu.VMEM((3 * depth, chol[0].shape[1]), jnp.bfloat16),
        in_specs=[WHOLE] * len(chol),
        out_specs=WHOLE,
        compiler_params=params(),
        name="stack_cholesky",
    )(*chol)


def finish_kernel(n, m, unit, scale, s_ref, *refs):
    capped, noise = refs[:n], refs[n : n + m]
    stack, prior, out_ref = refs[n + m], refs[n + m + 1], refs[-1]
    x, b = pl.program_id(0), pl.program_id(1)
    sums = lax.dot_general(
        stack_fields([part[:, 0] for part in capped], noise_pieces(noise, unit)),
        stack[...],
        DOT,
        preferred_element_type=jnp.float32,
    )
    rows = sums.shape[0] // 2
    at = pl.ds(pl.multiple_of(b * rows, rows), rows)
    for c in range(2):
        out_ref[0, 0, :, c, :] = scale * (prior[c, x, s_ref[0], at, :] + sums[c * rows : (c + 1) * rows])


def finish(capped, noise, stack, prior, unit, scalars, scale, earlier, block):
    _, across, _, rows, pairs = prior.shape
    blocks = rows // block
    in_specs = [pl.BlockSpec((2, 1, part.shape[2], block), lambda x, b, s: (0, x, 0, b)) for part in capped]
    in_specs += noise_specs(unit, block, lambda x, b, s: (x * CORES + s[0], 0, b))
    in_specs += [WHOLE, WHOLE]
    operands = [scalars, *capped, *([noise] * len(unit)), stack, prior]
    aliases = {}
    if earlier is not None:
        in_specs.append(pl.BlockSpec(memory_space=pl.ANY))
        aliases = {len(operands): 0}
        operands.append(earlier)
    return pl.pallas_call(
        functools.partial(finish_kernel, len(capped), len(unit), unit, scale),
        out_shape=jax.ShapeDtypeStruct((across, CORES, rows, 2, pairs), jnp.float32),
        grid_spec=pltpu.PrefetchScalarGridSpec(
            num_scalar_prefetch=1,
            grid=(across, blocks),
            in_specs=in_specs,
            out_specs=pl.BlockSpec((1, 1, block, 2, pairs), lambda x, b, s: (x, s[0], b, 0, 0)),
        ),
        input_output_aliases=aliases,
        compiler_params=params(),
        cost_estimate=pl.CostEstimate(
            flops=4 * across * rows * pairs * stack.shape[0], bytes_accessed=8 * across * rows * pairs, transcendentals=0
        ),
        name="finish",
    )(*operands)


def per_device(ring_size, pair_size, cholesky_tensor, green_function, mean_field, field_noise):
    shard, pairs = cholesky_tensor.shape
    channels, walkers, _ = green_function.shape
    fields = ring_size * shard
    total_pairs = pair_size * pairs
    across = pair_size // CORES
    rows = walkers // pair_size

    place, member = lax.axis_index("field"), lax.axis_index("pair")
    core, chip = member % CORES, member // CORES
    owners = [(place - step) % ring_size for step in range(ring_size)]
    mine_scalars = jnp.stack([core, *owners]).astype(jnp.int32)
    other_scalars = jnp.stack([1 - core, *owners]).astype(jnp.int32)
    own_half, mate_half = mine_scalars[:1], other_scalars[:1]

    ring = [(i, (i + 1) % ring_size) for i in range(ring_size)]
    mates = [(i, i ^ 1) for i in range(pair_size)]

    cut = 2 * shard // 3
    cuts = [(0, cut), (cut, shard - cut)] if cut % 16 == 0 and (shard - cut) % 16 == 0 else [(0, shard)]
    held = [[lax.slice_in_dim(cholesky_tensor, start, start + n, axis=0) for start, n in cuts]]
    for _ in range(ring_size - 1):
        held.append([lax.ppermute(part, "field", ring) for part in held[-1]])
    held[0] = [cholesky_tensor]
    pieces = {0: [(0, 0, shard, shard)]}
    for step in range(1, ring_size):
        pieces[step] = [(step, start, n, shard) for start, n in cuts]

    together = 1
    while together * shard % 16 or (ring_size > 8 and together * 8 < ring_size):
        together *= 2
    units = []
    for first in range(0, ring_size, together):
        steps = range(first, min(first + together, ring_size))
        unit = [(piece, part) for step in steps for piece, part in zip(pieces[step], held[step])]
        last = first + together >= ring_size
        units += [[one] for one in unit] if last and together == 1 else [unit]
    final = len(cuts) if together == 1 else 1

    green = green_function.reshape(channels, across, CORES, rows, pairs)
    high, low = split_green(green)
    noise = field_noise.reshape(pair_size, rows, ring_size, shard).transpose(2, 0, 3, 1)
    means = mean_field.reshape(channels, ring_size, shard)

    def mean_of(piece):
        step, start, n, _ = piece
        return lax.dynamic_index_in_dim(means, owners[step], 1, keepdims=False)[:, start : start + n]

    def capped_of(unit):
        parts = [part for _, part in unit]
        sent = bias_of(high, low, parts, mate_half)
        arrived = lax.ppermute(sent, "pair", mates)
        sums = bias_of(high, low, parts, own_half) + arrived
        reach = CORES
        while reach < pair_size:
            sums = sums + lax.ppermute(sums, "pair", [(i, i ^ reach) for i in range(pair_size)])
            reach *= 2
        mean = jnp.concatenate([mean_of(piece) for piece, _ in unit], 1)[:, None, :, None]
        mine = 2.0 * jnp.tanh((sums - mean) / 2.0)
        return mine, lax.ppermute(mine, "pair", mates)

    capped = [capped_of(unit) for unit in units]

    sizes = (across, rows, pairs)
    operator = None
    early = units[:-final]
    for first in range(0, len(early), 2):
        group = range(first, min(first + 2, len(early)))
        operator = accumulate(
            [capped[u][0] for u in group],
            [capped[u][1] for u in group],
            noise,
            [part for u in group for _, part in units[u]],
            [piece for u in group for piece, _ in units[u]],
            mine_scalars,
            operator,
            sizes,
        )
    late = range(len(early), len(units))
    stack = stack_of([part for u in late for _, part in units[u]])
    late_pieces = [piece for u in late for piece, _ in units[u]]
    scale = math.sqrt(total_pairs / fields)
    block = rows // 2 if rows % 256 == 0 else rows
    one_body = finish(
        [capped[u][0] for u in late], noise, stack, operator, late_pieces, mine_scalars, scale, None, block
    )
    one_body = finish(
        [capped[u][1] for u in late], noise, stack, operator, late_pieces, other_scalars, scale, one_body, block
    )

    share = jnp.zeros((channels, fields, rows), jnp.float32)
    for unit, (mine, _) in zip(units, capped):
        own = lax.dynamic_index_in_dim(mine, chip, 1, keepdims=False)
        at = 0
        for (step, start, n, _), _ in unit:
            part = own[:, at : at + n]
            share = lax.dynamic_update_slice_in_dim(share, part, owners[step] * shard + start, axis=1)
            at += n
    return (share.transpose(0, 2, 1), one_body.reshape(walkers, channels, pairs))


def solution(mesh):
    return jax.shard_map(
        functools.partial(per_device, mesh.shape["field"], mesh.shape["pair"]),
        mesh=mesh,
        in_specs=(
            P(("grp", "field"), "pair"),
            P(None, ("grp", "field"), "pair"),
            P(None, "grp"),
            P(("grp", "field"), None),
        ),
        out_specs=(P(None, ("grp", "field", "pair"), None), P(("grp", "field"), None, "pair")),
        check_vma=False,
    )
```

time: 420 us -> 317 us (0.75)
  waiting for transfers between devices: 236 us -> 56 us
  matrix products: 105 us -> 0 us
  Pallas kernels: 0 us -> 104 us
  local copies, waits for them, and re-layouts: 58.8 us -> 121 us
  starting transfers between devices: 0.12 us -> 14.6 us
  other arithmetic: 5.65 us -> 19.1 us
  between operations: 13.8 us -> 1.07 us
    all_gather x2 -> x0, waiting for transfers between devices: 179 us -> none  [the longest x1 133 us: per_device(): lax.all_gather(cholesky_tensor, 'field', axis=0, tiled=True)]
    dot_general x2 -> x0, matrix products: 105 us -> none  [the longest x1 52.7 us: per_device(): jnp.einsum('cwp,fp->cwf', green_function, lax.all_gather(cholesky_tensor,...]
    pallas_call x0 -> x16, Pallas kernels: none -> 104 us  [the longest x10 45.5 us: bias_of(): pl.pallas_call(functools.partial(bias_kernel, len(parts)), out_shape=jax....]
    reduce_scatter x1 -> x0, waiting for transfers between devices: 56.7 us -> none  [per_device(): lax.psum_scatter(partial_bias, 'pair', scatter_dimension=1, tiled=True)]
    ppermute x0 -> x21, waiting for transfers between devices: none -> 56 us  [the longest x6 49.6 us: per_device(): held.append([lax.ppermute(part, 'field', ring) for part in held[-1]])]
    dynamic_update_slice x0 -> x7, local copies, waits for them, and re-layouts: none -> 16.5 us  [per_device(): lax.dynamic_update_slice_in_dim(share, part, owners[step] * shard + start...]
    unnamed x7 -> x56, local copies, waits for them, and re-layouts: 58.8 us -> 74 us
    ppermute x0 -> x21, starting transfers between devices: none -> 14.6 us  [the longest x6 7.33 us: per_device(): held.append([lax.ppermute(part, 'field', ring) for part in held[-1]])]
  transfers between devices with their start and end apart: 3 -> 21, of which waited for: 3 -> 3; matrix products, arithmetic and copies ran while one was open for 0% -> 20% of each run, Pallas kernels for 0% -> 30%
where the time goes in v1:
time: 317 us; the launch traced here: 315 us
  local copies, waits for them, and re-layouts  121 us (38%)
  Pallas kernels  104 us (33%)
  waiting for transfers between devices  56 us (18%)
  other arithmetic  19.1 us (6%)
  starting transfers between devices  14.6 us (5%)
    unnamed x56, local copies, waits for them, and re-layouts  74 us
    ppermute x6, waiting for transfers between devices, per_device(): held.append([lax.ppermute(part, 'field', ring) for part in held[-1]])  49.6 us
    pallas_call x10, Pallas kernels, bias_of(): pl.pallas_call(functools.partial(bias_kernel, len(parts)), out_shape=jax....  45.5 us
    pallas_call x2, Pallas kernels, accumulate(): pl.pallas_call(functools.partial(accumulate_kernel, len(mine), len(unit),...  29.4 us
    pallas_call x2, Pallas kernels, finish(): pl.pallas_call(functools.partial(finish_kernel, len(capped), len(unit), u...  17.4 us
    dynamic_update_slice x7, local copies, waits for them, and re-layouts, per_device(): lax.dynamic_update_slice_in_dim(share, part, owners[step] * shard + start...  16.5 us
    mul x5, other arithmetic, capped_of(): mine = 2.0 * jnp.tanh((sums - mean) / 2.0)  10.8 us
    squeeze x8, local copies, waits for them, and re-layouts, per_device(): own = lax.dynamic_index_in_dim(mine, chip, 1, keepdims=False)  10.1 us
  transfers between devices with their start and end apart: 21, of which 3 were waited for; matrix products, arithmetic and copies ran while one was open for 20% of the time, Pallas kernels for 30%

profile of v1, /device:TPU:0, one launch (start us, length us, event | category | flops | bytes accessed | tf_op | source)
XLA Modules:
  0.0 315.3 jit_solution(8850265492039480843)
XLA Ops:
  7.8 39.2 %collective-permute-done.3.refs_1_.refs_9_ = f32[64,2304]{1,0:T(8,128)S(1)} collective-permute-done((f32[64,2304]{1,0:T(8,128)S(1)}, f32[64,2304]{1,0:T(8,128)S(1)}, u32[]{:S(2)}, u32[]{:S(2)}) %collective-permute-start.3) | collective-permute-done | bytes 589856 | tf_op jit(solution)/shard_map/ppermute | solution.py:241
  47.0 9.5 %split_green.1 = (bf16[2,2,2,256,2304]{4,3,2,1,0:T(8,128)(2,1)S(1)}, bf16[2,2,2,256,2304]{4,3,2,1,0:T(8,128)(2,1)S(1)}) custom-call(f32[2,2,2,256,2304]{4,3,2,1,0:T(8,128)} %bitcast.42), custom_call_target="tpu_custom_call" | custom-call | flops 14155776 | bytes 18874368 | tf_op jit(solution)/shard_map/split_green/pallas_call | solution.py:38
  66.3 3.7 %copy-done.1 = bf16[2,2,2,256,2304]{4,3,2,1,0:T(8,128)(2,1)S(1)} copy-done((bf16[2,2,2,256,2304]{4,3,2,1,0:T(8,128)(2,1)S(1)}, bf16[2,2,2,256,2304]{4,3,2,1,0:T(8,128)(2,1)}, u32[]{:S(2)}) %copy-start.1) | copy-done | bytes 9437208
  69.9 3.7 %copy-done.7 = bf16[2,2,2,256,2304]{4,3,2,1,0:T(8,128)(2,1)S(1)} copy-done((bf16[2,2,2,256,2304]{4,3,2,1,0:T(8,128)(2,1)S(1)}, bf16[2,2,2,256,2304]{4,3,2,1,0:T(8,128)(2,1)}, u32[]{:S(2)}) %copy-start.7) | copy-done | bytes 9437208
  73.6 5.7 %bias.13 = f32[2,2,192,256]{3,2,1,0:T(8,128)} custom-call(s32[1]{0:T(128)} %bitcast.2.half_ref, bf16[2,2,2,256,2304]{4,3,2,1,0:T(8,128)(2,1)S(1)} %copy-done.1, bf16[2,2,2,256,2304]{4,3,2,1,0:T(8,128)(2,1)S(1)} %copy-done.7, f32[128,2304]{1,0:T(8,128)} %collective-permute-done.2.refs_0_.refs_8_, f32[64,2304]{1,0:T(8,128)S(1)} %collective-permute-done.3.refs_1_.refs_9_), custom_call_target="tpu_custom_call" | custom-call | flops 2717908992 | bytes 1769472 | tf_op jit(solution)/shard_map/bias/pallas_call | solution.py:66
  86.5 6.0 %reshape.28 = f32[4,256,4,192]{3,2,1,0:T(4,128)} reshape(f32[1024,768]{1,0:T(8,128)} %param.7) | data formatting | bytes 6291456 | tf_op jit(solution)/shard_map/reshape | solution.py:260
  96.1 10.4 %collective-permute-done.13.refs_0_.refs_1_ = f32[64,2304]{1,0:T(8,128)} collective-permute-done((f32[64,2304]{1,0:T(8,128)}, f32[64,2304]{1,0:T(8,128)}, u32[]{:S(2)}, u32[]{:S(2)}) %collective-permute-start.13) | collective-permute-done | bytes 589856 | tf_op jit(solution)/shard_map/ppermute | solution.py:241
  106.5 3.7 %copy-done.2 = bf16[2,2,2,256,2304]{4,3,2,1,0:T(8,128)(2,1)S(1)} copy-done((bf16[2,2,2,256,2304]{4,3,2,1,0:T(8,128)(2,1)S(1)}, bf16[2,2,2,256,2304]{4,3,2,1,0:T(8,128)(2,1)}, u32[]{:S(2)}) %copy-start.2) | copy-done | bytes 9437208
  110.2 3.7 %copy-done.8 = bf16[2,2,2,256,2304]{4,3,2,1,0:T(8,128)(2,1)S(1)} copy-done((bf16[2,2,2,256,2304]{4,3,2,1,0:T(8,128)(2,1)S(1)}, bf16[2,2,2,256,2304]{4,3,2,1,0:T(8,128)(2,1)}, u32[]{:S(2)}) %copy-start.8) | copy-done | bytes 9437208
  113.9 4.2 %bias.19 = f32[2,2,64,256]{3,2,1,0:T(8,128)S(1)} custom-call(s32[1]{0:T(128)} %bitcast.2.half_ref, bf16[2,2,2,256,2304]{4,3,2,1,0:T(8,128)(2,1)S(1)} %copy-done.2, bf16[2,2,2,256,2304]{4,3,2,1,0:T(8,128)(2,1)S(1)} %copy-done.8, f32[64,2304]{1,0:T(8,128)} %collective-permute-done.13.refs_0_.refs_1_), custom_call_target="tpu_custom_call" | custom-call | flops 905969664 | bytes 589824 | tf_op jit(solution)/shard_map/bias/pallas_call | solution.py:66
  118.1 4.8 %bias.12 = f32[2,2,192,256]{3,2,1,0:T(8,128)S(1)} custom-call(s32[1]{0:T(128)} %bitcast.half_ref, bf16[2,2,2,256,2304]{4,3,2,1,0:T(8,128)(2,1)S(1)} %copy-done.2, bf16[2,2,2,256,2304]{4,3,2,1,0:T(8,128)(2,1)S(1)} %copy-done.8, f32[128,2304]{1,0:T(8,128)} %collective-permute-done.2.refs_0_.refs_8_, f32[64,2304]{1,0:T(8,128)S(1)} %copy-done.22), custom_call_target="tpu_custom_call" | custom-call | flops 2717908992 | bytes 1769472 | tf_op jit(solution)/shard_map/bias/pallas_call | solution.py:66
  122.9 4.1 %bias.18 = f32[2,2,64,256]{3,2,1,0:T(8,128)S(1)} custom-call(s32[1]{0:T(128)} %bitcast.half_ref, bf16[2,2,2,256,2304]{4,3,2,1,0:T(8,128)(2,1)S(1)} %copy-done.2, bf16[2,2,2,256,2304]{4,3,2,1,0:T(8,128)(2,1)S(1)} %copy-done.8, f32[64,2304]{1,0:T(8,128)} %collective-permute-done.13.refs_0_.refs_1_), custom_call_target="tpu_custom_call" | custom-call | flops 905969664 | bytes 589824 | tf_op jit(solution)/shard_map/bias/pallas_call | solution.py:66
  131.3 5.8 %bias.15 = f32[2,2,192,256]{3,2,1,0:T(8,128)} custom-call(s32[1]{0:T(128)} %bitcast.2.half_ref, bf16[2,2,2,256,2304]{4,3,2,1,0:T(8,128)(2,1)S(1)} %copy-done.2, bf16[2,2,2,256,2304]{4,3,2,1,0:T(8,128)(2,1)S(1)} %copy-done.8, f32[128,2304]{1,0:T(8,128)} %collective-permute-done.6.refs_0_.refs_4_, f32[64,2304]{1,0:T(8,128)} %collective-permute-done.7.refs_1_.refs_5_), custom_call_target="tpu_custom_call" | custom-call | flops 2717908992 | bytes 1769472 | tf_op jit(solution)/shard_map/bias/pallas_call | solution.py:66
  148.6 6.4 %collective-permute-done.15 = f32[2,2,64,256]{3,2,1,0:T(8,128)} collective-permute-done((f32[2,2,64,256]{3,2,1,0:T(8,128)S(1)}, f32[2,2,64,256]{3,2,1,0:T(8,128)}, u32[]{:S(2)}, u32[]{:S(2)}) %collective-permute-start.15) | collective-permute-done | bytes 262176 | tf_op jit(solution)/shard_map/ppermute | solution.py:274
  156.2 3.7 %copy-done.3 = bf16[2,2,2,256,2304]{4,3,2,1,0:T(8,128)(2,1)S(1)} copy-done((bf16[2,2,2,256,2304]{4,3,2,1,0:T(8,128)(2,1)S(1)}, bf16[2,2,2,256,2304]{4,3,2,1,0:T(8,128)(2,1)}, u32[]{:S(2)}) %copy-start.3) | copy-done | bytes 9437208
  159.9 3.7 %copy-done.9 = bf16[2,2,2,256,2304]{4,3,2,1,0:T(8,128)(2,1)S(1)} copy-done((bf16[2,2,2,256,2304]{4,3,2,1,0:T(8,128)(2,1)S(1)}, bf16[2,2,2,256,2304]{4,3,2,1,0:T(8,128)(2,1)}, u32[]{:S(2)}) %copy-start.9) | copy-done | bytes 9437208
  163.5 4.9 %bias.14 = f32[2,2,192,256]{3,2,1,0:T(8,128)S(1)} custom-call(s32[1]{0:T(128)} %bitcast.half_ref, bf16[2,2,2,256,2304]{4,3,2,1,0:T(8,128)(2,1)S(1)} %copy-done.3, bf16[2,2,2,256,2304]{4,3,2,1,0:T(8,128)(2,1)S(1)} %copy-done.9, f32[128,2304]{1,0:T(8,128)} %collective-permute-done.6.refs_0_.refs_4_, f32[64,2304]{1,0:T(8,128)} %collective-permute-done.7.refs_1_.refs_5_), custom_call_target="tpu_custom_call" | custom-call | flops 2717908992 | bytes 1769472 | tf_op jit(solution)/shard_map/bias/pallas_call | solution.py:66
  176.0 3.7 %copy-done.4 = bf16[2,2,2,256,2304]{4,3,2,1,0:T(8,128)(2,1)S(1)} copy-done((bf16[2,2,2,256,2304]{4,3,2,1,0:T(8,128)(2,1)S(1)}, bf16[2,2,2,256,2304]{4,3,2,1,0:T(8,128)(2,1)}, u32[]{:S(2)}) %copy-start.4) | copy-done | bytes 9437208
  179.7 3.7 %copy-done.10 = bf16[2,2,2,256,2304]{4,3,2,1,0:T(8,128)(2,1)S(1)} copy-done((bf16[2,2,2,256,2304]{4,3,2,1,0:T(8,128)(2,1)S(1)}, bf16[2,2,2,256,2304]{4,3,2,1,0:T(8,128)(2,1)}, u32[]{:S(2)}) %copy-start.10) | copy-done | bytes 9437208
  183.4 4.9 %bias.17 = f32[2,2,128,256]{3,2,1,0:T(8,128)} custom-call(s32[1]{0:T(128)} %bitcast.2.half_ref, bf16[2,2,2,256,2304]{4,3,2,1,0:T(8,128)(2,1)S(1)} %copy-done.4, bf16[2,2,2,256,2304]{4,3,2,1,0:T(8,128)(2,1)S(1)} %copy-done.10, f32[128,2304]{1,0:T(8,128)} %collective-permute-done.10.refs_0_), custom_call_target="tpu_custom_call" | custom-call | flops 1811939328 | bytes 1179648 | tf_op jit(solution)/shard_map/bias/pallas_call | solution.py:66
  197.1 3.7 %copy-done.5 = bf16[2,2,2,256,2304]{4,3,2,1,0:T(8,128)(2,1)S(1)} copy-done((bf16[2,2,2,256,2304]{4,3,2,1,0:T(8,128)(2,1)S(1)}, bf16[2,2,2,256,2304]{4,3,2,1,0:T(8,128)(2,1)}, u32[]{:S(2)}) %copy-start.5) | copy-done | bytes 9437208
  200.7 3.7 %copy-done.11 = bf16[2,2,2,256,2304]{4,3,2,1,0:T(8,128)(2,1)S(1)} copy-done((bf16[2,2,2,256,2304]{4,3,2,1,0:T(8,128)(2,1)S(1)}, bf16[2,2,2,256,2304]{4,3,2,1,0:T(8,128)(2,1)}, u32[]{:S(2)}) %copy-start.11) | copy-done | bytes 9437208
  204.4 4.1 %bias.16 = f32[2,2,128,256]{3,2,1,0:T(8,128)S(1)} custom-call(s32[1]{0:T(128)} %bitcast.half_ref, bf16[2,2,2,256,2304]{4,3,2,1,0:T(8,128)(2,1)S(1)} %copy-done.5, bf16[2,2,2,256,2304]{4,3,2,1,0:T(8,128)(2,1)S(1)} %copy-done.11, f32[128,2304]{1,0:T(8,128)} %collective-permute-done.10.refs_0_), custom_call_target="tpu_custom_call" | custom-call | flops 1811939328 | bytes 1179648 | tf_op jit(solution)/shard_map/bias/pallas_call | solution.py:66
  214.2 16.2 %accumulate.2.refs_6_ = f32[2,2,2,256,2304]{4,3,2,1,0:T(8,128)S(1)} custom-call(s32[5]{0:T(128)S(1)} %stack.35.s_ref, f32[2,2,192,256]{3,2,1,0:T(8,128)} %tanh_multiply_fusion.2.refs_0_, f32[2,2,192,256]{3,2,1,0:T(8,128)} %tanh_multiply_fusion.1.refs_1_, f32[2,2,192,256]{3,2,1,0:T(8,128)} %collective-permute-done.19.refs_2_, ...), custom_call_target="tpu_custom_call" | custom-call | flops 10871635968 | bytes 3538944 | tf_op jit(solution)/shard_map/accumulate/pallas_call | solution.py:138
  230.4 6.8 %copy-done.12 = f32[2,2,2,256,2304]{4,3,2,1,0:T(8,128)} copy-done((f32[2,2,2,256,2304]{4,3,2,1,0:T(8,128)}, f32[2,2,2,256,2304]{4,3,2,1,0:T(8,128)S(1)}, u32[]{:S(2)}) %copy-start.12) | copy-done | bytes 18874392
  259.1 6.4 %copy-done.13 = f32[2,2,2,256,2304]{4,3,2,1,0:T(8,128)S(1)} copy-done((f32[2,2,2,256,2304]{4,3,2,1,0:T(8,128)S(1)}, f32[2,2,2,256,2304]{4,3,2,1,0:T(8,128)}, u32[]{:S(2)}) %copy-start.13) | copy-done | bytes 18874392
  265.5 13.2 %accumulate.3.refs_5_ = f32[2,2,2,256,2304]{4,3,2,1,0:T(8,128)S(1)} custom-call(s32[5]{0:T(128)S(1)} %stack.35.s_ref, f32[2,2,192,256]{3,2,1,0:T(8,128)} %tanh_multiply_fusion.refs_0_, f32[2,2,192,256]{3,2,1,0:T(8,128)} %collective-permute-done.18.refs_1_, f32[4,4,192,256]{3,2,1,0:T(8,128)S(1)} %bitcast.35, ...), custom_call_target="tpu_custom_call", output_to_operand_aliasing={{}: (7, {})} | custom-call | flops 5435817984 | bytes 1769472 | tf_op jit(solution)/shard_map/accumulate/pallas_call | solution.py:138
  278.7 6.5 %copy-done.14 = f32[2,2,2,256,2304]{4,3,2,1,0:T(8,128)} copy-done((f32[2,2,2,256,2304]{4,3,2,1,0:T(8,128)}, f32[2,2,2,256,2304]{4,3,2,1,0:T(8,128)S(1)}, u32[]{:S(2)}) %copy-start.14) | copy-done | bytes 18874392
  285.2 6.4 %copy-done.15 = f32[2,2,2,256,2304]{4,3,2,1,0:T(8,128)S(1)} copy-done((f32[2,2,2,256,2304]{4,3,2,1,0:T(8,128)S(1)}, f32[2,2,2,256,2304]{4,3,2,1,0:T(8,128)}, u32[]{:S(2)}) %copy-start.15) | copy-done | bytes 18874392
  291.5 8.8 %finish.2.refs_6_ = f32[2,2,256,2,2304]{4,3,2,1,0:T(2,128)} custom-call(s32[5]{0:T(128)S(1)} %stack.35.s_ref, f32[2,2,128,256]{3,2,1,0:T(8,128)} %tanh_multiply_fusion.3.refs_0_, f32[2,2,64,256]{3,2,1,0:T(8,128)S(1)} %tanh_multiply_fusion.4.refs_1_, f32[4,4,192,256]{3,2,1,0:T(8,128)S(1)} %bitcast.37, f32[4,4,192,256]{3,2,1,0:T(8,128)S(1)} %bitcast.38, ...), custom_call_target="tpu_custom_call" | custom-call | flops 2717908992 | bytes 9437184 | tf_op jit(solution)/shard_map/finish/pallas_call | solution.py:201
  300.3 6.4 %copy-done.16 = f32[2,2,2,256,2304]{4,3,2,1,0:T(8,128)S(1)} copy-done((f32[2,2,2,256,2304]{4,3,2,1,0:T(8,128)S(1)}, f32[2,2,2,256,2304]{4,3,2,1,0:T(8,128)}, u32[]{:S(2)}) %copy-start.16) | copy-done | bytes 18874392
  306.7 8.6 %finish.3 = f32[2,2,256,2,2304]{4,3,2,1,0:T(2,128)} custom-call(s32[5]{0:T(128)S(1)} %stack.34.s_ref, f32[2,2,128,256]{3,2,1,0:T(8,128)} %collective-permute-done.16.refs_0_, f32[2,2,64,256]{3,2,1,0:T(8,128)} %collective-permute-done.17.refs_1_, f32[4,4,192,256]{3,2,1,0:T(8,128)S(1)} %bitcast.39, ...), custom_call_target="tpu_custom_call", output_to_operand_aliasing={{}: (7, {})} | custom-call | flops 2717908992 | bytes 9437184 | tf_op jit(solution)/shard_map/finish/pallas_call | solution.py:201
  (126 shorter events, 88.2 us)
Async XLA Ops:
  3.1 60.2 %collective-permute-start.2 = (f32[128,2304]{1,0:T(8,128)}, f32[128,2304]{1,0:T(8,128)}, u32[]{:S(2)}, u32[]{:S(2)}) collective-permute-start(f32[128,2304]{1,0:T(8,128)} %slice.30), channel_id=1, source_target_pairs={{0,4},{4,8},{8,12},{12,0},{1,5},{5,9},{9,13},{13,1},{2,6},{6,10},{... | collective-permute-start | bytes 3538952 | tf_op jit(solution)/shard_map/ppermute | solution.py:241
  6.2 40.8 %collective-permute-start.3 = (f32[64,2304]{1,0:T(8,128)S(1)}, f32[64,2304]{1,0:T(8,128)S(1)}, u32[]{:S(2)}, u32[]{:S(2)}) collective-permute-start(f32[64,2304]{1,0:T(8,128)S(1)} %slice.31), channel_id=1, source_target_pairs={{0,4},{4,8},{8,12},{12,0},{1,5},{5,9},{9,13},{13,1},{2,6},{6,10},{... | collective-permute-start | bytes 1769480 | tf_op jit(solution)/shard_map/ppermute | solution.py:241
  47.0 19.3 %copy-start.21 = (f32[64,2304]{1,0:T(8,128)}, f32[64,2304]{1,0:T(8,128)S(1)}, u32[]{:S(2)}) copy-start(f32[64,2304]{1,0:T(8,128)S(1)} %collective-permute-done.3.refs_1_.refs_9_) | copy-start | bytes 1769476
  47.0 17.7 %collective-permute-start.7 = (f32[64,2304]{1,0:T(8,128)S(1)}, f32[64,2304]{1,0:T(8,128)}, u32[]{:S(2)}, u32[]{:S(2)}) collective-permute-start(f32[64,2304]{1,0:T(8,128)S(1)} %collective-permute-done.3.refs_1_.refs_9_), channel_id=1, source_target_pairs={{0,4},{4,8},{8,12},{12,0},{1,5},{5,9},{9,13},{13,1},{2,6},{6,10},{... | collective-permute-start | bytes 1769480 | tf_op jit(solution)/shard_map/ppermute | solution.py:241
  56.6 6.8 %copy-start.6 = (bf16[2,2,2,256,2304]{4,3,2,1,0:T(8,128)(2,1)}, bf16[2,2,2,256,2304]{4,3,2,1,0:T(8,128)(2,1)S(1)}, u32[]{:S(2)}) copy-start(bf16[2,2,2,256,2304]{4,3,2,1,0:T(8,128)(2,1)S(1)} %get-tuple-element.5.low_ref) | copy-start | bytes 28311556
  56.6 8.0 %copy-start.25 = (f32[2,768]{1,0:T(2,128)S(1)}, f32[2,768]{1,0:T(2,128)}, u32[]{:S(2)}) copy-start(f32[2,768]{1,0:T(2,128)} %param.6) | copy-start | bytes 18436
  63.3 19.5 %collective-permute-start = (f32[2,2,192,256]{3,2,1,0:T(8,128)S(1)}, f32[2,2,192,256]{3,2,1,0:T(8,128)}, u32[]{:S(2)}, u32[]{:S(2)}) collective-permute-start(f32[2,2,192,256]{3,2,1,0:T(8,128)S(1)} %bias.11), channel_id=1, source_target_pairs={{0,1},{1,0},{2,3},{3,2},{4,5},{5,4},{6,7},{7,6},{8,9},{9,8},{10,11... | collective-permute-start | bytes 2359304 | tf_op jit(solution)/shard_map/ppermute | solution.py:270
  63.3 68.0 %collective-permute-start.6 = (f32[128,2304]{1,0:T(8,128)}, f32[128,2304]{1,0:T(8,128)}, u32[]{:S(2)}, u32[]{:S(2)}) collective-permute-start(f32[128,2304]{1,0:T(8,128)} %collective-permute-done.2.refs_0_.refs_8_), channel_id=1, source_target_pairs={{0,4},{4,8},{8,12},{12,0},{1,5},{5,9},{9,13},{13,1},{2,6},{6,10},{... | collective-permute-start | bytes 3538952 | tf_op jit(solution)/shard_map/ppermute | solution.py:241
  64.7 41.9 %collective-permute-start.13 = (f32[64,2304]{1,0:T(8,128)}, f32[64,2304]{1,0:T(8,128)}, u32[]{:S(2)}, u32[]{:S(2)}) collective-permute-start(f32[64,2304]{1,0:T(8,128)} %collective-permute-done.7.refs_1_.refs_5_), channel_id=1, source_target_pairs={{0,4},{4,8},{8,12},{12,0},{1,5},{5,9},{9,13},{13,1},{2,6},{6,10},{... | collective-permute-start | bytes 1769480 | tf_op jit(solution)/shard_map/ppermute | solution.py:241
  79.3 47.7 %collective-permute-start.4 = (f32[2,2,192,256]{3,2,1,0:T(8,128)}, f32[2,2,192,256]{3,2,1,0:T(8,128)}, u32[]{:S(2)}, u32[]{:S(2)}) collective-permute-start(f32[2,2,192,256]{3,2,1,0:T(8,128)} %bias.13), channel_id=1, source_target_pairs={{0,1},{1,0},{2,3},{3,2},{4,5},{5,4},{6,7},{7,6},{8,9},{9,8},{10,11... | collective-permute-start | bytes 2359304 | tf_op jit(solution)/shard_map/ppermute | solution.py:270
  84.9 52.2 %collective-permute-start.1 = (f32[2,2,192,256]{3,2,1,0:T(8,128)}, f32[2,2,192,256]{3,2,1,0:T(8,128)}, u32[]{:S(2)}, u32[]{:S(2)}) collective-permute-start(f32[2,2,192,256]{3,2,1,0:T(8,128)} %add.113), channel_id=1, source_target_pairs={{0,2},{1,3},{2,0},{3,1},{4,6},{5,7},{6,4},{7,5},{8,10},{9,11},{10,... | collective-permute-start | bytes 2359304 | tf_op jit(solution)/shard_map/ppermute | solution.py:274
  118.1 12.6 %collective-permute-start.14 = (f32[2,2,64,256]{3,2,1,0:T(8,128)S(1)}, f32[2,2,64,256]{3,2,1,0:T(8,128)S(1)}, u32[]{:S(2)}, u32[]{:S(2)}) collective-permute-start(f32[2,2,64,256]{3,2,1,0:T(8,128)S(1)} %bias.19), channel_id=1, source_target_pairs={{0,1},{1,0},{2,3},{3,2},{4,5},{5,4},{6,7},{7,6},{8,9},{9,8},{10,11... | collective-permute-start | bytes 786440 | tf_op jit(solution)/shard_map/ppermute | solution.py:270
  129.2 42.9 %collective-permute-start.5 = (f32[2,2,192,256]{3,2,1,0:T(8,128)}, f32[2,2,192,256]{3,2,1,0:T(8,128)}, u32[]{:S(2)}, u32[]{:S(2)}) collective-permute-start(f32[2,2,192,256]{3,2,1,0:T(8,128)} %add.119), channel_id=1, source_target_pairs={{0,2},{1,3},{2,0},{3,1},{4,6},{5,7},{6,4},{7,5},{8,10},{9,11},{10,... | collective-permute-start | bytes 2359304 | tf_op jit(solution)/shard_map/ppermute | solution.py:274
  130.7 6.5 %copy-start.24 = (f32[2,2,64,256]{3,2,1,0:T(8,128)}, f32[2,2,64,256]{3,2,1,0:T(8,128)S(1)}, u32[]{:S(2)}) copy-start(f32[2,2,64,256]{3,2,1,0:T(8,128)S(1)} %add.138) | copy-start | bytes 786436
  130.7 24.3 %collective-permute-start.15 = (f32[2,2,64,256]{3,2,1,0:T(8,128)S(1)}, f32[2,2,64,256]{3,2,1,0:T(8,128)}, u32[]{:S(2)}, u32[]{:S(2)}) collective-permute-start(f32[2,2,64,256]{3,2,1,0:T(8,128)S(1)} %add.138), channel_id=1, source_target_pairs={{0,2},{1,3},{2,0},{3,1},{4,6},{5,7},{6,4},{7,5},{8,10},{9,11},{10,... | collective-permute-start | bytes 786440 | tf_op jit(solution)/shard_map/ppermute | solution.py:274
  137.2 31.3 %collective-permute-start.8 = (f32[2,2,192,256]{3,2,1,0:T(8,128)}, f32[2,2,192,256]{3,2,1,0:T(8,128)}, u32[]{:S(2)}, u32[]{:S(2)}) collective-permute-start(f32[2,2,192,256]{3,2,1,0:T(8,128)} %bias.15), channel_id=1, source_target_pairs={{0,1},{1,0},{2,3},{3,2},{4,5},{5,4},{6,7},{7,6},{8,9},{9,8},{10,11... | collective-permute-start | bytes 2359304 | tf_op jit(solution)/shard_map/ppermute | solution.py:270
  137.2 38.8 %collective-permute-start.10 = (f32[128,2304]{1,0:T(8,128)}, f32[128,2304]{1,0:T(8,128)}, u32[]{:S(2)}, u32[]{:S(2)}) collective-permute-start(f32[128,2304]{1,0:T(8,128)} %collective-permute-done.6.refs_0_.refs_4_), channel_id=1, source_target_pairs={{0,4},{4,8},{8,12},{12,0},{1,5},{5,9},{9,13},{13,1},{2,6},{6,10},{... | collective-permute-start | bytes 3538952 | tf_op jit(solution)/shard_map/ppermute | solution.py:241
  139.6 74.5 %collective-permute-start.19 = (f32[2,2,192,256]{3,2,1,0:T(8,128)}, f32[2,2,192,256]{3,2,1,0:T(8,128)}, u32[]{:S(2)}, u32[]{:S(2)}) collective-permute-start(f32[2,2,192,256]{3,2,1,0:T(8,128)} %tanh_multiply_fusion.2.refs_0_), channel_id=1, source_target_pairs={{0,1},{1,0},{2,3},{3,2},{4,5},{5,4},{6,7},{7,6},{8,9},{9,8},{10,11... | collective-permute-start | bytes 2359304 | tf_op jit(solution)/shard_map/ppermute | solution.py:278
  170.6 37.9 %collective-permute-start.9 = (f32[2,2,192,256]{3,2,1,0:T(8,128)}, f32[2,2,192,256]{3,2,1,0:T(8,128)}, u32[]{:S(2)}, u32[]{:S(2)}) collective-permute-start(f32[2,2,192,256]{3,2,1,0:T(8,128)} %add.126), channel_id=1, source_target_pairs={{0,2},{1,3},{2,0},{3,1},{4,6},{5,7},{6,4},{7,5},{8,10},{9,11},{10,... | collective-permute-start | bytes 2359304 | tf_op jit(solution)/shard_map/ppermute | solution.py:274
  174.6 39.6 %collective-permute-start.20 = (f32[2,2,192,256]{3,2,1,0:T(8,128)}, f32[2,2,192,256]{3,2,1,0:T(8,128)}, u32[]{:S(2)}, u32[]{:S(2)}) collective-permute-start(f32[2,2,192,256]{3,2,1,0:T(8,128)} %tanh_multiply_fusion.1.refs_1_), channel_id=1, source_target_pairs={{0,1},{1,0},{2,3},{3,2},{4,5},{5,4},{6,7},{7,6},{8,9},{9,8},{10,11... | collective-permute-start | bytes 2359304 | tf_op jit(solution)/shard_map/ppermute | solution.py:278
  174.6 125.7 %collective-permute-start.17 = (f32[2,2,64,256]{3,2,1,0:T(8,128)S(1)}, f32[2,2,64,256]{3,2,1,0:T(8,128)}, u32[]{:S(2)}, u32[]{:S(2)}) collective-permute-start(f32[2,2,64,256]{3,2,1,0:T(8,128)S(1)} %tanh_multiply_fusion.4.refs_1_), channel_id=1, source_target_pairs={{0,1},{1,0},{2,3},{3,2},{4,5},{5,4},{6,7},{7,6},{8,9},{9,8},{10,11... | collective-permute-start | bytes 786440 | tf_op jit(solution)/shard_map/ppermute | solution.py:278
  188.3 23.4 %collective-permute-start.11 = (f32[2,2,128,256]{3,2,1,0:T(8,128)}, f32[2,2,128,256]{3,2,1,0:T(8,128)}, u32[]{:S(2)}, u32[]{:S(2)}) collective-permute-start(f32[2,2,128,256]{3,2,1,0:T(8,128)} %bias.17), channel_id=1, source_target_pairs={{0,1},{1,0},{2,3},{3,2},{4,5},{5,4},{6,7},{7,6},{8,9},{9,8},{10,11... | collective-permute-start | bytes 1572872 | tf_op jit(solution)/shard_map/ppermute | solution.py:270
  208.6 5.6 %copy-start.20 = (f32[192,2304]{1,0:T(8,128)S(1)}, f32[192,2304]{1,0:T(8,128)}, u32[]{:S(2)}) copy-start(f32[192,2304]{1,0:T(8,128)} %refs_7_.1) | copy-start | bytes 5308420
  211.2 47.9 %collective-permute-start.18 = (f32[2,2,192,256]{3,2,1,0:T(8,128)}, f32[2,2,192,256]{3,2,1,0:T(8,128)}, u32[]{:S(2)}, u32[]{:S(2)}) collective-permute-start(f32[2,2,192,256]{3,2,1,0:T(8,128)} %tanh_multiply_fusion.refs_0_), channel_id=1, source_target_pairs={{0,1},{1,0},{2,3},{3,2},{4,5},{5,4},{6,7},{7,6},{8,9},{9,8},{10,11... | collective-permute-start | bytes 2359304 | tf_op jit(solution)/shard_map/ppermute | solution.py:278
  213.6 35.2 %collective-permute-start.12 = (f32[2,2,128,256]{3,2,1,0:T(8,128)}, f32[2,2,128,256]{3,2,1,0:T(8,128)}, u32[]{:S(2)}, u32[]{:S(2)}) collective-permute-start(f32[2,2,128,256]{3,2,1,0:T(8,128)} %add.133), channel_id=1, source_target_pairs={{0,2},{1,3},{2,0},{3,1},{4,6},{5,7},{6,4},{7,5},{8,10},{9,11},{10,... | collective-permute-start | bytes 1572872 | tf_op jit(solution)/shard_map/ppermute | solution.py:274
  230.4 6.9 %copy-start.12 = (f32[2,2,2,256,2304]{4,3,2,1,0:T(8,128)}, f32[2,2,2,256,2304]{4,3,2,1,0:T(8,128)S(1)}, u32[]{:S(2)}) copy-start(f32[2,2,2,256,2304]{4,3,2,1,0:T(8,128)S(1)} %accumulate.2.refs_6_) | copy-start | bytes 56623108
  250.9 49.4 %collective-permute-start.16 = (f32[2,2,128,256]{3,2,1,0:T(8,128)}, f32[2,2,128,256]{3,2,1,0:T(8,128)}, u32[]{:S(2)}, u32[]{:S(2)}) collective-permute-start(f32[2,2,128,256]{3,2,1,0:T(8,128)} %tanh_multiply_fusion.3.refs_0_), channel_id=1, source_target_pairs={{0,1},{1,0},{2,3},{3,2},{4,5},{5,4},{6,7},{7,6},{8,9},{9,8},{10,11... | collective-permute-start | bytes 1572872 | tf_op jit(solution)/shard_map/ppermute | solution.py:278
  259.1 6.4 %copy-start.13 = (f32[2,2,2,256,2304]{4,3,2,1,0:T(8,128)S(1)}, f32[2,2,2,256,2304]{4,3,2,1,0:T(8,128)}, u32[]{:S(2)}) copy-start(f32[2,2,2,256,2304]{4,3,2,1,0:T(8,128)} %copy-done.12) | copy-start | bytes 56623108
  265.5 19.7 %copy-start.18 = (bf16[576,2304]{1,0:T(8,128)(2,1)S(1)}, bf16[576,2304]{1,0:T(8,128)(2,1)}, u32[]{:S(2)}) copy-start(bf16[576,2304]{1,0:T(8,128)(2,1)} %copy-done.17) | copy-start | bytes 7962628
  278.7 6.5 %copy-start.14 = (f32[2,2,2,256,2304]{4,3,2,1,0:T(8,128)}, f32[2,2,2,256,2304]{4,3,2,1,0:T(8,128)S(1)}, u32[]{:S(2)}) copy-start(f32[2,2,2,256,2304]{4,3,2,1,0:T(8,128)S(1)} %accumulate.3.refs_5_) | copy-start | bytes 56623108
  285.2 6.4 %copy-start.15 = (f32[2,2,2,256,2304]{4,3,2,1,0:T(8,128)S(1)}, f32[2,2,2,256,2304]{4,3,2,1,0:T(8,128)}, u32[]{:S(2)}) copy-start(f32[2,2,2,256,2304]{4,3,2,1,0:T(8,128)} %copy-done.14) | copy-start | bytes 56623108
  300.3 6.4 %copy-start.16 = (f32[2,2,2,256,2304]{4,3,2,1,0:T(8,128)S(1)}, f32[2,2,2,256,2304]{4,3,2,1,0:T(8,128)}, u32[]{:S(2)}) copy-start(f32[2,2,2,256,2304]{4,3,2,1,0:T(8,128)} %copy-done.14) | copy-start | bytes 56623108
  (15 other events, 57.5 us)

commit v2 on v0

v2 whole, which is shorter than its diff:
```python
import functools
import math

import jax
import jax.numpy as jnp
from jax import lax
from jax.experimental import pallas as pl
from jax.experimental.pallas import tpu as pltpu
from jax.sharding import PartitionSpec as P

CORES = 2
MIB = 1024 * 1024
ROWS_DOT = (((1,), (1,)), ((), ()))
DOT = (((1,), (0,)), ((), ()))
WHOLE = pl.BlockSpec(memory_space=pltpu.VMEM)
COST = pl.CostEstimate(flops=1, bytes_accessed=1, transcendentals=0)


def split(x):
    high = x.astype(jnp.bfloat16)
    return high, (x - high.astype(jnp.float32)).astype(jnp.bfloat16)


def params(mib):
    return pltpu.CompilerParams(vmem_limit_bytes=mib * MIB)


def stacked(parts):
    return parts[0] if len(parts) == 1 else jnp.concatenate(parts, 0)


def split_green_kernel(s_ref, green_ref, own_high_ref, own_low_ref, mate_high_ref, mate_low_ref):
    at = (pl.program_id(0), pl.program_id(1))
    high, low = split(green_ref[0, 0, 0])
    own = pl.program_id(2) == s_ref[0]

    @pl.when(own)
    def _():
        own_high_ref[at], own_low_ref[at] = high, low

    @pl.when(jnp.logical_not(own))
    def _():
        mate_high_ref[at], mate_low_ref[at] = high, low


def split_green(scalars, green):
    channels, across, cores, rows, pairs = green.shape
    return pl.pallas_call(
        split_green_kernel,
        out_shape=[pltpu.VMEM((channels, across, rows, pairs), jnp.bfloat16)] * 4,
        grid=(channels, across, cores),
        in_specs=[
            pl.BlockSpec(memory_space=pltpu.SMEM),
            pl.BlockSpec((1, 1, 1, rows, pairs), lambda c, x, h: (c, x, h, 0, 0)),
        ],
        out_specs=[WHOLE] * 4,
        compiler_params=params(12),
        cost_estimate=COST,
        name="split_green",
    )(scalars, green)


def bias_kernel(n, high_ref, low_ref, *refs):
    parts, out_refs, chol = refs[:n], refs[n:-1], refs[-1]
    fields = chol.shape[0] // 2
    chol[:fields], chol[fields:] = split(stacked([part[...] for part in parts]))
    channels, across = high_ref.shape[:2]
    for c in range(channels):
        for x in range(across):
            both = lax.dot_general(chol[...], high_ref[c, x], ROWS_DOT, preferred_element_type=jnp.float32)
            cross = lax.dot_general(chol[:fields], low_ref[c, x], ROWS_DOT, preferred_element_type=jnp.float32)
            out_refs[c][x] = both[:fields] + (both[fields:] + cross)


def bias_of(high, low, parts):
    channels, across, rows, pairs = high.shape
    fields = sum(part.shape[0] for part in parts)
    return pl.pallas_call(
        functools.partial(bias_kernel, len(parts)),
        out_shape=[jax.ShapeDtypeStruct((across, fields, rows), jnp.float32)] * channels,
        in_specs=[WHOLE] * (2 + len(parts)),
        out_specs=[WHOLE] * channels,
        scratch_shapes=[pltpu.VMEM((2 * fields, pairs), jnp.bfloat16)],
        compiler_params=params(10),
        cost_estimate=COST,
        name="bias",
    )(high, low, *parts)


def add_kernel(n, *refs):
    for c in range(n):
        refs[-1][c] = refs[c][...] + refs[n + c][...]


def add(a, b):
    return pl.pallas_call(
        functools.partial(add_kernel, len(a)),
        out_shape=jax.ShapeDtypeStruct((len(a), *a[0].shape), a[0].dtype),
        in_specs=[WHOLE] * (2 * len(a)),
        out_specs=WHOLE,
        compiler_params=params(6),
        cost_estimate=COST,
        name="add",
    )(*a, *b)


def cap_kernel(unit, s_ref, mean_ref, sums_ref, more_ref, *refs):
    channels, across, fields, _ = sums_ref.shape
    capped_refs, share_ref = refs[-1 - channels : -1], refs[-1]
    means = [mean_ref[s_ref[2 + step], start : start + rows] for step, start, rows, _ in unit]
    for c in range(channels):
        mean = stacked([column[:, c : c + 1] for column in means])
        for x in range(across):
            capped_refs[c][x] = 2.0 * jnp.tanh((sums_ref[c, x] + more_ref[c, x] - mean) / 2.0)
        at = 0
        for step, start, rows, shard in unit:
            to = pl.ds(pl.multiple_of(s_ref[2 + step] * shard + start, 8), rows)
            share_ref[c, to, :] = capped_refs[c][s_ref[1], at : at + rows]
            at += rows


def cap(unit, scalars, means, sums, more, share, all_fields):
    channels, _, _, rows = sums.shape
    operands = [scalars, means, sums, more]
    in_specs = [pl.BlockSpec(memory_space=pltpu.SMEM), WHOLE, WHOLE, WHOLE]
    aliases = {}
    if share is not None:
        aliases = {len(operands): channels}
        operands.append(share)
        in_specs.append(WHOLE)
    return pl.pallas_call(
        functools.partial(cap_kernel, unit),
        out_shape=[jax.ShapeDtypeStruct(sums.shape[1:], jnp.float32)] * channels
        + [pltpu.VMEM((channels, all_fields, rows), jnp.float32)],
        in_specs=in_specs,
        out_specs=[WHOLE] * (channels + 1),
        input_output_aliases=aliases,
        compiler_params=params(8),
        cost_estimate=COST,
        name="cap",
    )(*operands)


def stack_chol(out, parts):
    high, low = split(stacked([part[...] for part in parts]))
    depth = high.shape[0]
    out[:depth] = high
    out[depth : 2 * depth] = high
    out[2 * depth :] = low


def stack_fields(capped, noise):
    first = stacked(noise) - stacked(capped[0::2])
    second = -stacked(capped[1::2])
    high, low = split(jnp.concatenate([first, second], 1))
    return jnp.concatenate([high, low, high], 0).T


def noise_specs(unit, noise, lanes, rows):
    apart, blocks = noise.shape[1] > 1, rows // lanes

    def spec(step, shard):
        def at(x, h, b, s):
            share = x * CORES + h
            return (s[2 + step], share, 0, b) if apart else (s[2 + step], 0, 0, share * blocks + b)

        return pl.BlockSpec((1, 1, shard, lanes), at)

    return [spec(step, shard) for step, _, _, shard in unit]


def noise_pieces(refs, unit):
    return [ref[0, 0, start : start + rows] for ref, (_, start, rows, _) in zip(refs, unit)]


def stack_kernel(*refs):
    stack_chol(refs[-1], refs[:-1])


def stack_of(chol):
    depth = sum(part.shape[0] for part in chol)
    return pl.pallas_call(
        stack_kernel,
        out_shape=pltpu.VMEM((3 * depth, chol[0].shape[1]), jnp.bfloat16),
        in_specs=[WHOLE] * len(chol),
        out_specs=WHOLE,
        compiler_params=params(12),
        cost_estimate=COST,
        name="stack_cholesky",
    )(*chol)


def finish_kernel(n, m, unit, scale, with_share, s_ref, *refs):
    capped, noise, stack = refs[:n], refs[n : n + m], refs[n + m]
    left = refs[-1]
    out_ref = refs[-3] if with_share else refs[-2]
    x, p = pl.program_id(0), pl.program_id(1)

    if with_share:

        @pl.when((x == 0) & (p == 0))
        def _():
            for c in range(2):
                refs[-2][c] = refs[-4][c].T

    @pl.when(p == 0)
    def _():
        left[...] = stack_fields([part[0] for part in capped], noise_pieces(noise, unit))

    width = out_ref.shape[-1]
    columns = pl.ds(pl.multiple_of(p * width, 128), width)
    sums = scale * lax.dot_general(left[...], stack[:, columns], DOT, preferred_element_type=jnp.float32)
    rows = sums.shape[0] // 2
    for c in range(2):
        out_ref[0, 0, :, c, :] = sums[c * rows : (c + 1) * rows]


def finish(capped, noise, stack, unit, scalars, scale, earlier, share, sizes):
    across, rows, pairs = sizes
    tiles = 3 if pairs % 384 == 0 else 1
    in_specs = [pl.BlockSpec((1, *part.shape[1:]), lambda x, p, s: (x, 0, 0)) for part in capped]
    in_specs += [
        pl.BlockSpec(spec.block_shape, lambda x, p, s, at=spec.index_map: at(x, s[0], 0, s))
        for spec in noise_specs(unit, noise, rows, rows)
    ]
    in_specs += [WHOLE]
    operands = [scalars, *capped, *([noise] * len(unit)), stack]
    aliases = {}
    if earlier is not None:
        in_specs.append(pl.BlockSpec(memory_space=pl.ANY))
        aliases = {len(operands): 0}
        operands.append(earlier)
    out_shape = [jax.ShapeDtypeStruct((across, CORES, rows, 2, pairs), jnp.float32)]
    out_specs = [pl.BlockSpec((1, 1, rows, 2, pairs // tiles), lambda x, p, s: (x, s[0], 0, 0, p))]
    if share is not None:
        turned = (share.shape[0], share.shape[2], share.shape[1])
        out_shape.append(jax.ShapeDtypeStruct(turned, jnp.float32))
        out_specs.append(pl.BlockSpec(turned, lambda x, p, s: (0, 0, 0)))
        in_specs.append(WHOLE)
        operands.append(share)
    return pl.pallas_call(
        functools.partial(finish_kernel, len(capped), len(unit), unit, scale, share is not None),
        out_shape=out_shape,
        grid_spec=pltpu.PrefetchScalarGridSpec(
            num_scalar_prefetch=1,
            grid=(across, tiles),
            in_specs=in_specs,
            out_specs=out_specs,
            scratch_shapes=[pltpu.VMEM((2 * rows, stack.shape[0]), jnp.bfloat16)],
        ),
        input_output_aliases=aliases,
        compiler_params=params(36),
        cost_estimate=COST,
        name="finish",
    )(*operands)


def after(x, *earlier):
    return lax.optimization_barrier((x, *earlier))[0]


def per_device(ring_size, pair_size, cholesky_tensor, green_function, mean_field, field_noise):
    shard, pairs = cholesky_tensor.shape
    channels, walkers, _ = green_function.shape
    fields = ring_size * shard
    total_pairs = pair_size * pairs
    across = pair_size // CORES
    rows = walkers // pair_size
    sizes = (across, rows, pairs)
    scale = math.sqrt(total_pairs / fields)

    place, member = lax.axis_index("field"), lax.axis_index("pair")
    core, chip = member % CORES, member // CORES
    owners = [(place - step) % ring_size for step in range(ring_size)]
    own_scalars = jnp.stack([core, chip, *owners]).astype(jnp.int32)
    mate_scalars = jnp.stack([1 - core, chip, *owners]).astype(jnp.int32)

    ring = [(i, (i + 1) % ring_size) for i in range(ring_size)]
    mates = [(i, i ^ 1) for i in range(pair_size)]

    count = 2 if shard % 32 == 0 and ring_size > 2 else 1
    cuts = [(i * (shard // count), shard // count) for i in range(count)]
    pieces = [(step, start, n, shard) for step in range(1, ring_size) for start, n in cuts]
    held = {(0, start): lax.slice_in_dim(cholesky_tensor, start, start + n, axis=0) for start, n in cuts}

    own_piece = (0, 0, shard, shard)
    if count > 1:
        units = [[own_piece]] + [pieces[i : i + 2] for i in range(0, len(pieces) - 2, 2)] + [[p] for p in pieces[-2:]]
    else:
        run = 1
        while run * shard % 16 or run * 8 < ring_size:
            run *= 2
        line = [own_piece, *pieces]
        units = [line[i : i + run] for i in range(0, len(line), run)]
    n_units = len(units)

    def hop(step, start, token):
        held[step, start] = lax.ppermute(after(held[step - 1, start], *token), "field", ring)

    def parts_of(unit):
        return [cholesky_tensor if piece == own_piece else held[piece[0], piece[1]] for piece in unit]

    for start, _ in cuts:
        hop(1, start, ())
    green = green_function.reshape(channels, across, CORES, rows, pairs)
    turned = field_noise.T
    if rows % 128:
        noise = turned.reshape(ring_size, shard, pair_size, rows).transpose(0, 2, 1, 3)
    else:
        noise = turned.reshape(ring_size, 1, shard, walkers)
    means = mean_field.T.reshape(ring_size, shard, channels)
    ready = [held[0, start] for start, _ in cuts] + [noise, means, mate_scalars]
    own_high, own_low, mate_high, mate_low = split_green(after(own_scalars, *ready), green)
    state = {"share": None, "token": ()}
    fronts, sums, own, mate = {}, {}, {}, {}

    def front(u):
        parts = parts_of(units[u])
        parts[0] = after(parts[0], *state["token"])
        sent = bias_of(mate_high, mate_low, parts)
        arrived = [lax.ppermute(part, "pair", mates) for part in sent]
        kept = bias_of(own_high, own_low, [after(parts[0], *sent), *parts[1:]])
        state["token"] = tuple(kept)
        fronts[u] = (kept, arrived)

    def across_chips(u):
        kept, arrived = fronts[u]
        total = add(kept, arrived)
        reach = CORES
        while 2 * reach < pair_size:
            more = lax.ppermute(total, "pair", [(i, i ^ reach) for i in range(pair_size)])
            total = add([total[c] for c in range(channels)], [more[c] for c in range(channels)])
            reach *= 2
        sums[u] = (total, lax.ppermute(total, "pair", [(i, i ^ reach) for i in range(pair_size)]))

    def back(u):
        total, more = sums[u]
        *own[u], state["share"] = cap(
            units[u], own_scalars, means, total, more, state["share"], fields
        )
        mate[u] = [lax.ppermute(part, "pair", mates) for part in own[u]]

    def send_on(piece):
        step, start, _, _ = piece
        arrived = held[step, start]
        if step + 1 < ring_size:
            hop(step + 1, start, state["token"])
        state["token"] = (*state["token"], arrived)

    if count > 1:
        front(0)
        across_chips(0)
        for step in range(1, ring_size):
            send_on(pieces[2 * step - 2])
            if step + 1 == ring_size:
                front(n_units - 2)
            state["token"] += (sums[step - 1][0],) + ((own[step - 2][0],) if step > 1 else ())
            send_on(pieces[2 * step - 1])
            if step + 1 < ring_size:
                front(step)
                across_chips(step)
                back(step - 1)
        across_chips(n_units - 2)
        state["token"] += (sums[n_units - 2][0],)
        front(n_units - 1)
        across_chips(n_units - 1)
        state["token"] += (sums[n_units - 1][0],)
    else:
        for u, unit in enumerate(units):
            for piece in unit:
                if piece != own_piece:
                    send_on(piece)
            front(u)
            across_chips(u)
    for u in range(n_units):
        if u not in own:
            back(u)
    line = [piece for unit in units for piece in unit]
    parts = [part for unit in units for part in parts_of(unit)]
    stack = stack_of([after(parts[0], *state["token"]), *parts[1:]])
    (one_body,) = finish(
        [part for u in range(n_units) for part in own[u]], noise, stack, line, own_scalars, scale, None, None, sizes
    )
    one_body, capped = finish(
        [part for u in range(n_units) for part in mate[u]], noise, stack, line, mate_scalars, scale, one_body,
        state["share"], sizes,
    )
    return (capped, one_body.reshape(walkers, channels, pairs))


def solution(mesh):
    return jax.shard_map(
        functools.partial(per_device, mesh.shape["field"], mesh.shape["pair"]),
        mesh=mesh,
        in_specs=(
            P(("grp", "field"), "pair"),
            P(None, ("grp", "field"), "pair"),
            P(None, "grp"),
            P(("grp", "field"), None),
        ),
        out_specs=(P(None, ("grp", "field", "pair"), None), P(("grp", "field"), None, "pair")),
        check_vma=False,
    )
```

time: 420 us -> 186 us (0.44)
  waiting for transfers between devices: 236 us -> 73.3 us
  matrix products: 105 us -> 0 us
  Pallas kernels: 0 us -> 83.1 us
  local copies, waits for them, and re-layouts: 58.8 us -> 11.9 us
  starting transfers between devices: 0.12 us -> 16.9 us
  between operations: 13.8 us -> 0.97 us
  other arithmetic: 5.65 us -> 0 us
    all_gather x2 -> x0, waiting for transfers between devices: 179 us -> none  [the longest x1 133 us: per_device(): lax.all_gather(cholesky_tensor, 'field', axis=0, tiled=True)]
    dot_general x2 -> x0, matrix products: 105 us -> none  [the longest x1 52.7 us: per_device(): jnp.einsum('cwp,fp->cwf', green_function, lax.all_gather(cholesky_tensor,...]
    pallas_call x0 -> x24, Pallas kernels: none -> 83.1 us  [the longest x10 36.1 us: bias_of(): pl.pallas_call(functools.partial(bias_kernel, len(parts)), out_shape=[jax...]
    ppermute x0 -> x31, waiting for transfers between devices: none -> 73.3 us  [the longest x6 59.9 us: hop(): lax.ppermute(after(held[step - 1, start], *token), 'field', ring)]
    reduce_scatter x1 -> x0, waiting for transfers between devices: 56.7 us -> none  [per_device(): lax.psum_scatter(partial_bias, 'pair', scatter_dimension=1, tiled=True)]
    unnamed x7 -> x6, local copies, waits for them, and re-layouts: 58.8 us -> 6.37 us
    ppermute x0 -> x31, starting transfers between devices: none -> 16.9 us  [the longest x6 6.34 us: hop(): lax.ppermute(after(held[step - 1, start], *token), 'field', ring)]
  transfers between devices with their start and end apart: 3 -> 31, of which waited for: 3 -> 7; matrix products, arithmetic and copies ran while one was open for 0% -> 1% of each run, Pallas kernels for 0% -> 35%
where the time goes in v2:
time: 186 us
  Pallas kernels  83.1 us (45%)
  waiting for transfers between devices  73.3 us (39%)
  starting transfers between devices  16.9 us (9%)
  local copies, waits for them, and re-layouts  11.9 us (6%)
    ppermute x6, waiting for transfers between devices, hop(): lax.ppermute(after(held[step - 1, start], *token), 'field', ring)  59.9 us
    pallas_call x10, Pallas kernels, bias_of(): pl.pallas_call(functools.partial(bias_kernel, len(parts)), out_shape=[jax...  36.1 us
    pallas_call x2, Pallas kernels, finish(): pl.pallas_call(functools.partial(finish_kernel, len(capped), len(unit), u...  34.1 us
    ppermute x5, waiting for transfers between devices, across_chips(): lax.ppermute(total, 'pair', [(i, i ^ reach) for i in range(pair_size)])  13.3 us
    unnamed x6, local copies, waits for them, and re-layouts  6.37 us
    ppermute x6, starting transfers between devices, hop(): lax.ppermute(after(held[step - 1, start], *token), 'field', ring)  6.34 us
    pallas_call x1, Pallas kernels, split_green(): pl.pallas_call(split_green_kernel, out_shape=[pltpu.VMEM((channels, acros...  6.2 us
    ppermute x5, starting transfers between devices, across_chips(): lax.ppermute(total, 'pair', [(i, i ^ reach) for i in range(pair_size)])  5.89 us
  transfers between devices with their start and end apart: 31, of which 7 were waited for; matrix products, arithmetic and copies ran while one was open for 1% of the time, Pallas kernels for 35%

profile of v2, /device:TPU:0, one launch (start us, length us, event | category | flops | bytes accessed | tf_op | source)
XLA Modules:
  0.0 186.1 jit_solution(18037324327923364111)
XLA Ops:
  0.6 2.8 %fusion = (f32[96,2304]{1,0:T(8,128)}, f32[96,2304]{1,0:T(8,128)}) fusion(f32[192,2304]{1,0:T(8,128)} %refs_0_.2), kind=kLoop, calls=%fused_computation | loop fusion | bytes 3538944 | tf_op jit(solution)/shard_map/slice | solution.py:284
  3.4 3.0 %collective-permute-start.5 = (f32[96,2304]{1,0:T(8,128)}, f32[96,2304]{1,0:T(8,128)}, u32[]{:S(2)}, u32[]{:S(2)}) collective-permute-start(f32[96,2304]{1,0:T(8,128)} %get-tuple-element.115), channel_id=1, source_target_pairs={{0,4},{4,8},{8,12},{12,0},{1,5},{5,9},{9,13},{13,1},{2,6},{6,10},{... | collective-permute-start | bytes 2654216 | tf_op jit(solution)/shard_map/ppermute | solution.py:298
  6.4 1.6 collective-permute-start.6
  8.4 2.4 %copy.12 = f32[768,1024]{1,0:T(8,128)S(1)} copy(f32[768,1024]{0,1:T(8,128)} %bitcast.34) | data formatting | bytes 6291456 | tf_op jit(solution)/shard_map/transpose | solution.py:306
  10.8 6.4 %copy-done.1 = f32[2,1024,2304]{2,1,0:T(8,128)S(1)} copy-done((f32[2,1024,2304]{2,1,0:T(8,128)S(1)}, f32[2,1024,2304]{2,1,0:T(8,128)}, u32[]{:S(2)}) %copy-start.1) | copy-done | bytes 18874392
  17.1 6.2 %split_green.1 = (bf16[2,2,256,2304]{3,2,1,0:T(8,128)(2,1)S(1)}, bf16[2,2,256,2304]{3,2,1,0:T(8,128)(2,1)S(1)}, bf16[2,2,256,2304]{3,2,1,0:T(8,128)(2,1)S(1)}, bf16[2,2,256,2304]{3,2,1,0:T(8,128)(2,1)S(1)}) custom-call(s32[6]{0:T(128)S(1)} %stack.40.s_ref, f32[2,2,2,256,2304]{4,3,2,1,0:T(8,128)S(1)} %bitcast.27), custom_call_target="tpu_custom_call" | custom-call | flops 1 | bytes 1 | tf_op jit(solution)/shard_map/split_green/pallas_call | solution.py:48
  23.3 3.5 %bias.10 = (f32[2,192,256]{2,1,0:T(8,128)S(1)}, f32[2,192,256]{2,1,0:T(8,128)S(1)}) custom-call(bf16[2,2,256,2304]{3,2,1,0:T(8,128)(2,1)S(1)} %get-tuple-element.61.high_ref, bf16[2,2,256,2304]{3,2,1,0:T(8,128)(2,1)S(1)} %get-tuple-element.62.low_ref, f32[192,2304]{1,0:T(8,128)S(1)} %copy-done), custom_call_target="tpu_custom_call" | custom-call | flops 1 | bytes 1 | tf_op jit(solution)/shard_map/bias/pallas_call | solution.py:78
  27.4 3.5 %bias.11 = (f32[2,192,256]{2,1,0:T(8,128)S(1)}, f32[2,192,256]{2,1,0:T(8,128)S(1)}) custom-call(bf16[2,2,256,2304]{3,2,1,0:T(8,128)(2,1)S(1)} %get-tuple-element.59.high_ref, bf16[2,2,256,2304]{3,2,1,0:T(8,128)(2,1)S(1)} %get-tuple-element.60.low_ref, f32[192,2304]{1,0:T(8,128)S(1)} %copy-done), custom_call_target="tpu_custom_call" | custom-call | flops 1 | bytes 1 | tf_op jit(solution)/shard_map/bias/pallas_call | solution.py:78
  30.9 1.6 collective-permute-start.12
  32.7 15.5 %collective-permute-done.6.refs_1_.refs_2_ = f32[96,2304]{1,0:T(8,128)} collective-permute-done((f32[96,2304]{1,0:T(8,128)}, f32[96,2304]{1,0:T(8,128)}, u32[]{:S(2)}, u32[]{:S(2)}) %collective-permute-start.6) | collective-permute-done | bytes 884768 | tf_op jit(solution)/shard_map/ppermute | solution.py:298
  48.2 1.7 collective-permute-start.2
  49.9 4.9 %bias.12 = (f32[2,192,256]{2,1,0:T(8,128)S(1)}, f32[2,192,256]{2,1,0:T(8,128)S(1)}) custom-call(bf16[2,2,256,2304]{3,2,1,0:T(8,128)(2,1)S(1)} %get-tuple-element.61.high_ref, bf16[2,2,256,2304]{3,2,1,0:T(8,128)(2,1)S(1)} %get-tuple-element.62.low_ref, f32[96,2304]{1,0:T(8,128)} %collective-permute-done.5.refs_0_.refs_1_, ...), custom_call_target="tpu_custom_call" | custom-call | flops 1 | bytes 1 | tf_op jit(solution)/shard_map/bias/pallas_call | solution.py:78
  55.5 4.9 %bias.13 = (f32[2,192,256]{2,1,0:T(8,128)S(1)}, f32[2,192,256]{2,1,0:T(8,128)S(1)}) custom-call(bf16[2,2,256,2304]{3,2,1,0:T(8,128)(2,1)S(1)} %get-tuple-element.59.high_ref, bf16[2,2,256,2304]{3,2,1,0:T(8,128)(2,1)S(1)} %get-tuple-element.60.low_ref, f32[96,2304]{1,0:T(8,128)} %collective-permute-done.5.refs_0_.refs_1_, ...), custom_call_target="tpu_custom_call" | custom-call | flops 1 | bytes 1 | tf_op jit(solution)/shard_map/bias/pallas_call | solution.py:78
  60.4 6.6 %collective-permute-done.12.refs_0_.refs_3_ = f32[96,2304]{1,0:T(8,128)S(1)} collective-permute-done((f32[96,2304]{1,0:T(8,128)}, f32[96,2304]{1,0:T(8,128)S(1)}, u32[]{:S(2)}, u32[]{:S(2)}) %collective-permute-start.12) | collective-permute-done | bytes 884768 | tf_op jit(solution)/shard_map/ppermute | solution.py:298
  67.1 0.8 cap.5
  68.0 18.0 %collective-permute-done.13.refs_1_.refs_4_ = f32[96,2304]{1,0:T(8,128)S(1)} collective-permute-done((f32[96,2304]{1,0:T(8,128)}, f32[96,2304]{1,0:T(8,128)S(1)}, u32[]{:S(2)}, u32[]{:S(2)}) %collective-permute-start.13) | collective-permute-done | bytes 884768 | tf_op jit(solution)/shard_map/ppermute | solution.py:298
  86.0 1.7 collective-permute-start.9
  87.7 3.5 %bias.14 = (f32[2,192,256]{2,1,0:T(8,128)S(1)}, f32[2,192,256]{2,1,0:T(8,128)S(1)}) custom-call(bf16[2,2,256,2304]{3,2,1,0:T(8,128)(2,1)S(1)} %get-tuple-element.61.high_ref, bf16[2,2,256,2304]{3,2,1,0:T(8,128)(2,1)S(1)} %get-tuple-element.62.low_ref, f32[96,2304]{1,0:T(8,128)S(1)} %collective-permute-done.12.refs_0_.refs_3_, ...), custom_call_target="tpu_custom_call" | custom-call | flops 1 | bytes 1 | tf_op jit(solution)/shard_map/bias/pallas_call | solution.py:78
  91.8 3.5 %bias.15 = (f32[2,192,256]{2,1,0:T(8,128)S(1)}, f32[2,192,256]{2,1,0:T(8,128)S(1)}) custom-call(bf16[2,2,256,2304]{3,2,1,0:T(8,128)(2,1)S(1)} %get-tuple-element.59.high_ref, bf16[2,2,256,2304]{3,2,1,0:T(8,128)(2,1)S(1)} %get-tuple-element.60.low_ref, f32[96,2304]{1,0:T(8,128)S(1)} %collective-permute-done.12.refs_0_.refs_3_, ...), custom_call_target="tpu_custom_call" | custom-call | flops 1 | bytes 1 | tf_op jit(solution)/shard_map/bias/pallas_call | solution.py:78
  95.8 9.1 %collective-permute-done.19.refs_0_.refs_5_ = f32[96,2304]{1,0:T(8,128)S(1)} collective-permute-done((f32[96,2304]{1,0:T(8,128)S(1)}, f32[96,2304]{1,0:T(8,128)S(1)}, u32[]{:S(2)}, u32[]{:S(2)}) %collective-permute-start.19) | collective-permute-done | bytes 884768 | tf_op jit(solution)/shard_map/ppermute | solution.py:298
  105.0 3.1 %bias.16 = (f32[2,96,256]{2,1,0:T(8,128)S(1)}, f32[2,96,256]{2,1,0:T(8,128)S(1)}) custom-call(bf16[2,2,256,2304]{3,2,1,0:T(8,128)(2,1)S(1)} %get-tuple-element.61.high_ref, bf16[2,2,256,2304]{3,2,1,0:T(8,128)(2,1)S(1)} %get-tuple-element.62.low_ref, f32[96,2304]{1,0:T(8,128)S(1)} %collective-permute-done.19.refs_0_.refs_5_), custom_call_target="tpu_custom_call" | custom-call | flops 1 | bytes 1 | tf_op jit(solution)/shard_map/bias/pallas_call | solution.py:78
  108.6 0.8 cap.6
  109.4 3.1 %bias.17 = (f32[2,96,256]{2,1,0:T(8,128)S(1)}, f32[2,96,256]{2,1,0:T(8,128)S(1)}) custom-call(bf16[2,2,256,2304]{3,2,1,0:T(8,128)(2,1)S(1)} %get-tuple-element.59.high_ref, bf16[2,2,256,2304]{3,2,1,0:T(8,128)(2,1)S(1)} %get-tuple-element.60.low_ref, f32[96,2304]{1,0:T(8,128)S(1)} %collective-permute-done.19.refs_0_.refs_5_), custom_call_target="tpu_custom_call" | custom-call | flops 1 | bytes 1 | tf_op jit(solution)/shard_map/bias/pallas_call | solution.py:78
  112.5 10.6 %collective-permute-done.25.refs_0_.refs_6_ = f32[96,2304]{1,0:T(8,128)S(1)} collective-permute-done((f32[96,2304]{1,0:T(8,128)S(1)}, f32[96,2304]{1,0:T(8,128)S(1)}, u32[]{:S(2)}, u32[]{:S(2)}) %collective-permute-start.25) | collective-permute-done | bytes 884768 | tf_op jit(solution)/shard_map/ppermute | solution.py:298
  123.1 3.1 %bias.18 = (f32[2,96,256]{2,1,0:T(8,128)S(1)}, f32[2,96,256]{2,1,0:T(8,128)S(1)}) custom-call(bf16[2,2,256,2304]{3,2,1,0:T(8,128)(2,1)S(1)} %get-tuple-element.61.high_ref, bf16[2,2,256,2304]{3,2,1,0:T(8,128)(2,1)S(1)} %get-tuple-element.62.low_ref, f32[96,2304]{1,0:T(8,128)S(1)} %collective-permute-done.25.refs_0_.refs_6_), custom_call_target="tpu_custom_call" | custom-call | flops 1 | bytes 1 | tf_op jit(solution)/shard_map/bias/pallas_call | solution.py:78
  126.8 1.5 collective-permute-start.22
  128.3 3.1 %bias.19 = (f32[2,96,256]{2,1,0:T(8,128)S(1)}, f32[2,96,256]{2,1,0:T(8,128)S(1)}) custom-call(bf16[2,2,256,2304]{3,2,1,0:T(8,128)(2,1)S(1)} %get-tuple-element.59.high_ref, bf16[2,2,256,2304]{3,2,1,0:T(8,128)(2,1)S(1)} %get-tuple-element.60.low_ref, f32[96,2304]{1,0:T(8,128)S(1)} %collective-permute-done.25.refs_0_.refs_6_), custom_call_target="tpu_custom_call" | custom-call | flops 1 | bytes 1 | tf_op jit(solution)/shard_map/bias/pallas_call | solution.py:78
  133.4 5.3 %collective-permute-done.22.more_ref = f32[2,2,96,256]{3,2,1,0:T(8,128)S(1)} collective-permute-done((f32[2,2,96,256]{3,2,1,0:T(8,128)S(1)}, f32[2,2,96,256]{3,2,1,0:T(8,128)S(1)}, u32[]{:S(2)}, u32[]{:S(2)}) %collective-permute-start.22) | collective-permute-done | bytes 393248 | tf_op jit(solution)/shard_map/ppermute | solution.py:334
  138.7 8.0 %collective-permute-done.28.more_ref = f32[2,2,96,256]{3,2,1,0:T(8,128)S(1)} collective-permute-done((f32[2,2,96,256]{3,2,1,0:T(8,128)S(1)}, f32[2,2,96,256]{3,2,1,0:T(8,128)S(1)}, u32[]{:S(2)}, u32[]{:S(2)}) %collective-permute-start.28) | collective-permute-done | bytes 393248 | tf_op jit(solution)/shard_map/ppermute | solution.py:334
  149.3 2.8 %stack_cholesky.1.refs_17_ = bf16[2304,2304]{1,0:T(8,128)(2,1)S(1)} custom-call(f32[192,2304]{1,0:T(8,128)S(1)} %copy-done, f32[96,2304]{1,0:T(8,128)} %collective-permute-done.5.refs_0_.refs_1_, f32[96,2304]{1,0:T(8,128)} %collective-permute-done.6.refs_1_.refs_2_, f32[96,2304]{1,0:T(8,128)S(1)} %collective-permute-done.12.refs_0_.refs_3_, ...), custom_call_target="tpu_custom_call" | custom-call | flops 1 | bytes 1 | tf_op jit(solution)/shard_map/stack_cholesky/pallas_call | solution.py:182
  152.0 16.8 %finish.2.refs_18_ = f32[2,2,256,2,2304]{4,3,2,1,0:T(2,128)} custom-call(s32[6]{0:T(128)S(1)} %stack.40.s_ref, f32[2,192,256]{2,1,0:T(8,128)S(1)} %get-tuple-element.68.refs_0_, f32[2,192,256]{2,1,0:T(8,128)S(1)} %get-tuple-element.69.refs_1_, f32[2,192,256]{2,1,0:T(8,128)S(1)} %get-tuple-element.77.refs_2_, f32[2,192,256]{2,1,0:T(8,128)S(1)} %get-tuple-element.78.refs_3_, ...), custom_call_target="tpu_custom_call" | custom-call | flops 1 | bytes 1 | tf_op jit(solution)/shard_map/finish/pallas_call | solution.py:241
  168.9 17.3 %finish.3 = (f32[2,2,256,2,2304]{4,3,2,1,0:T(2,128)}, f32[2,256,768]{2,1,0:T(8,128)}) custom-call(s32[6]{0:T(128)S(1)} %stack.38.s_ref, f32[2,192,256]{2,1,0:T(8,128)S(1)} %collective-permute-done.3.refs_0_, f32[2,192,256]{2,1,0:T(8,128)S(1)} %collective-permute-done.4.refs_1_, ...), custom_call_target="tpu_custom_call", output_to_operand_aliasing={{0}: (19, {})} | custom-call | flops 1 | bytes 1 | tf_op jit(solution)/shard_map/finish/pallas_call | solution.py:241
  (65 shorter events, 8.6 us)
Async XLA Ops:
  0.6 7.5 %copy-start.2 = (f32[2,768]{1,0:T(2,128)S(1)}, f32[2,768]{1,0:T(2,128)}, u32[]{:S(2)}) copy-start(f32[2,768]{1,0:T(2,128)} %param.6) | copy-start | bytes 18436
  3.4 27.5 %collective-permute-start.5 = (f32[96,2304]{1,0:T(8,128)}, f32[96,2304]{1,0:T(8,128)}, u32[]{:S(2)}, u32[]{:S(2)}) collective-permute-start(f32[96,2304]{1,0:T(8,128)} %get-tuple-element.115), channel_id=1, source_target_pairs={{0,4},{4,8},{8,12},{12,0},{1,5},{5,9},{9,13},{13,1},{2,6},{6,10},{... | collective-permute-start | bytes 2654216 | tf_op jit(solution)/shard_map/ppermute | solution.py:298
  6.4 41.8 %collective-permute-start.6 = (f32[96,2304]{1,0:T(8,128)}, f32[96,2304]{1,0:T(8,128)}, u32[]{:S(2)}, u32[]{:S(2)}) collective-permute-start(f32[96,2304]{1,0:T(8,128)} %get-tuple-element.114), channel_id=1, source_target_pairs={{0,4},{4,8},{8,12},{12,0},{1,5},{5,9},{9,13},{13,1},{2,6},{6,10},{... | collective-permute-start | bytes 2654216 | tf_op jit(solution)/shard_map/ppermute | solution.py:298
  26.8 5.7 %collective-permute-start = (f32[2,192,256]{2,1,0:T(8,128)S(1)}, f32[2,192,256]{2,1,0:T(8,128)S(1)}, u32[]{:S(2)}, u32[]{:S(2)}) collective-permute-start(f32[2,192,256]{2,1,0:T(8,128)S(1)} %get-tuple-element.63), channel_id=1, source_target_pairs={{0,1},{1,0},{2,3},{3,2},{4,5},{5,4},{6,7},{7,6},{8,9},{9,8},{10,11... | collective-permute-start | bytes 1179656 | tf_op jit(solution)/shard_map/ppermute | solution.py:321
  26.9 5.7 %collective-permute-start.1 = (f32[2,192,256]{2,1,0:T(8,128)S(1)}, f32[2,192,256]{2,1,0:T(8,128)S(1)}, u32[]{:S(2)}, u32[]{:S(2)}) collective-permute-start(f32[2,192,256]{2,1,0:T(8,128)S(1)} %get-tuple-element.64), channel_id=1, source_target_pairs={{0,1},{1,0},{2,3},{3,2},{4,5},{5,4},{6,7},{7,6},{8,9},{9,8},{10,11... | collective-permute-start | bytes 1179656 | tf_op jit(solution)/shard_map/ppermute | solution.py:321
  30.9 36.1 %collective-permute-start.12 = (f32[96,2304]{1,0:T(8,128)}, f32[96,2304]{1,0:T(8,128)S(1)}, u32[]{:S(2)}, u32[]{:S(2)}) collective-permute-start(f32[96,2304]{1,0:T(8,128)} %collective-permute-done.5.refs_0_.refs_1_), channel_id=1, source_target_pairs={{0,4},{4,8},{8,12},{12,0},{1,5},{5,9},{9,13},{13,1},{2,6},{6,10},{... | collective-permute-start | bytes 2654216 | tf_op jit(solution)/shard_map/ppermute | solution.py:298
  48.2 37.8 %collective-permute-start.13 = (f32[96,2304]{1,0:T(8,128)}, f32[96,2304]{1,0:T(8,128)S(1)}, u32[]{:S(2)}, u32[]{:S(2)}) collective-permute-start(f32[96,2304]{1,0:T(8,128)} %collective-permute-done.6.refs_1_.refs_2_), channel_id=1, source_target_pairs={{0,4},{4,8},{8,12},{12,0},{1,5},{5,9},{9,13},{13,1},{2,6},{6,10},{... | collective-permute-start | bytes 2654216 | tf_op jit(solution)/shard_map/ppermute | solution.py:298
  48.2 18.9 %collective-permute-start.2 = (f32[2,2,192,256]{3,2,1,0:T(8,128)S(1)}, f32[2,2,192,256]{3,2,1,0:T(8,128)S(1)}, u32[]{:S(2)}, u32[]{:S(2)}) collective-permute-start(f32[2,2,192,256]{3,2,1,0:T(8,128)S(1)} %add.30.sums_ref), channel_id=1, source_target_pairs={{0,2},{1,3},{2,0},{3,1},{4,6},{5,7},{6,4},{7,5},{8,10},{9,11},{10,... | collective-permute-start | bytes 2359304 | tf_op jit(solution)/shard_map/ppermute | solution.py:334
  54.9 13.0 %collective-permute-start.7 = (f32[2,192,256]{2,1,0:T(8,128)S(1)}, f32[2,192,256]{2,1,0:T(8,128)S(1)}, u32[]{:S(2)}, u32[]{:S(2)}) collective-permute-start(f32[2,192,256]{2,1,0:T(8,128)S(1)} %get-tuple-element.71), channel_id=1, source_target_pairs={{0,1},{1,0},{2,3},{3,2},{4,5},{5,4},{6,7},{7,6},{8,9},{9,8},{10,11... | collective-permute-start | bytes 1179656 | tf_op jit(solution)/shard_map/ppermute | solution.py:321
  55.0 12.9 %collective-permute-start.8 = (f32[2,192,256]{2,1,0:T(8,128)S(1)}, f32[2,192,256]{2,1,0:T(8,128)S(1)}, u32[]{:S(2)}, u32[]{:S(2)}) collective-permute-start(f32[2,192,256]{2,1,0:T(8,128)S(1)} %get-tuple-element.72), channel_id=1, source_target_pairs={{0,1},{1,0},{2,3},{3,2},{4,5},{5,4},{6,7},{7,6},{8,9},{9,8},{10,11... | collective-permute-start | bytes 1179656 | tf_op jit(solution)/shard_map/ppermute | solution.py:321
  67.0 37.9 %collective-permute-start.19 = (f32[96,2304]{1,0:T(8,128)S(1)}, f32[96,2304]{1,0:T(8,128)S(1)}, u32[]{:S(2)}, u32[]{:S(2)}) collective-permute-start(f32[96,2304]{1,0:T(8,128)S(1)} %collective-permute-done.12.refs_0_.refs_3_), channel_id=1, source_target_pairs={{0,4},{4,8},{8,12},{12,0},{1,5},{5,9},{9,13},{13,1},{2,6},{6,10},{... | collective-permute-start | bytes 2654216 | tf_op jit(solution)/shard_map/ppermute | solution.py:298
  86.0 37.1 %collective-permute-start.25 = (f32[96,2304]{1,0:T(8,128)S(1)}, f32[96,2304]{1,0:T(8,128)S(1)}, u32[]{:S(2)}, u32[]{:S(2)}) collective-permute-start(f32[96,2304]{1,0:T(8,128)S(1)} %collective-permute-done.13.refs_1_.refs_4_), channel_id=1, source_target_pairs={{0,4},{4,8},{8,12},{12,0},{1,5},{5,9},{9,13},{13,1},{2,6},{6,10},{... | collective-permute-start | bytes 2654216 | tf_op jit(solution)/shard_map/ppermute | solution.py:298
  86.0 22.6 %collective-permute-start.9 = (f32[2,2,192,256]{3,2,1,0:T(8,128)S(1)}, f32[2,2,192,256]{3,2,1,0:T(8,128)S(1)}, u32[]{:S(2)}, u32[]{:S(2)}) collective-permute-start(f32[2,2,192,256]{3,2,1,0:T(8,128)S(1)} %add.31.sums_ref), channel_id=1, source_target_pairs={{0,2},{1,3},{2,0},{3,1},{4,6},{5,7},{6,4},{7,5},{8,10},{9,11},{10,... | collective-permute-start | bytes 2359304 | tf_op jit(solution)/shard_map/ppermute | solution.py:334
  91.3 4.1 %collective-permute-start.14 = (f32[2,192,256]{2,1,0:T(8,128)S(1)}, f32[2,192,256]{2,1,0:T(8,128)S(1)}, u32[]{:S(2)}, u32[]{:S(2)}) collective-permute-start(f32[2,192,256]{2,1,0:T(8,128)S(1)} %get-tuple-element.82), channel_id=1, source_target_pairs={{0,1},{1,0},{2,3},{3,2},{4,5},{5,4},{6,7},{7,6},{8,9},{9,8},{10,11... | collective-permute-start | bytes 1179656 | tf_op jit(solution)/shard_map/ppermute | solution.py:321
  91.3 4.0 %collective-permute-start.15 = (f32[2,192,256]{2,1,0:T(8,128)S(1)}, f32[2,192,256]{2,1,0:T(8,128)S(1)}, u32[]{:S(2)}, u32[]{:S(2)}) collective-permute-start(f32[2,192,256]{2,1,0:T(8,128)S(1)} %get-tuple-element.83), channel_id=1, source_target_pairs={{0,1},{1,0},{2,3},{3,2},{4,5},{5,4},{6,7},{7,6},{8,9},{9,8},{10,11... | collective-permute-start | bytes 1179656 | tf_op jit(solution)/shard_map/ppermute | solution.py:321
  95.5 36.6 %collective-permute-start.16 = (f32[2,2,192,256]{3,2,1,0:T(8,128)S(1)}, f32[2,2,192,256]{3,2,1,0:T(8,128)S(1)}, u32[]{:S(2)}, u32[]{:S(2)}) collective-permute-start(f32[2,2,192,256]{3,2,1,0:T(8,128)S(1)} %add.32.sums_ref), channel_id=1, source_target_pairs={{0,2},{1,3},{2,0},{3,1},{4,6},{5,7},{6,4},{7,5},{8,10},{9,11},{10,... | collective-permute-start | bytes 2359304 | tf_op jit(solution)/shard_map/ppermute | solution.py:334
  108.0 4.4 %collective-permute-start.20 = (f32[2,96,256]{2,1,0:T(8,128)S(1)}, f32[2,96,256]{2,1,0:T(8,128)S(1)}, u32[]{:S(2)}, u32[]{:S(2)}) collective-permute-start(f32[2,96,256]{2,1,0:T(8,128)S(1)} %get-tuple-element.92), channel_id=1, source_target_pairs={{0,1},{1,0},{2,3},{3,2},{4,5},{5,4},{6,7},{7,6},{8,9},{9,8},{10,11... | collective-permute-start | bytes 589832 | tf_op jit(solution)/shard_map/ppermute | solution.py:321
  108.1 4.3 %collective-permute-start.21 = (f32[2,96,256]{2,1,0:T(8,128)S(1)}, f32[2,96,256]{2,1,0:T(8,128)S(1)}, u32[]{:S(2)}, u32[]{:S(2)}) collective-permute-start(f32[2,96,256]{2,1,0:T(8,128)S(1)} %get-tuple-element.93), channel_id=1, source_target_pairs={{0,1},{1,0},{2,3},{3,2},{4,5},{5,4},{6,7},{7,6},{8,9},{9,8},{10,11... | collective-permute-start | bytes 589832 | tf_op jit(solution)/shard_map/ppermute | solution.py:321
  126.2 5.2 %collective-permute-start.26 = (f32[2,96,256]{2,1,0:T(8,128)S(1)}, f32[2,96,256]{2,1,0:T(8,128)S(1)}, u32[]{:S(2)}, u32[]{:S(2)}) collective-permute-start(f32[2,96,256]{2,1,0:T(8,128)S(1)} %get-tuple-element.102), channel_id=1, source_target_pairs={{0,1},{1,0},{2,3},{3,2},{4,5},{5,4},{6,7},{7,6},{8,9},{9,8},{10,11... | collective-permute-start | bytes 589832 | tf_op jit(solution)/shard_map/ppermute | solution.py:321
  126.2 5.1 %collective-permute-start.27 = (f32[2,96,256]{2,1,0:T(8,128)S(1)}, f32[2,96,256]{2,1,0:T(8,128)S(1)}, u32[]{:S(2)}, u32[]{:S(2)}) collective-permute-start(f32[2,96,256]{2,1,0:T(8,128)S(1)} %get-tuple-element.103), channel_id=1, source_target_pairs={{0,1},{1,0},{2,3},{3,2},{4,5},{5,4},{6,7},{7,6},{8,9},{9,8},{10,11... | collective-permute-start | bytes 589832 | tf_op jit(solution)/shard_map/ppermute | solution.py:321
  126.7 6.6 %collective-permute-start.4 = (f32[2,192,256]{2,1,0:T(8,128)S(1)}, f32[2,192,256]{2,1,0:T(8,128)S(1)}, u32[]{:S(2)}, u32[]{:S(2)}) collective-permute-start(f32[2,192,256]{2,1,0:T(8,128)S(1)} %get-tuple-element.69.refs_1_), channel_id=1, source_target_pairs={{0,1},{1,0},{2,3},{3,2},{4,5},{5,4},{6,7},{7,6},{8,9},{9,8},{10,11... | collective-permute-start | bytes 1179656 | tf_op jit(solution)/shard_map/ppermute | solution.py:341
  126.8 11.9 %collective-permute-start.22 = (f32[2,2,96,256]{3,2,1,0:T(8,128)S(1)}, f32[2,2,96,256]{3,2,1,0:T(8,128)S(1)}, u32[]{:S(2)}, u32[]{:S(2)}) collective-permute-start(f32[2,2,96,256]{3,2,1,0:T(8,128)S(1)} %add.33.sums_ref), channel_id=1, source_target_pairs={{0,2},{1,3},{2,0},{3,1},{4,6},{5,7},{6,4},{7,5},{8,10},{9,11},{10,... | collective-permute-start | bytes 1179656 | tf_op jit(solution)/shard_map/ppermute | solution.py:334
  131.4 15.3 %collective-permute-start.28 = (f32[2,2,96,256]{3,2,1,0:T(8,128)S(1)}, f32[2,2,96,256]{3,2,1,0:T(8,128)S(1)}, u32[]{:S(2)}, u32[]{:S(2)}) collective-permute-start(f32[2,2,96,256]{3,2,1,0:T(8,128)S(1)} %add.34.sums_ref), channel_id=1, source_target_pairs={{0,2},{1,3},{2,0},{3,1},{4,6},{5,7},{6,4},{7,5},{8,10},{9,11},{10,... | collective-permute-start | bytes 1179656 | tf_op jit(solution)/shard_map/ppermute | solution.py:334
  132.0 16.0 %collective-permute-start.3 = (f32[2,192,256]{2,1,0:T(8,128)S(1)}, f32[2,192,256]{2,1,0:T(8,128)S(1)}, u32[]{:S(2)}, u32[]{:S(2)}) collective-permute-start(f32[2,192,256]{2,1,0:T(8,128)S(1)} %get-tuple-element.68.refs_0_), channel_id=1, source_target_pairs={{0,1},{1,0},{2,3},{3,2},{4,5},{5,4},{6,7},{7,6},{8,9},{9,8},{10,11... | collective-permute-start | bytes 1179656 | tf_op jit(solution)/shard_map/ppermute | solution.py:341
  132.0 16.6 %collective-permute-start.11 = (f32[2,192,256]{2,1,0:T(8,128)S(1)}, f32[2,192,256]{2,1,0:T(8,128)S(1)}, u32[]{:S(2)}, u32[]{:S(2)}) collective-permute-start(f32[2,192,256]{2,1,0:T(8,128)S(1)} %get-tuple-element.78.refs_3_), channel_id=1, source_target_pairs={{0,1},{1,0},{2,3},{3,2},{4,5},{5,4},{6,7},{7,6},{8,9},{9,8},{10,11... | collective-permute-start | bytes 1179656 | tf_op jit(solution)/shard_map/ppermute | solution.py:341
  133.3 15.4 %collective-permute-start.10 = (f32[2,192,256]{2,1,0:T(8,128)S(1)}, f32[2,192,256]{2,1,0:T(8,128)S(1)}, u32[]{:S(2)}, u32[]{:S(2)}) collective-permute-start(f32[2,192,256]{2,1,0:T(8,128)S(1)} %get-tuple-element.77.refs_2_), channel_id=1, source_target_pairs={{0,1},{1,0},{2,3},{3,2},{4,5},{5,4},{6,7},{7,6},{8,9},{9,8},{10,11... | collective-permute-start | bytes 1179656 | tf_op jit(solution)/shard_map/ppermute | solution.py:341
  138.7 10.5 %collective-permute-start.17 = (f32[2,192,256]{2,1,0:T(8,128)S(1)}, f32[2,192,256]{2,1,0:T(8,128)S(1)}, u32[]{:S(2)}, u32[]{:S(2)}) collective-permute-start(f32[2,192,256]{2,1,0:T(8,128)S(1)} %get-tuple-element.88.refs_4_), channel_id=1, source_target_pairs={{0,1},{1,0},{2,3},{3,2},{4,5},{5,4},{6,7},{7,6},{8,9},{9,8},{10,11... | collective-permute-start | bytes 1179656 | tf_op jit(solution)/shard_map/ppermute | solution.py:341
  146.7 22.1 %collective-permute-start.18 = (f32[2,192,256]{2,1,0:T(8,128)S(1)}, f32[2,192,256]{2,1,0:T(8,128)S(1)}, u32[]{:S(2)}, u32[]{:S(2)}) collective-permute-start(f32[2,192,256]{2,1,0:T(8,128)S(1)} %get-tuple-element.89.refs_5_), channel_id=1, source_target_pairs={{0,1},{1,0},{2,3},{3,2},{4,5},{5,4},{6,7},{7,6},{8,9},{9,8},{10,11... | collective-permute-start | bytes 1179656 | tf_op jit(solution)/shard_map/ppermute | solution.py:341
  148.1 20.7 %collective-permute-start.23 = (f32[2,96,256]{2,1,0:T(8,128)S(1)}, f32[2,96,256]{2,1,0:T(8,128)S(1)}, u32[]{:S(2)}, u32[]{:S(2)}) collective-permute-start(f32[2,96,256]{2,1,0:T(8,128)S(1)} %get-tuple-element.98.refs_6_), channel_id=1, source_target_pairs={{0,1},{1,0},{2,3},{3,2},{4,5},{5,4},{6,7},{7,6},{8,9},{9,8},{10,11... | collective-permute-start | bytes 589832 | tf_op jit(solution)/shard_map/ppermute | solution.py:341
  148.7 20.2 %collective-permute-start.24 = (f32[2,96,256]{2,1,0:T(8,128)S(1)}, f32[2,96,256]{2,1,0:T(8,128)S(1)}, u32[]{:S(2)}, u32[]{:S(2)}) collective-permute-start(f32[2,96,256]{2,1,0:T(8,128)S(1)} %get-tuple-element.99.refs_7_), channel_id=1, source_target_pairs={{0,1},{1,0},{2,3},{3,2},{4,5},{5,4},{6,7},{7,6},{8,9},{9,8},{10,11... | collective-permute-start | bytes 589832 | tf_op jit(solution)/shard_map/ppermute | solution.py:341
  148.8 20.1 %collective-permute-start.29 = (f32[2,96,256]{2,1,0:T(8,128)S(1)}, f32[2,96,256]{2,1,0:T(8,128)S(1)}, u32[]{:S(2)}, u32[]{:S(2)}) collective-permute-start(f32[2,96,256]{2,1,0:T(8,128)S(1)} %get-tuple-element.108.refs_8_), channel_id=1, source_target_pairs={{0,1},{1,0},{2,3},{3,2},{4,5},{5,4},{6,7},{7,6},{8,9},{9,8},{10,11... | collective-permute-start | bytes 589832 | tf_op jit(solution)/shard_map/ppermute | solution.py:341
  149.2 19.7 %collective-permute-start.30 = (f32[2,96,256]{2,1,0:T(8,128)S(1)}, f32[2,96,256]{2,1,0:T(8,128)S(1)}, u32[]{:S(2)}, u32[]{:S(2)}) collective-permute-start(f32[2,96,256]{2,1,0:T(8,128)S(1)} %get-tuple-element.109.refs_9_), channel_id=1, source_target_pairs={{0,1},{1,0},{2,3},{3,2},{4,5},{5,4},{6,7},{7,6},{8,9},{9,8},{10,11... | collective-permute-start | bytes 589832 | tf_op jit(solution)/shard_map/ppermute | solution.py:341
  (2 other events, 12.6 us)

commit v3 on v2

--- a/solution.py
+++ b/solution.py
@@ -190,69 +190,91 @@
     )(*chol)
 
 
-def finish_kernel(n, m, unit, scale, with_share, s_ref, *refs):
-    capped, noise, stack = refs[:n], refs[n : n + m], refs[n + m]
-    left = refs[-1]
-    out_ref = refs[-3] if with_share else refs[-2]
-    x, p = pl.program_id(0), pl.program_id(1)
-
-    if with_share:
-
-        @pl.when((x == 0) & (p == 0))
-        def _():
-            for c in range(2):
-                refs[-2][c] = refs[-4][c].T
+def begin_kernel(n, unit, s_ref, *refs):
+    mine, other, noise, (stack, out_ref) = refs[:n], refs[n : 2 * n], refs[2 * n : -2], refs[-2:]
+    x, core = pl.program_id(0), pl.program_id(1)
+    own = core == s_ref[0]
+    capped = [jnp.where(own, a[0], b[0]) for a, b in zip(mine, other)]
+    out_ref[x, core] = lax.dot_general(
+        stack_fields(capped, noise_pieces(noise, unit)), stack[...], DOT, preferred_element_type=jnp.float32
+    )
+
+
+def begin(mine, other, noise, stack, unit, scalars, sizes):
+    across, rows, pairs = sizes
+    in_specs = [pl.BlockSpec((1, *part.shape[1:]), lambda x, h, s: (x, 0, 0)) for part in (*mine, *other)]
+    in_specs += [
+        pl.BlockSpec(spec.block_shape, lambda x, h, s, at=spec.index_map: at(x, h, 0, s))
+        for spec in noise_specs(unit, noise, rows, rows)
+    ]
+    return pl.pallas_call(
+        functools.partial(begin_kernel, len(mine), unit),
+        out_shape=pltpu.VMEM((across, CORES, 2 * rows, pairs), jnp.float32),
+        grid_spec=pltpu.PrefetchScalarGridSpec(
+            num_scalar_prefetch=1, grid=(across, CORES), in_specs=[*in_specs, WHOLE], out_specs=WHOLE
+        ),
+        compiler_params=params(16),
+        cost_estimate=COST,
+        name="begin",
+    )(scalars, *mine, *other, *([noise] * len(unit)), stack)
+
+
+def finish_kernel(n, m, unit, scale, s_ref, *refs):
+    mine, other, noise = refs[:n], refs[n : 2 * n], refs[2 * n : 2 * n + m]
+    stack, prior, share, out_ref, turned_ref, left = refs[2 * n + m :]
+    turn, x, p = pl.program_id(0), pl.program_id(1), pl.program_id(2)
+    core = (s_ref[0] + turn) % CORES
+
+    @pl.when((turn == 0) & (x == 0) & (p == 0))
+    def _():
+        for c in range(2):
+            turned_ref[c] = share[c].T
 
     @pl.when(p == 0)
     def _():
-        left[...] = stack_fields([part[0] for part in capped], noise_pieces(noise, unit))
+        capped = [jnp.where(turn == 0, a[0], b[0]) for a, b in zip(mine, other)]
+        left[...] = stack_fields(capped, noise_pieces(noise, unit))
 
     width = out_ref.shape[-1]
     columns = pl.ds(pl.multiple_of(p * width, 128), width)
-    sums = scale * lax.dot_general(left[...], stack[:, columns], DOT, preferred_element_type=jnp.float32)
+    sums = lax.dot_general(left[...], stack[:, columns], DOT, preferred_element_type=jnp.float32)
     rows = sums.shape[0] // 2
     for c in range(2):
-        out_ref[0, 0, :, c, :] = sums[c * rows : (c + 1) * rows]
-
-
-def finish(capped, noise, stack, unit, scalars, scale, earlier, share, sizes):
+        part = slice(c * rows, (c + 1) * rows)
+        out_ref[0, 0, :, c, :] = scale * (prior[x, core, part, columns] + sums[part])
+
+
+def finish(mine, other, noise, stack, prior, share, unit, scalars, scale, sizes):
     across, rows, pairs = sizes
     tiles = 3 if pairs % 384 == 0 else 1
-    in_specs = [pl.BlockSpec((1, *part.shape[1:]), lambda x, p, s: (x, 0, 0)) for part in capped]
+    turned = (share.shape[0], share.shape[2], share.shape[1])
+    in_specs = [pl.BlockSpec((1, *part.shape[1:]), lambda t, x, p, s: (x, 0, 0)) for part in (*mine, *other)]
     in_specs += [
-        pl.BlockSpec(spec.block_shape, lambda x, p, s, at=spec.index_map: at(x, s[0], 0, s))
+        pl.BlockSpec(spec.block_shape, lambda t, x, p, s, at=spec.index_map: at(x, (s[0] + t) % CORES, 0, s))
         for spec in noise_specs(unit, noise, rows, rows)
     ]
-    in_specs += [WHOLE]
-    operands = [scalars, *capped, *([noise] * len(unit)), stack]
-    aliases = {}
-    if earlier is not None:
-        in_specs.append(pl.BlockSpec(memory_space=pl.ANY))
-        aliases = {len(operands): 0}
-        operands.append(earlier)
-    out_shape = [jax.ShapeDtypeStruct((across, CORES, rows, 2, pairs), jnp.float32)]
-    out_specs = [pl.BlockSpec((1, 1, rows, 2, pairs // tiles), lambda x, p, s: (x, s[0], 0, 0, p))]
-    if share is not None:
-        turned = (share.shape[0], share.shape[2], share.shape[1])
-        out_shape.append(jax.ShapeDtypeStruct(turned, jnp.float32))
-        out_specs.append(pl.BlockSpec(turned, lambda x, p, s: (0, 0, 0)))
-        in_specs.append(WHOLE)
-        operands.append(share)
-    return pl.pallas_call(
-        functools.partial(finish_kernel, len(capped), len(unit), unit, scale, share is not None),
-        out_shape=out_shape,
+    return pl.pallas_call(
+        functools.partial(finish_kernel, len(mine), len(unit), unit, scale),
+        out_shape=[
+            jax.ShapeDtypeStruct((across, CORES, rows, 2, pairs), jnp.float32),
+            jax.ShapeDtypeStruct(turned, jnp.float32),
+        ],
         grid_spec=pltpu.PrefetchScalarGridSpec(
             num_scalar_prefetch=1,
-            grid=(across, tiles),
-            in_specs=in_specs,
-            out_specs=out_specs,
+            grid=(CORES, across, tiles),
+            in_specs=[*in_specs, WHOLE, WHOLE, WHOLE],
+            out_specs=[
+                pl.BlockSpec(
+                    (1, 1, rows, 2, pairs // tiles), lambda t, x, p, s: (x, (s[0] + t) % CORES, 0, 0, p)
+                ),
+                pl.BlockSpec(turned, lambda t, x, p, s: (0, 0, 0)),
+            ],
             scratch_shapes=[pltpu.VMEM((2 * rows, stack.shape[0]), jnp.bfloat16)],
         ),
-        input_output_aliases=aliases,
-        compiler_params=params(36),
+        compiler_params=params(16),
         cost_estimate=COST,
         name="finish",
-    )(*operands)
+    )(scalars, *mine, *other, *([noise] * len(unit)), stack, prior, share)
 
 
 def after(x, *earlier):
@@ -333,10 +355,10 @@
             reach *= 2
         sums[u] = (total, lax.ppermute(total, "pair", [(i, i ^ reach) for i in range(pair_size)]))
 
-    def back(u):
+    def back(u, tie=()):
         total, more = sums[u]
         *own[u], state["share"] = cap(
-            units[u], own_scalars, means, total, more, state["share"], fields
+            units[u], own_scalars, after(means, *tie), total, more, state["share"], fields
         )
         mate[u] = [lax.ppermute(part, "pair", mates) for part in own[u]]
 
@@ -365,6 +387,7 @@
         front(n_units - 1)
         across_chips(n_units - 1)
         state["token"] += (sums[n_units - 1][0],)
+        final = 3
     else:
         for u, unit in enumerate(units):
             for piece in unit:
@@ -372,18 +395,28 @@
                     send_on(piece)
             front(u)
             across_chips(u)
-    for u in range(n_units):
+            if u:
+                back(u - 1)
+        state["token"] += (sums[n_units - 1][0],)
+        final = 1
+
+    def stack_and_pieces(chosen):
+        parts = [part for u in chosen for part in parts_of(units[u])]
+        return stack_of([after(parts[0], *state["token"]), *parts[1:]]), [piece for u in chosen for piece in units[u]]
+
+    def channels_of(capped, chosen):
+        return [part for u in chosen for part in capped[u]]
+
+    first, late = range(n_units - final), range(n_units - final, n_units)
+    stack, line = stack_and_pieces(first)
+    operator = begin(channels_of(own, first), channels_of(mate, first), noise, stack, line, own_scalars, sizes)
+    stack, line = stack_and_pieces(late)
+    for u in late:
         if u not in own:
-            back(u)
-    line = [piece for unit in units for piece in unit]
-    parts = [part for unit in units for part in parts_of(unit)]
-    stack = stack_of([after(parts[0], *state["token"]), *parts[1:]])
-    (one_body,) = finish(
-        [part for u in range(n_units) for part in own[u]], noise, stack, line, own_scalars, scale, None, None, sizes
-    )
+            back(u, (operator, stack))
     one_body, capped = finish(
-        [part for u in range(n_units) for part in mate[u]], noise, stack, line, mate_scalars, scale, one_body,
-        state["share"], sizes,
+        channels_of(own, late), channels_of(mate, late), noise, stack, operator, state["share"], line, own_scalars,
+        scale, sizes,
     )
     return (capped, one_body.reshape(walkers, channels, pairs))
 

time: 186 us -> 179 us (0.962)
  waiting for transfers between devices: 73.3 us -> 60.5 us
  Pallas kernels: 83.1 us -> 86.2 us
  starting transfers between devices: 16.9 us -> 18.9 us
    ppermute x5, waiting for transfers between devices: 13.3 us -> 0.01 us  [across_chips(): lax.ppermute(total, 'pair', [(i, i ^ reach) for i in range(pair_size)])]
    pallas_call x2, Pallas kernels: 34.1 us -> 36.3 us  [the longest x1 22.2 us: finish(): pl.pallas_call(functools.partial(finish_kernel, len(mine), len(unit), uni...]
    ppermute x6, waiting for transfers between devices: 59.9 us -> 58 us  [hop(): lax.ppermute(after(held[step - 1, start], *token), 'field', ring)]
  transfers between devices with their start and end apart: 31 -> 31, of which waited for: 7 -> 10; matrix products, arithmetic and copies ran while one was open for 1% -> 1% of each run, Pallas kernels for 35% -> 36%
where the time goes in v3:
time: 179 us; the launch traced here: 178 us
  Pallas kernels  86.2 us (48%)
  waiting for transfers between devices  60.5 us (34%)
  starting transfers between devices  18.9 us (11%)
  local copies, waits for them, and re-layouts  11.8 us (7%)
    ppermute x6, waiting for transfers between devices, hop(): lax.ppermute(after(held[step - 1, start], *token), 'field', ring)  58 us
    pallas_call x10, Pallas kernels, bias_of(): pl.pallas_call(functools.partial(bias_kernel, len(parts)), out_shape=[jax...  36.2 us
    pallas_call x1, Pallas kernels, finish(): pl.pallas_call(functools.partial(finish_kernel, len(mine), len(unit), uni...  22.2 us
    pallas_call x1, Pallas kernels, begin(): pl.pallas_call(functools.partial(begin_kernel, len(mine), unit), out_shap...  14.2 us
    ppermute x5, starting transfers between devices, across_chips(): lax.ppermute(total, 'pair', [(i, i ^ reach) for i in range(pair_size)])  7.37 us
    pallas_call x1, Pallas kernels, split_green(): pl.pallas_call(split_green_kernel, out_shape=[pltpu.VMEM((channels, acros...  6.53 us
    unnamed x6, local copies, waits for them, and re-layouts  6.38 us
    ppermute x6, starting transfers between devices, hop(): lax.ppermute(after(held[step - 1, start], *token), 'field', ring)  6.34 us
  transfers between devices with their start and end apart: 31, of which 10 were waited for; matrix products, arithmetic and copies ran while one was open for 1% of the time, Pallas kernels for 36%

profile of v3, /device:TPU:0, one launch (start us, length us, event | category | flops | bytes accessed | tf_op | source)
XLA Modules:
  0.0 178.3 jit_solution(18160021398990866706)
XLA Ops:
  0.6 2.8 %fusion = (f32[96,2304]{1,0:T(8,128)}, f32[96,2304]{1,0:T(8,128)}) fusion(f32[192,2304]{1,0:T(8,128)} %refs_0_.2), kind=kLoop, calls=%fused_computation | loop fusion | bytes 3538944 | tf_op jit(solution)/shard_map/slice | solution.py:306
  3.4 3.0 %collective-permute-start.3 = (f32[96,2304]{1,0:T(8,128)}, f32[96,2304]{1,0:T(8,128)}, u32[]{:S(2)}, u32[]{:S(2)}) collective-permute-start(f32[96,2304]{1,0:T(8,128)} %get-tuple-element.119), channel_id=1, source_target_pairs={{0,4},{4,8},{8,12},{12,0},{1,5},{5,9},{9,13},{13,1},{2,6},{6,10},{... | collective-permute-start | bytes 2654216 | tf_op jit(solution)/shard_map/ppermute | solution.py:320
  6.4 1.6 collective-permute-start.4
  8.2 2.4 %copy.11 = f32[768,1024]{1,0:T(8,128)S(1)} copy(f32[768,1024]{0,1:T(8,128)} %bitcast.25) | data formatting | bytes 6291456 | tf_op jit(solution)/shard_map/transpose | solution.py:328
  10.7 6.4 %copy-done.1 = f32[2,1024,2304]{2,1,0:T(8,128)S(1)} copy-done((f32[2,1024,2304]{2,1,0:T(8,128)S(1)}, f32[2,1024,2304]{2,1,0:T(8,128)}, u32[]{:S(2)}) %copy-start.1) | copy-done | bytes 18874392
  17.1 6.5 %split_green.1 = (bf16[2,2,256,2304]{3,2,1,0:T(8,128)(2,1)S(1)}, bf16[2,2,256,2304]{3,2,1,0:T(8,128)(2,1)S(1)}, bf16[2,2,256,2304]{3,2,1,0:T(8,128)(2,1)S(1)}, bf16[2,2,256,2304]{3,2,1,0:T(8,128)(2,1)S(1)}) custom-call(s32[6]{0:T(128)S(1)} %stack.34.s_ref, f32[2,2,2,256,2304]{4,3,2,1,0:T(8,128)S(1)} %bitcast.19), custom_call_target="tpu_custom_call" | custom-call | flops 1 | bytes 1 | tf_op jit(solution)/shard_map/split_green/pallas_call | solution.py:48
  23.6 3.5 %bias.10 = (f32[2,192,256]{2,1,0:T(8,128)S(1)}, f32[2,192,256]{2,1,0:T(8,128)S(1)}) custom-call(bf16[2,2,256,2304]{3,2,1,0:T(8,128)(2,1)S(1)} %get-tuple-element.63.high_ref, bf16[2,2,256,2304]{3,2,1,0:T(8,128)(2,1)S(1)} %get-tuple-element.64.low_ref, f32[192,2304]{1,0:T(8,128)S(1)} %copy-done), custom_call_target="tpu_custom_call" | custom-call | flops 1 | bytes 1 | tf_op jit(solution)/shard_map/bias/pallas_call | solution.py:78
  27.7 3.5 %bias.11 = (f32[2,192,256]{2,1,0:T(8,128)S(1)}, f32[2,192,256]{2,1,0:T(8,128)S(1)}) custom-call(bf16[2,2,256,2304]{3,2,1,0:T(8,128)(2,1)S(1)} %get-tuple-element.61.high_ref, bf16[2,2,256,2304]{3,2,1,0:T(8,128)(2,1)S(1)} %get-tuple-element.62.low_ref, f32[192,2304]{1,0:T(8,128)S(1)} %copy-done), custom_call_target="tpu_custom_call" | custom-call | flops 1 | bytes 1 | tf_op jit(solution)/shard_map/bias/pallas_call | solution.py:78
  31.2 1.6 collective-permute-start.13
  33.0 15.2 %collective-permute-done.4.refs_1_.refs_2_ = f32[96,2304]{1,0:T(8,128)} collective-permute-done((f32[96,2304]{1,0:T(8,128)}, f32[96,2304]{1,0:T(8,128)}, u32[]{:S(2)}, u32[]{:S(2)}) %collective-permute-start.4) | collective-permute-done | bytes 884768 | tf_op jit(solution)/shard_map/ppermute | solution.py:320
  48.2 1.7 collective-permute-start.2
  49.9 5.0 %bias.12 = (f32[2,192,256]{2,1,0:T(8,128)S(1)}, f32[2,192,256]{2,1,0:T(8,128)S(1)}) custom-call(bf16[2,2,256,2304]{3,2,1,0:T(8,128)(2,1)S(1)} %get-tuple-element.63.high_ref, bf16[2,2,256,2304]{3,2,1,0:T(8,128)(2,1)S(1)} %get-tuple-element.64.low_ref, f32[96,2304]{1,0:T(8,128)} %collective-permute-done.3.refs_0_.refs_1_, ...), custom_call_target="tpu_custom_call" | custom-call | flops 1 | bytes 1 | tf_op jit(solution)/shard_map/bias/pallas_call | solution.py:78
  55.5 5.0 %bias.13 = (f32[2,192,256]{2,1,0:T(8,128)S(1)}, f32[2,192,256]{2,1,0:T(8,128)S(1)}) custom-call(bf16[2,2,256,2304]{3,2,1,0:T(8,128)(2,1)S(1)} %get-tuple-element.61.high_ref, bf16[2,2,256,2304]{3,2,1,0:T(8,128)(2,1)S(1)} %get-tuple-element.62.low_ref, f32[96,2304]{1,0:T(8,128)} %collective-permute-done.3.refs_0_.refs_1_, ...), custom_call_target="tpu_custom_call" | custom-call | flops 1 | bytes 1 | tf_op jit(solution)/shard_map/bias/pallas_call | solution.py:78
  60.5 6.6 %collective-permute-done.13.refs_0_ = f32[96,2304]{1,0:T(8,128)S(1)} collective-permute-done((f32[96,2304]{1,0:T(8,128)}, f32[96,2304]{1,0:T(8,128)S(1)}, u32[]{:S(2)}, u32[]{:S(2)}) %collective-permute-start.13) | collective-permute-done | bytes 884768 | tf_op jit(solution)/shard_map/ppermute | solution.py:320
  67.2 1.8 collective-permute-start.7
  69.7 16.3 %collective-permute-done.12.refs_1_ = f32[96,2304]{1,0:T(8,128)S(1)} collective-permute-done((f32[96,2304]{1,0:T(8,128)}, f32[96,2304]{1,0:T(8,128)S(1)}, u32[]{:S(2)}, u32[]{:S(2)}) %collective-permute-start.12) | collective-permute-done | bytes 884768 | tf_op jit(solution)/shard_map/ppermute | solution.py:320
  86.0 3.5 %bias.14 = (f32[2,192,256]{2,1,0:T(8,128)S(1)}, f32[2,192,256]{2,1,0:T(8,128)S(1)}) custom-call(bf16[2,2,256,2304]{3,2,1,0:T(8,128)(2,1)S(1)} %get-tuple-element.63.high_ref, bf16[2,2,256,2304]{3,2,1,0:T(8,128)(2,1)S(1)} %get-tuple-element.64.low_ref, f32[96,2304]{1,0:T(8,128)S(1)} %collective-permute-done.13.refs_0_, ...), custom_call_target="tpu_custom_call" | custom-call | flops 1 | bytes 1 | tf_op jit(solution)/shard_map/bias/pallas_call | solution.py:78
  90.1 3.5 %bias.15 = (f32[2,192,256]{2,1,0:T(8,128)S(1)}, f32[2,192,256]{2,1,0:T(8,128)S(1)}) custom-call(bf16[2,2,256,2304]{3,2,1,0:T(8,128)(2,1)S(1)} %get-tuple-element.61.high_ref, bf16[2,2,256,2304]{3,2,1,0:T(8,128)(2,1)S(1)} %get-tuple-element.62.low_ref, f32[96,2304]{1,0:T(8,128)S(1)} %collective-permute-done.13.refs_0_, ...), custom_call_target="tpu_custom_call" | custom-call | flops 1 | bytes 1 | tf_op jit(solution)/shard_map/bias/pallas_call | solution.py:78
  93.7 11.3 %collective-permute-done.15.refs_0_.refs_2_ = f32[96,2304]{1,0:T(8,128)S(1)} collective-permute-done((f32[96,2304]{1,0:T(8,128)S(1)}, f32[96,2304]{1,0:T(8,128)S(1)}, u32[]{:S(2)}, u32[]{:S(2)}) %collective-permute-start.15) | collective-permute-done | bytes 884768 | tf_op jit(solution)/shard_map/ppermute | solution.py:320
  105.0 3.1 %bias.16 = (f32[2,96,256]{2,1,0:T(8,128)S(1)}, f32[2,96,256]{2,1,0:T(8,128)S(1)}) custom-call(bf16[2,2,256,2304]{3,2,1,0:T(8,128)(2,1)S(1)} %get-tuple-element.63.high_ref, bf16[2,2,256,2304]{3,2,1,0:T(8,128)(2,1)S(1)} %get-tuple-element.64.low_ref, f32[96,2304]{1,0:T(8,128)S(1)} %collective-permute-done.15.refs_0_.refs_2_), custom_call_target="tpu_custom_call" | custom-call | flops 1 | bytes 1 | tf_op jit(solution)/shard_map/bias/pallas_call | solution.py:78
  108.8 1.8 %collective-permute-start.22 = (f32[2,2,192,256]{3,2,1,0:T(8,128)S(1)}, f32[2,2,192,256]{3,2,1,0:T(8,128)S(1)}, u32[]{:S(2)}, u32[]{:S(2)}) collective-permute-start(f32[2,2,192,256]{3,2,1,0:T(8,128)S(1)} %add.32.sums_ref), channel_id=1, source_target_pairs={{0,2},{1,3},{2,0},{3,1},{4,6},{5,7},{6,4},{7,5},{8,10},{9,11},{10,... | collective-permute-start | bytes 2359304 | tf_op jit(solution)/shard_map/ppermute | solution.py:356
  111.4 3.1 %bias.17 = (f32[2,96,256]{2,1,0:T(8,128)S(1)}, f32[2,96,256]{2,1,0:T(8,128)S(1)}) custom-call(bf16[2,2,256,2304]{3,2,1,0:T(8,128)(2,1)S(1)} %get-tuple-element.61.high_ref, bf16[2,2,256,2304]{3,2,1,0:T(8,128)(2,1)S(1)} %get-tuple-element.62.low_ref, f32[96,2304]{1,0:T(8,128)S(1)} %collective-permute-done.15.refs_0_.refs_2_), custom_call_target="tpu_custom_call" | custom-call | flops 1 | bytes 1 | tf_op jit(solution)/shard_map/bias/pallas_call | solution.py:78
  114.5 8.6 %collective-permute-done.14.refs_0_.refs_3_ = f32[96,2304]{1,0:T(8,128)S(1)} collective-permute-done((f32[96,2304]{1,0:T(8,128)S(1)}, f32[96,2304]{1,0:T(8,128)S(1)}, u32[]{:S(2)}, u32[]{:S(2)}) %collective-permute-start.14) | collective-permute-done | bytes 884768 | tf_op jit(solution)/shard_map/ppermute | solution.py:320
  123.1 3.1 %bias.18 = (f32[2,96,256]{2,1,0:T(8,128)S(1)}, f32[2,96,256]{2,1,0:T(8,128)S(1)}) custom-call(bf16[2,2,256,2304]{3,2,1,0:T(8,128)(2,1)S(1)} %get-tuple-element.63.high_ref, bf16[2,2,256,2304]{3,2,1,0:T(8,128)(2,1)S(1)} %get-tuple-element.64.low_ref, f32[96,2304]{1,0:T(8,128)S(1)} %collective-permute-done.14.refs_0_.refs_3_), custom_call_target="tpu_custom_call" | custom-call | flops 1 | bytes 1 | tf_op jit(solution)/shard_map/bias/pallas_call | solution.py:78
  128.5 1.5 collective-permute-start.23
  130.0 3.1 %bias.19 = (f32[2,96,256]{2,1,0:T(8,128)S(1)}, f32[2,96,256]{2,1,0:T(8,128)S(1)}) custom-call(bf16[2,2,256,2304]{3,2,1,0:T(8,128)(2,1)S(1)} %get-tuple-element.61.high_ref, bf16[2,2,256,2304]{3,2,1,0:T(8,128)(2,1)S(1)} %get-tuple-element.62.low_ref, f32[96,2304]{1,0:T(8,128)S(1)} %collective-permute-done.14.refs_0_.refs_3_), custom_call_target="tpu_custom_call" | custom-call | flops 1 | bytes 1 | tf_op jit(solution)/shard_map/bias/pallas_call | solution.py:78
  133.7 1.0 stack_cholesky.3.refs_16_
  134.7 2.1 %stack_cholesky.2.refs_11_ = bf16[1152,2304]{1,0:T(8,128)(2,1)S(1)} custom-call(f32[192,2304]{1,0:T(8,128)S(1)} %copy-done, f32[96,2304]{1,0:T(8,128)} %collective-permute-done.3.refs_0_.refs_1_, f32[96,2304]{1,0:T(8,128)} %collective-permute-done.4.refs_1_.refs_2_), custom_call_target="tpu_custom_call" | custom-call | flops 1 | bytes 1 | tf_op jit(solution)/shard_map/stack_cholesky/pallas_call | solution.py:182
  136.9 14.2 %begin.1.refs_17_ = f32[2,2,512,2304]{3,2,1,0:T(8,128)S(1)} custom-call(s32[6]{0:T(128)S(1)} %stack.34.s_ref, f32[2,192,256]{2,1,0:T(8,128)S(1)} %get-tuple-element.70.refs_0_, f32[2,192,256]{2,1,0:T(8,128)S(1)} %get-tuple-element.71.refs_1_, f32[2,192,256]{2,1,0:T(8,128)S(1)} %get-tuple-element.79.refs_2_, f32[2,192,256]{2,1,0:T(8,128)S(1)} %get-tuple-element.80.refs_3_, ...), custom_call_target="tpu_custom_call" | custom-call | flops 1 | bytes 1 | tf_op jit(solution)/shard_map/begin/pallas_call | solution.py:210
  151.1 0.8 cap.7
  155.0 0.9 collective-permute-done.29.refs_10_
  156.2 22.2 %finish.1 = (f32[2,2,256,2,2304]{4,3,2,1,0:T(2,128)}, f32[2,256,768]{2,1,0:T(8,128)}) custom-call(s32[6]{0:T(128)S(1)} %stack.34.s_ref, f32[2,192,256]{2,1,0:T(8,128)S(1)} %get-tuple-element.107.refs_0_, f32[2,192,256]{2,1,0:T(8,128)S(1)} %get-tuple-element.108.refs_1_, f32[2,96,256]{2,1,0:T(8,128)S(1)} %get-tuple-element.110.refs_2_, ...), custom_call_target="tpu_custom_call" | custom-call | flops 1 | bytes 1 | tf_op jit(solution)/shard_map/finish/pallas_call | solution.py:256
  (65 shorter events, 10.9 us)
Async XLA Ops:
  0.6 7.4 %copy-start.2 = (f32[2,768]{1,0:T(2,128)S(1)}, f32[2,768]{1,0:T(2,128)}, u32[]{:S(2)}) copy-start(f32[2,768]{1,0:T(2,128)} %param.6) | copy-start | bytes 18436
  3.4 27.8 %collective-permute-start.3 = (f32[96,2304]{1,0:T(8,128)}, f32[96,2304]{1,0:T(8,128)}, u32[]{:S(2)}, u32[]{:S(2)}) collective-permute-start(f32[96,2304]{1,0:T(8,128)} %get-tuple-element.119), channel_id=1, source_target_pairs={{0,4},{4,8},{8,12},{12,0},{1,5},{5,9},{9,13},{13,1},{2,6},{6,10},{... | collective-permute-start | bytes 2654216 | tf_op jit(solution)/shard_map/ppermute | solution.py:320
  6.4 41.8 %collective-permute-start.4 = (f32[96,2304]{1,0:T(8,128)}, f32[96,2304]{1,0:T(8,128)}, u32[]{:S(2)}, u32[]{:S(2)}) collective-permute-start(f32[96,2304]{1,0:T(8,128)} %get-tuple-element.118), channel_id=1, source_target_pairs={{0,4},{4,8},{8,12},{12,0},{1,5},{5,9},{9,13},{13,1},{2,6},{6,10},{... | collective-permute-start | bytes 2654216 | tf_op jit(solution)/shard_map/ppermute | solution.py:320
  27.1 5.7 %collective-permute-start = (f32[2,192,256]{2,1,0:T(8,128)S(1)}, f32[2,192,256]{2,1,0:T(8,128)S(1)}, u32[]{:S(2)}, u32[]{:S(2)}) collective-permute-start(f32[2,192,256]{2,1,0:T(8,128)S(1)} %get-tuple-element.65), channel_id=1, source_target_pairs={{0,1},{1,0},{2,3},{3,2},{4,5},{5,4},{6,7},{7,6},{8,9},{9,8},{10,11... | collective-permute-start | bytes 1179656 | tf_op jit(solution)/shard_map/ppermute | solution.py:343
  27.2 5.7 %collective-permute-start.1 = (f32[2,192,256]{2,1,0:T(8,128)S(1)}, f32[2,192,256]{2,1,0:T(8,128)S(1)}, u32[]{:S(2)}, u32[]{:S(2)}) collective-permute-start(f32[2,192,256]{2,1,0:T(8,128)S(1)} %get-tuple-element.66), channel_id=1, source_target_pairs={{0,1},{1,0},{2,3},{3,2},{4,5},{5,4},{6,7},{7,6},{8,9},{9,8},{10,11... | collective-permute-start | bytes 1179656 | tf_op jit(solution)/shard_map/ppermute | solution.py:343
  31.2 35.8 %collective-permute-start.13 = (f32[96,2304]{1,0:T(8,128)}, f32[96,2304]{1,0:T(8,128)S(1)}, u32[]{:S(2)}, u32[]{:S(2)}) collective-permute-start(f32[96,2304]{1,0:T(8,128)} %collective-permute-done.3.refs_0_.refs_1_), channel_id=1, source_target_pairs={{0,4},{4,8},{8,12},{12,0},{1,5},{5,9},{9,13},{13,1},{2,6},{6,10},{... | collective-permute-start | bytes 2654216 | tf_op jit(solution)/shard_map/ppermute | solution.py:320
  48.2 37.8 %collective-permute-start.12 = (f32[96,2304]{1,0:T(8,128)}, f32[96,2304]{1,0:T(8,128)S(1)}, u32[]{:S(2)}, u32[]{:S(2)}) collective-permute-start(f32[96,2304]{1,0:T(8,128)} %collective-permute-done.4.refs_1_.refs_2_), channel_id=1, source_target_pairs={{0,4},{4,8},{8,12},{12,0},{1,5},{5,9},{9,13},{13,1},{2,6},{6,10},{... | collective-permute-start | bytes 2654216 | tf_op jit(solution)/shard_map/ppermute | solution.py:320
  48.2 20.7 %collective-permute-start.2 = (f32[2,2,192,256]{3,2,1,0:T(8,128)S(1)}, f32[2,2,192,256]{3,2,1,0:T(8,128)S(1)}, u32[]{:S(2)}, u32[]{:S(2)}) collective-permute-start(f32[2,2,192,256]{3,2,1,0:T(8,128)S(1)} %add.30.sums_ref), channel_id=1, source_target_pairs={{0,2},{1,3},{2,0},{3,1},{4,6},{5,7},{6,4},{7,5},{8,10},{9,11},{10,... | collective-permute-start | bytes 2359304 | tf_op jit(solution)/shard_map/ppermute | solution.py:356
  54.9 12.2 %collective-permute-start.5 = (f32[2,192,256]{2,1,0:T(8,128)S(1)}, f32[2,192,256]{2,1,0:T(8,128)S(1)}, u32[]{:S(2)}, u32[]{:S(2)}) collective-permute-start(f32[2,192,256]{2,1,0:T(8,128)S(1)} %get-tuple-element.73), channel_id=1, source_target_pairs={{0,1},{1,0},{2,3},{3,2},{4,5},{5,4},{6,7},{7,6},{8,9},{9,8},{10,11... | collective-permute-start | bytes 1179656 | tf_op jit(solution)/shard_map/ppermute | solution.py:343
  55.0 12.1 %collective-permute-start.6 = (f32[2,192,256]{2,1,0:T(8,128)S(1)}, f32[2,192,256]{2,1,0:T(8,128)S(1)}, u32[]{:S(2)}, u32[]{:S(2)}) collective-permute-start(f32[2,192,256]{2,1,0:T(8,128)S(1)} %get-tuple-element.74), channel_id=1, source_target_pairs={{0,1},{1,0},{2,3},{3,2},{4,5},{5,4},{6,7},{7,6},{8,9},{9,8},{10,11... | collective-permute-start | bytes 1179656 | tf_op jit(solution)/shard_map/ppermute | solution.py:343
  67.0 37.9 %collective-permute-start.15 = (f32[96,2304]{1,0:T(8,128)S(1)}, f32[96,2304]{1,0:T(8,128)S(1)}, u32[]{:S(2)}, u32[]{:S(2)}) collective-permute-start(f32[96,2304]{1,0:T(8,128)S(1)} %collective-permute-done.13.refs_0_), channel_id=1, source_target_pairs={{0,4},{4,8},{8,12},{12,0},{1,5},{5,9},{9,13},{13,1},{2,6},{6,10},{... | collective-permute-start | bytes 2654216 | tf_op jit(solution)/shard_map/ppermute | solution.py:320
  67.2 41.6 %collective-permute-start.7 = (f32[2,2,192,256]{3,2,1,0:T(8,128)S(1)}, f32[2,2,192,256]{3,2,1,0:T(8,128)S(1)}, u32[]{:S(2)}, u32[]{:S(2)}) collective-permute-start(f32[2,2,192,256]{3,2,1,0:T(8,128)S(1)} %add.31.sums_ref), channel_id=1, source_target_pairs={{0,2},{1,3},{2,0},{3,1},{4,6},{5,7},{6,4},{7,5},{8,10},{9,11},{10,... | collective-permute-start | bytes 2359304 | tf_op jit(solution)/shard_map/ppermute | solution.py:356
  86.0 37.1 %collective-permute-start.14 = (f32[96,2304]{1,0:T(8,128)S(1)}, f32[96,2304]{1,0:T(8,128)S(1)}, u32[]{:S(2)}, u32[]{:S(2)}) collective-permute-start(f32[96,2304]{1,0:T(8,128)S(1)} %collective-permute-done.12.refs_1_), channel_id=1, source_target_pairs={{0,4},{4,8},{8,12},{12,0},{1,5},{5,9},{9,13},{13,1},{2,6},{6,10},{... | collective-permute-start | bytes 2654216 | tf_op jit(solution)/shard_map/ppermute | solution.py:320
  89.6 18.6 %collective-permute-start.16 = (f32[2,192,256]{2,1,0:T(8,128)S(1)}, f32[2,192,256]{2,1,0:T(8,128)S(1)}, u32[]{:S(2)}, u32[]{:S(2)}) collective-permute-start(f32[2,192,256]{2,1,0:T(8,128)S(1)} %get-tuple-element.86), channel_id=1, source_target_pairs={{0,1},{1,0},{2,3},{3,2},{4,5},{5,4},{6,7},{7,6},{8,9},{9,8},{10,11... | collective-permute-start | bytes 1179656 | tf_op jit(solution)/shard_map/ppermute | solution.py:343
  89.6 19.0 %collective-permute-start.17 = (f32[2,192,256]{2,1,0:T(8,128)S(1)}, f32[2,192,256]{2,1,0:T(8,128)S(1)}, u32[]{:S(2)}, u32[]{:S(2)}) collective-permute-start(f32[2,192,256]{2,1,0:T(8,128)S(1)} %get-tuple-element.87), channel_id=1, source_target_pairs={{0,1},{1,0},{2,3},{3,2},{4,5},{5,4},{6,7},{7,6},{8,9},{9,8},{10,11... | collective-permute-start | bytes 1179656 | tf_op jit(solution)/shard_map/ppermute | solution.py:343
  108.0 6.4 %collective-permute-start.18 = (f32[2,96,256]{2,1,0:T(8,128)S(1)}, f32[2,96,256]{2,1,0:T(8,128)S(1)}, u32[]{:S(2)}, u32[]{:S(2)}) collective-permute-start(f32[2,96,256]{2,1,0:T(8,128)S(1)} %get-tuple-element.92), channel_id=1, source_target_pairs={{0,1},{1,0},{2,3},{3,2},{4,5},{5,4},{6,7},{7,6},{8,9},{9,8},{10,11... | collective-permute-start | bytes 589832 | tf_op jit(solution)/shard_map/ppermute | solution.py:343
  108.1 6.3 %collective-permute-start.19 = (f32[2,96,256]{2,1,0:T(8,128)S(1)}, f32[2,96,256]{2,1,0:T(8,128)S(1)}, u32[]{:S(2)}, u32[]{:S(2)}) collective-permute-start(f32[2,96,256]{2,1,0:T(8,128)S(1)} %get-tuple-element.93), channel_id=1, source_target_pairs={{0,1},{1,0},{2,3},{3,2},{4,5},{5,4},{6,7},{7,6},{8,9},{9,8},{10,11... | collective-permute-start | bytes 589832 | tf_op jit(solution)/shard_map/ppermute | solution.py:343
  108.6 18.2 %collective-permute-start.9 = (f32[2,192,256]{2,1,0:T(8,128)S(1)}, f32[2,192,256]{2,1,0:T(8,128)S(1)}, u32[]{:S(2)}, u32[]{:S(2)}) collective-permute-start(f32[2,192,256]{2,1,0:T(8,128)S(1)} %get-tuple-element.71.refs_1_), channel_id=1, source_target_pairs={{0,1},{1,0},{2,3},{3,2},{4,5},{5,4},{6,7},{7,6},{8,9},{9,8},{10,11... | collective-permute-start | bytes 1179656 | tf_op jit(solution)/shard_map/ppermute | solution.py:363
  108.8 42.3 %collective-permute-start.22 = (f32[2,2,192,256]{3,2,1,0:T(8,128)S(1)}, f32[2,2,192,256]{3,2,1,0:T(8,128)S(1)}, u32[]{:S(2)}, u32[]{:S(2)}) collective-permute-start(f32[2,2,192,256]{3,2,1,0:T(8,128)S(1)} %add.32.sums_ref), channel_id=1, source_target_pairs={{0,2},{1,3},{2,0},{3,1},{4,6},{5,7},{6,4},{7,5},{8,10},{9,11},{10,... | collective-permute-start | bytes 2359304 | tf_op jit(solution)/shard_map/ppermute | solution.py:356
  126.2 1.5 collective-permute-start.20
  126.2 6.9 %collective-permute-start.8 = (f32[2,192,256]{2,1,0:T(8,128)S(1)}, f32[2,192,256]{2,1,0:T(8,128)S(1)}, u32[]{:S(2)}, u32[]{:S(2)}) collective-permute-start(f32[2,192,256]{2,1,0:T(8,128)S(1)} %get-tuple-element.70.refs_0_), channel_id=1, source_target_pairs={{0,1},{1,0},{2,3},{3,2},{4,5},{5,4},{6,7},{7,6},{8,9},{9,8},{10,11... | collective-permute-start | bytes 1179656 | tf_op jit(solution)/shard_map/ppermute | solution.py:363
  126.7 1.8 collective-permute-start.21
  126.8 10.0 %collective-permute-start.11 = (f32[2,192,256]{2,1,0:T(8,128)S(1)}, f32[2,192,256]{2,1,0:T(8,128)S(1)}, u32[]{:S(2)}, u32[]{:S(2)}) collective-permute-start(f32[2,192,256]{2,1,0:T(8,128)S(1)} %get-tuple-element.80.refs_3_), channel_id=1, source_target_pairs={{0,1},{1,0},{2,3},{3,2},{4,5},{5,4},{6,7},{7,6},{8,9},{9,8},{10,11... | collective-permute-start | bytes 1179656 | tf_op jit(solution)/shard_map/ppermute | solution.py:363
  127.7 9.2 %collective-permute-start.10 = (f32[2,192,256]{2,1,0:T(8,128)S(1)}, f32[2,192,256]{2,1,0:T(8,128)S(1)}, u32[]{:S(2)}, u32[]{:S(2)}) collective-permute-start(f32[2,192,256]{2,1,0:T(8,128)S(1)} %get-tuple-element.79.refs_2_), channel_id=1, source_target_pairs={{0,1},{1,0},{2,3},{3,2},{4,5},{5,4},{6,7},{7,6},{8,9},{9,8},{10,11... | collective-permute-start | bytes 1179656 | tf_op jit(solution)/shard_map/ppermute | solution.py:363
  128.5 23.9 %collective-permute-start.23 = (f32[2,2,96,256]{3,2,1,0:T(8,128)S(1)}, f32[2,2,96,256]{3,2,1,0:T(8,128)S(1)}, u32[]{:S(2)}, u32[]{:S(2)}) collective-permute-start(f32[2,2,96,256]{3,2,1,0:T(8,128)S(1)} %add.33.sums_ref), channel_id=1, source_target_pairs={{0,2},{1,3},{2,0},{3,1},{4,6},{5,7},{6,4},{7,5},{8,10},{9,11},{10,... | collective-permute-start | bytes 1179656 | tf_op jit(solution)/shard_map/ppermute | solution.py:356
  133.1 20.5 %collective-permute-start.24 = (f32[2,2,96,256]{3,2,1,0:T(8,128)S(1)}, f32[2,2,96,256]{3,2,1,0:T(8,128)S(1)}, u32[]{:S(2)}, u32[]{:S(2)}) collective-permute-start(f32[2,2,96,256]{3,2,1,0:T(8,128)S(1)} %add.34.sums_ref), channel_id=1, source_target_pairs={{0,2},{1,3},{2,0},{3,1},{4,6},{5,7},{6,4},{7,5},{8,10},{9,11},{10,... | collective-permute-start | bytes 1179656 | tf_op jit(solution)/shard_map/ppermute | solution.py:356
  151.8 3.1 %collective-permute-start.25 = (f32[2,192,256]{2,1,0:T(8,128)S(1)}, f32[2,192,256]{2,1,0:T(8,128)S(1)}, u32[]{:S(2)}, u32[]{:S(2)}) collective-permute-start(f32[2,192,256]{2,1,0:T(8,128)S(1)} %get-tuple-element.107.refs_0_), channel_id=1, source_target_pairs={{0,1},{1,0},{2,3},{3,2},{4,5},{5,4},{6,7},{7,6},{8,9},{9,8},{10,11... | collective-permute-start | bytes 1179656 | tf_op jit(solution)/shard_map/ppermute | solution.py:363
  151.9 3.0 %collective-permute-start.26 = (f32[2,192,256]{2,1,0:T(8,128)S(1)}, f32[2,192,256]{2,1,0:T(8,128)S(1)}, u32[]{:S(2)}, u32[]{:S(2)}) collective-permute-start(f32[2,192,256]{2,1,0:T(8,128)S(1)} %get-tuple-element.108.refs_1_), channel_id=1, source_target_pairs={{0,1},{1,0},{2,3},{3,2},{4,5},{5,4},{6,7},{7,6},{8,9},{9,8},{10,11... | collective-permute-start | bytes 1179656 | tf_op jit(solution)/shard_map/ppermute | solution.py:363
  153.1 1.5 collective-permute-start.27
  153.2 1.7 collective-permute-start.28
  154.4 1.5 collective-permute-start.29
  154.6 1.5 collective-permute-start.30
  (2 other events, 12.9 us)

commit v4 on v3

--- a/solution.py
+++ b/solution.py
@@ -303,7 +303,10 @@
     count = 2 if shard % 32 == 0 and ring_size > 2 else 1
     cuts = [(i * (shard // count), shard // count) for i in range(count)]
     pieces = [(step, start, n, shard) for step in range(1, ring_size) for start, n in cuts]
-    held = {(0, start): lax.slice_in_dim(cholesky_tensor, start, start + n, axis=0) for start, n in cuts}
+    held, cut = {}, cholesky_tensor
+    for start, n in cuts:
+        held[0, start] = lax.slice_in_dim(cut, start, start + n, axis=0)
+        cut = lax.optimization_barrier((cut, held[0, start]))[0]
 
     own_piece = (0, 0, shard, shard)
     if count > 1:

time: 179 us -> 178 us (level)
  waiting for transfers between devices: 60.5 us -> 58.1 us
  local copies, waits for them, and re-layouts: 11.8 us -> 14 us
    ppermute x6, waiting for transfers between devices: 58 us -> 55.6 us  [hop(): lax.ppermute(after(held[step - 1, start], *token), 'field', ring)]
    slice x1 -> x2, local copies, waits for them, and re-layouts: 2.75 us -> 4.27 us  [per_device(): held[0, start] = lax.slice_in_dim(cut, start, start + n, axis=0)]
    unnamed x6 -> x4, local copies, waits for them, and re-layouts: 6.38 us -> 6.37 us
  transfers between devices with their start and end apart: 31 -> 31, of which waited for: 10 -> 10; matrix products, arithmetic and copies ran while one was open for 1% -> 3% of each run, Pallas kernels for 36% -> 36%
where the time goes in v4:
time: 178 us; the launch traced here: 177 us
  Pallas kernels  85.3 us (48%)
  waiting for transfers between devices  58.1 us (33%)
  starting transfers between devices  18.9 us (11%)
  local copies, waits for them, and re-layouts  14 us (8%)
    ppermute x6, waiting for transfers between devices, hop(): lax.ppermute(after(held[step - 1, start], *token), 'field', ring)  55.6 us
    pallas_call x10, Pallas kernels, bias_of(): pl.pallas_call(functools.partial(bias_kernel, len(parts)), out_shape=[jax...  36.1 us
    pallas_call x1, Pallas kernels, finish(): pl.pallas_call(functools.partial(finish_kernel, len(mine), len(unit), uni...  22 us
    pallas_call x1, Pallas kernels, begin(): pl.pallas_call(functools.partial(begin_kernel, len(mine), unit), out_shap...  14.1 us
    ppermute x5, starting transfers between devices, across_chips(): lax.ppermute(total, 'pair', [(i, i ^ reach) for i in range(pair_size)])  7.38 us
    unnamed x4, local copies, waits for them, and re-layouts  6.37 us
    ppermute x6, starting transfers between devices, hop(): lax.ppermute(after(held[step - 1, start], *token), 'field', ring)  6.34 us
    pallas_call x1, Pallas kernels, split_green(): pl.pallas_call(split_green_kernel, out_shape=[pltpu.VMEM((channels, acros...  6.2 us
  transfers between devices with their start and end apart: 31, of which 10 were waited for; matrix products, arithmetic and copies ran while one was open for 3% of the time, Pallas kernels for 36%

profile of v4, /device:TPU:0, one launch (start us, length us, event | category | flops | bytes accessed | tf_op | source)
XLA Modules:
  0.0 177.2 jit_solution(12467829699903176268)
XLA Ops:
  0.6 2.1 %slice.6 = f32[96,2304]{1,0:T(8,128)} slice(f32[192,2304]{1,0:T(8,128)} %refs_0_.2), slice={[0:96], [0:2304]} | slice | bytes 1769472 | tf_op jit(solution)/shard_map/slice | solution.py:308
  2.8 3.0 %collective-permute-start.3 = (f32[96,2304]{1,0:T(8,128)}, f32[96,2304]{1,0:T(8,128)}, u32[]{:S(2)}, u32[]{:S(2)}) collective-permute-start(f32[96,2304]{1,0:T(8,128)} %slice.6), channel_id=1, source_target_pairs={{0,4},{4,8},{8,12},{12,0},{1,5},{5,9},{9,13},{13,1},{2,6},{6,10},{... | collective-permute-start | bytes 2654216 | tf_op jit(solution)/shard_map/ppermute | solution.py:323
  5.8 2.1 %slice.7 = f32[96,2304]{1,0:T(8,128)} slice(f32[192,2304]{1,0:T(8,128)} %refs_0_.2), slice={[96:192], [0:2304]} | slice | bytes 1769472 | tf_op jit(solution)/shard_map/slice | solution.py:308
  7.9 1.6 collective-permute-start.4
  10.4 2.4 %copy.11 = f32[768,1024]{1,0:T(8,128)S(1)} copy(f32[768,1024]{0,1:T(8,128)} %bitcast.25) | data formatting | bytes 6291456 | tf_op jit(solution)/shard_map/transpose | solution.py:331
  12.9 6.4 %copy-done.1 = f32[2,1024,2304]{2,1,0:T(8,128)S(1)} copy-done((f32[2,1024,2304]{2,1,0:T(8,128)S(1)}, f32[2,1024,2304]{2,1,0:T(8,128)}, u32[]{:S(2)}) %copy-start.1) | copy-done | bytes 18874392
  19.3 6.2 %split_green.1 = (bf16[2,2,256,2304]{3,2,1,0:T(8,128)(2,1)S(1)}, bf16[2,2,256,2304]{3,2,1,0:T(8,128)(2,1)S(1)}, bf16[2,2,256,2304]{3,2,1,0:T(8,128)(2,1)S(1)}, bf16[2,2,256,2304]{3,2,1,0:T(8,128)(2,1)S(1)}) custom-call(s32[6]{0:T(128)S(1)} %stack.34.s_ref, f32[2,2,2,256,2304]{4,3,2,1,0:T(8,128)S(1)} %bitcast.19), custom_call_target="tpu_custom_call" | custom-call | flops 1 | bytes 1 | tf_op jit(solution)/shard_map/split_green/pallas_call | solution.py:48
  25.5 3.5 %bias.10 = (f32[2,192,256]{2,1,0:T(8,128)S(1)}, f32[2,192,256]{2,1,0:T(8,128)S(1)}) custom-call(bf16[2,2,256,2304]{3,2,1,0:T(8,128)(2,1)S(1)} %get-tuple-element.65.high_ref, bf16[2,2,256,2304]{3,2,1,0:T(8,128)(2,1)S(1)} %get-tuple-element.66.low_ref, f32[192,2304]{1,0:T(8,128)S(1)} %copy-done), custom_call_target="tpu_custom_call" | custom-call | flops 1 | bytes 1 | tf_op jit(solution)/shard_map/bias/pallas_call | solution.py:78
  29.6 3.5 %bias.11 = (f32[2,192,256]{2,1,0:T(8,128)S(1)}, f32[2,192,256]{2,1,0:T(8,128)S(1)}) custom-call(bf16[2,2,256,2304]{3,2,1,0:T(8,128)(2,1)S(1)} %get-tuple-element.63.high_ref, bf16[2,2,256,2304]{3,2,1,0:T(8,128)(2,1)S(1)} %get-tuple-element.64.low_ref, f32[192,2304]{1,0:T(8,128)S(1)} %copy-done), custom_call_target="tpu_custom_call" | custom-call | flops 1 | bytes 1 | tf_op jit(solution)/shard_map/bias/pallas_call | solution.py:78
  33.1 1.6 collective-permute-start.13
  34.8 12.7 %collective-permute-done.4.refs_1_.refs_2_ = f32[96,2304]{1,0:T(8,128)} collective-permute-done((f32[96,2304]{1,0:T(8,128)}, f32[96,2304]{1,0:T(8,128)}, u32[]{:S(2)}, u32[]{:S(2)}) %collective-permute-start.4) | collective-permute-done | bytes 884768 | tf_op jit(solution)/shard_map/ppermute | solution.py:323
  47.6 1.7 collective-permute-start.2
  49.3 4.9 %bias.12 = (f32[2,192,256]{2,1,0:T(8,128)S(1)}, f32[2,192,256]{2,1,0:T(8,128)S(1)}) custom-call(bf16[2,2,256,2304]{3,2,1,0:T(8,128)(2,1)S(1)} %get-tuple-element.65.high_ref, bf16[2,2,256,2304]{3,2,1,0:T(8,128)(2,1)S(1)} %get-tuple-element.66.low_ref, f32[96,2304]{1,0:T(8,128)} %collective-permute-done.3.refs_0_.refs_1_, ...), custom_call_target="tpu_custom_call" | custom-call | flops 1 | bytes 1 | tf_op jit(solution)/shard_map/bias/pallas_call | solution.py:78
  54.8 4.9 %bias.13 = (f32[2,192,256]{2,1,0:T(8,128)S(1)}, f32[2,192,256]{2,1,0:T(8,128)S(1)}) custom-call(bf16[2,2,256,2304]{3,2,1,0:T(8,128)(2,1)S(1)} %get-tuple-element.63.high_ref, bf16[2,2,256,2304]{3,2,1,0:T(8,128)(2,1)S(1)} %get-tuple-element.64.low_ref, f32[96,2304]{1,0:T(8,128)} %collective-permute-done.3.refs_0_.refs_1_, ...), custom_call_target="tpu_custom_call" | custom-call | flops 1 | bytes 1 | tf_op jit(solution)/shard_map/bias/pallas_call | solution.py:78
  59.8 6.6 %collective-permute-done.13.refs_0_ = f32[96,2304]{1,0:T(8,128)S(1)} collective-permute-done((f32[96,2304]{1,0:T(8,128)}, f32[96,2304]{1,0:T(8,128)S(1)}, u32[]{:S(2)}, u32[]{:S(2)}) %collective-permute-start.13) | collective-permute-done | bytes 884768 | tf_op jit(solution)/shard_map/ppermute | solution.py:323
  66.5 1.8 %collective-permute-start.7 = (f32[2,2,192,256]{3,2,1,0:T(8,128)S(1)}, f32[2,2,192,256]{3,2,1,0:T(8,128)S(1)}, u32[]{:S(2)}, u32[]{:S(2)}) collective-permute-start(f32[2,2,192,256]{3,2,1,0:T(8,128)S(1)} %add.31.sums_ref), channel_id=1, source_target_pairs={{0,2},{1,3},{2,0},{3,1},{4,6},{5,7},{6,4},{7,5},{8,10},{9,11},{10,... | collective-permute-start | bytes 2359304 | tf_op jit(solution)/shard_map/ppermute | solution.py:359
  69.1 16.3 %collective-permute-done.12.refs_1_ = f32[96,2304]{1,0:T(8,128)S(1)} collective-permute-done((f32[96,2304]{1,0:T(8,128)}, f32[96,2304]{1,0:T(8,128)S(1)}, u32[]{:S(2)}, u32[]{:S(2)}) %collective-permute-start.12) | collective-permute-done | bytes 884768 | tf_op jit(solution)/shard_map/ppermute | solution.py:323
  85.4 3.5 %bias.14 = (f32[2,192,256]{2,1,0:T(8,128)S(1)}, f32[2,192,256]{2,1,0:T(8,128)S(1)}) custom-call(bf16[2,2,256,2304]{3,2,1,0:T(8,128)(2,1)S(1)} %get-tuple-element.65.high_ref, bf16[2,2,256,2304]{3,2,1,0:T(8,128)(2,1)S(1)} %get-tuple-element.66.low_ref, f32[96,2304]{1,0:T(8,128)S(1)} %collective-permute-done.13.refs_0_, ...), custom_call_target="tpu_custom_call" | custom-call | flops 1 | bytes 1 | tf_op jit(solution)/shard_map/bias/pallas_call | solution.py:78
  89.5 3.5 %bias.15 = (f32[2,192,256]{2,1,0:T(8,128)S(1)}, f32[2,192,256]{2,1,0:T(8,128)S(1)}) custom-call(bf16[2,2,256,2304]{3,2,1,0:T(8,128)(2,1)S(1)} %get-tuple-element.63.high_ref, bf16[2,2,256,2304]{3,2,1,0:T(8,128)(2,1)S(1)} %get-tuple-element.64.low_ref, f32[96,2304]{1,0:T(8,128)S(1)} %collective-permute-done.13.refs_0_, ...), custom_call_target="tpu_custom_call" | custom-call | flops 1 | bytes 1 | tf_op jit(solution)/shard_map/bias/pallas_call | solution.py:78
  93.0 11.3 %collective-permute-done.15.refs_0_.refs_2_ = f32[96,2304]{1,0:T(8,128)S(1)} collective-permute-done((f32[96,2304]{1,0:T(8,128)S(1)}, f32[96,2304]{1,0:T(8,128)S(1)}, u32[]{:S(2)}, u32[]{:S(2)}) %collective-permute-start.15) | collective-permute-done | bytes 884768 | tf_op jit(solution)/shard_map/ppermute | solution.py:323
  104.3 3.1 %bias.16 = (f32[2,96,256]{2,1,0:T(8,128)S(1)}, f32[2,96,256]{2,1,0:T(8,128)S(1)}) custom-call(bf16[2,2,256,2304]{3,2,1,0:T(8,128)(2,1)S(1)} %get-tuple-element.65.high_ref, bf16[2,2,256,2304]{3,2,1,0:T(8,128)(2,1)S(1)} %get-tuple-element.66.low_ref, f32[96,2304]{1,0:T(8,128)S(1)} %collective-permute-done.15.refs_0_.refs_2_), custom_call_target="tpu_custom_call" | custom-call | flops 1 | bytes 1 | tf_op jit(solution)/shard_map/bias/pallas_call | solution.py:78
  108.2 1.8 %collective-permute-start.22 = (f32[2,2,192,256]{3,2,1,0:T(8,128)S(1)}, f32[2,2,192,256]{3,2,1,0:T(8,128)S(1)}, u32[]{:S(2)}, u32[]{:S(2)}) collective-permute-start(f32[2,2,192,256]{3,2,1,0:T(8,128)S(1)} %add.32.sums_ref), channel_id=1, source_target_pairs={{0,2},{1,3},{2,0},{3,1},{4,6},{5,7},{6,4},{7,5},{8,10},{9,11},{10,... | collective-permute-start | bytes 2359304 | tf_op jit(solution)/shard_map/ppermute | solution.py:359
  110.7 3.1 %bias.17 = (f32[2,96,256]{2,1,0:T(8,128)S(1)}, f32[2,96,256]{2,1,0:T(8,128)S(1)}) custom-call(bf16[2,2,256,2304]{3,2,1,0:T(8,128)(2,1)S(1)} %get-tuple-element.63.high_ref, bf16[2,2,256,2304]{3,2,1,0:T(8,128)(2,1)S(1)} %get-tuple-element.64.low_ref, f32[96,2304]{1,0:T(8,128)S(1)} %collective-permute-done.15.refs_0_.refs_2_), custom_call_target="tpu_custom_call" | custom-call | flops 1 | bytes 1 | tf_op jit(solution)/shard_map/bias/pallas_call | solution.py:78
  113.9 8.6 %collective-permute-done.14.refs_0_.refs_3_ = f32[96,2304]{1,0:T(8,128)S(1)} collective-permute-done((f32[96,2304]{1,0:T(8,128)S(1)}, f32[96,2304]{1,0:T(8,128)S(1)}, u32[]{:S(2)}, u32[]{:S(2)}) %collective-permute-start.14) | collective-permute-done | bytes 884768 | tf_op jit(solution)/shard_map/ppermute | solution.py:323
  122.5 3.1 %bias.18 = (f32[2,96,256]{2,1,0:T(8,128)S(1)}, f32[2,96,256]{2,1,0:T(8,128)S(1)}) custom-call(bf16[2,2,256,2304]{3,2,1,0:T(8,128)(2,1)S(1)} %get-tuple-element.65.high_ref, bf16[2,2,256,2304]{3,2,1,0:T(8,128)(2,1)S(1)} %get-tuple-element.66.low_ref, f32[96,2304]{1,0:T(8,128)S(1)} %collective-permute-done.14.refs_0_.refs_3_), custom_call_target="tpu_custom_call" | custom-call | flops 1 | bytes 1 | tf_op jit(solution)/shard_map/bias/pallas_call | solution.py:78
  127.9 1.5 collective-permute-start.23
  129.4 3.1 %bias.19 = (f32[2,96,256]{2,1,0:T(8,128)S(1)}, f32[2,96,256]{2,1,0:T(8,128)S(1)}) custom-call(bf16[2,2,256,2304]{3,2,1,0:T(8,128)(2,1)S(1)} %get-tuple-element.63.high_ref, bf16[2,2,256,2304]{3,2,1,0:T(8,128)(2,1)S(1)} %get-tuple-element.64.low_ref, f32[96,2304]{1,0:T(8,128)S(1)} %collective-permute-done.14.refs_0_.refs_3_), custom_call_target="tpu_custom_call" | custom-call | flops 1 | bytes 1 | tf_op jit(solution)/shard_map/bias/pallas_call | solution.py:78
  133.1 0.9 stack_cholesky.3.refs_16_
  134.0 2.1 %stack_cholesky.2.refs_11_ = bf16[1152,2304]{1,0:T(8,128)(2,1)S(1)} custom-call(f32[192,2304]{1,0:T(8,128)S(1)} %copy-done, f32[96,2304]{1,0:T(8,128)} %collective-permute-done.3.refs_0_.refs_1_, f32[96,2304]{1,0:T(8,128)} %collective-permute-done.4.refs_1_.refs_2_), custom_call_target="tpu_custom_call" | custom-call | flops 1 | bytes 1 | tf_op jit(solution)/shard_map/stack_cholesky/pallas_call | solution.py:182
  136.1 14.1 %begin.1.refs_17_ = f32[2,2,512,2304]{3,2,1,0:T(8,128)S(1)} custom-call(s32[6]{0:T(128)S(1)} %stack.34.s_ref, f32[2,192,256]{2,1,0:T(8,128)S(1)} %get-tuple-element.72.refs_0_, f32[2,192,256]{2,1,0:T(8,128)S(1)} %get-tuple-element.73.refs_1_, f32[2,192,256]{2,1,0:T(8,128)S(1)} %get-tuple-element.81.refs_2_, f32[2,192,256]{2,1,0:T(8,128)S(1)} %get-tuple-element.82.refs_3_, ...), custom_call_target="tpu_custom_call" | custom-call | flops 1 | bytes 1 | tf_op jit(solution)/shard_map/begin/pallas_call | solution.py:210
  154.1 0.9 collective-permute-done.29.refs_10_
  155.3 22.0 %finish.1 = (f32[2,2,256,2,2304]{4,3,2,1,0:T(2,128)}, f32[2,256,768]{2,1,0:T(8,128)}) custom-call(s32[6]{0:T(128)S(1)} %stack.34.s_ref, f32[2,192,256]{2,1,0:T(8,128)S(1)} %get-tuple-element.109.refs_0_, f32[2,192,256]{2,1,0:T(8,128)S(1)} %get-tuple-element.110.refs_1_, f32[2,96,256]{2,1,0:T(8,128)S(1)} %get-tuple-element.112.refs_2_, ...), custom_call_target="tpu_custom_call" | custom-call | flops 1 | bytes 1 | tf_op jit(solution)/shard_map/finish/pallas_call | solution.py:256
  (64 shorter events, 12.4 us)
Async XLA Ops:
  2.8 30.3 %collective-permute-start.3 = (f32[96,2304]{1,0:T(8,128)}, f32[96,2304]{1,0:T(8,128)}, u32[]{:S(2)}, u32[]{:S(2)}) collective-permute-start(f32[96,2304]{1,0:T(8,128)} %slice.6), channel_id=1, source_target_pairs={{0,4},{4,8},{8,12},{12,0},{1,5},{5,9},{9,13},{13,1},{2,6},{6,10},{... | collective-permute-start | bytes 2654216 | tf_op jit(solution)/shard_map/ppermute | solution.py:323
  7.9 39.6 %collective-permute-start.4 = (f32[96,2304]{1,0:T(8,128)}, f32[96,2304]{1,0:T(8,128)}, u32[]{:S(2)}, u32[]{:S(2)}) collective-permute-start(f32[96,2304]{1,0:T(8,128)} %slice.7), channel_id=1, source_target_pairs={{0,4},{4,8},{8,12},{12,0},{1,5},{5,9},{9,13},{13,1},{2,6},{6,10},{... | collective-permute-start | bytes 2654216 | tf_op jit(solution)/shard_map/ppermute | solution.py:323
  12.9 6.4 %copy-start.1 = (f32[2,1024,2304]{2,1,0:T(8,128)S(1)}, f32[2,1024,2304]{2,1,0:T(8,128)}, u32[]{:S(2)}) copy-start(f32[2,1024,2304]{2,1,0:T(8,128)} %param.5) | copy-start | bytes 56623108
  29.0 5.7 %collective-permute-start = (f32[2,192,256]{2,1,0:T(8,128)S(1)}, f32[2,192,256]{2,1,0:T(8,128)S(1)}, u32[]{:S(2)}, u32[]{:S(2)}) collective-permute-start(f32[2,192,256]{2,1,0:T(8,128)S(1)} %get-tuple-element.67), channel_id=1, source_target_pairs={{0,1},{1,0},{2,3},{3,2},{4,5},{5,4},{6,7},{7,6},{8,9},{9,8},{10,11... | collective-permute-start | bytes 1179656 | tf_op jit(solution)/shard_map/ppermute | solution.py:346
  29.1 5.7 %collective-permute-start.1 = (f32[2,192,256]{2,1,0:T(8,128)S(1)}, f32[2,192,256]{2,1,0:T(8,128)S(1)}, u32[]{:S(2)}, u32[]{:S(2)}) collective-permute-start(f32[2,192,256]{2,1,0:T(8,128)S(1)} %get-tuple-element.68), channel_id=1, source_target_pairs={{0,1},{1,0},{2,3},{3,2},{4,5},{5,4},{6,7},{7,6},{8,9},{9,8},{10,11... | collective-permute-start | bytes 1179656 | tf_op jit(solution)/shard_map/ppermute | solution.py:346
  33.1 33.3 %collective-permute-start.13 = (f32[96,2304]{1,0:T(8,128)}, f32[96,2304]{1,0:T(8,128)S(1)}, u32[]{:S(2)}, u32[]{:S(2)}) collective-permute-start(f32[96,2304]{1,0:T(8,128)} %collective-permute-done.3.refs_0_.refs_1_), channel_id=1, source_target_pairs={{0,4},{4,8},{8,12},{12,0},{1,5},{5,9},{9,13},{13,1},{2,6},{6,10},{... | collective-permute-start | bytes 2654216 | tf_op jit(solution)/shard_map/ppermute | solution.py:323
  47.6 37.8 %collective-permute-start.12 = (f32[96,2304]{1,0:T(8,128)}, f32[96,2304]{1,0:T(8,128)S(1)}, u32[]{:S(2)}, u32[]{:S(2)}) collective-permute-start(f32[96,2304]{1,0:T(8,128)} %collective-permute-done.4.refs_1_.refs_2_), channel_id=1, source_target_pairs={{0,4},{4,8},{8,12},{12,0},{1,5},{5,9},{9,13},{13,1},{2,6},{6,10},{... | collective-permute-start | bytes 2654216 | tf_op jit(solution)/shard_map/ppermute | solution.py:323
  47.6 20.7 %collective-permute-start.2 = (f32[2,2,192,256]{3,2,1,0:T(8,128)S(1)}, f32[2,2,192,256]{3,2,1,0:T(8,128)S(1)}, u32[]{:S(2)}, u32[]{:S(2)}) collective-permute-start(f32[2,2,192,256]{3,2,1,0:T(8,128)S(1)} %add.30.sums_ref), channel_id=1, source_target_pairs={{0,2},{1,3},{2,0},{3,1},{4,6},{5,7},{6,4},{7,5},{8,10},{9,11},{10,... | collective-permute-start | bytes 2359304 | tf_op jit(solution)/shard_map/ppermute | solution.py:359
  54.3 12.2 %collective-permute-start.5 = (f32[2,192,256]{2,1,0:T(8,128)S(1)}, f32[2,192,256]{2,1,0:T(8,128)S(1)}, u32[]{:S(2)}, u32[]{:S(2)}) collective-permute-start(f32[2,192,256]{2,1,0:T(8,128)S(1)} %get-tuple-element.75), channel_id=1, source_target_pairs={{0,1},{1,0},{2,3},{3,2},{4,5},{5,4},{6,7},{7,6},{8,9},{9,8},{10,11... | collective-permute-start | bytes 1179656 | tf_op jit(solution)/shard_map/ppermute | solution.py:346
  54.3 12.1 %collective-permute-start.6 = (f32[2,192,256]{2,1,0:T(8,128)S(1)}, f32[2,192,256]{2,1,0:T(8,128)S(1)}, u32[]{:S(2)}, u32[]{:S(2)}) collective-permute-start(f32[2,192,256]{2,1,0:T(8,128)S(1)} %get-tuple-element.76), channel_id=1, source_target_pairs={{0,1},{1,0},{2,3},{3,2},{4,5},{5,4},{6,7},{7,6},{8,9},{9,8},{10,11... | collective-permute-start | bytes 1179656 | tf_op jit(solution)/shard_map/ppermute | solution.py:346
  66.4 37.9 %collective-permute-start.15 = (f32[96,2304]{1,0:T(8,128)S(1)}, f32[96,2304]{1,0:T(8,128)S(1)}, u32[]{:S(2)}, u32[]{:S(2)}) collective-permute-start(f32[96,2304]{1,0:T(8,128)S(1)} %collective-permute-done.13.refs_0_), channel_id=1, source_target_pairs={{0,4},{4,8},{8,12},{12,0},{1,5},{5,9},{9,13},{13,1},{2,6},{6,10},{... | collective-permute-start | bytes 2654216 | tf_op jit(solution)/shard_map/ppermute | solution.py:323
  66.5 41.6 %collective-permute-start.7 = (f32[2,2,192,256]{3,2,1,0:T(8,128)S(1)}, f32[2,2,192,256]{3,2,1,0:T(8,128)S(1)}, u32[]{:S(2)}, u32[]{:S(2)}) collective-permute-start(f32[2,2,192,256]{3,2,1,0:T(8,128)S(1)} %add.31.sums_ref), channel_id=1, source_target_pairs={{0,2},{1,3},{2,0},{3,1},{4,6},{5,7},{6,4},{7,5},{8,10},{9,11},{10,... | collective-permute-start | bytes 2359304 | tf_op jit(solution)/shard_map/ppermute | solution.py:359
  85.4 37.1 %collective-permute-start.14 = (f32[96,2304]{1,0:T(8,128)S(1)}, f32[96,2304]{1,0:T(8,128)S(1)}, u32[]{:S(2)}, u32[]{:S(2)}) collective-permute-start(f32[96,2304]{1,0:T(8,128)S(1)} %collective-permute-done.12.refs_1_), channel_id=1, source_target_pairs={{0,4},{4,8},{8,12},{12,0},{1,5},{5,9},{9,13},{13,1},{2,6},{6,10},{... | collective-permute-start | bytes 2654216 | tf_op jit(solution)/shard_map/ppermute | solution.py:323
  88.9 18.5 %collective-permute-start.16 = (f32[2,192,256]{2,1,0:T(8,128)S(1)}, f32[2,192,256]{2,1,0:T(8,128)S(1)}, u32[]{:S(2)}, u32[]{:S(2)}) collective-permute-start(f32[2,192,256]{2,1,0:T(8,128)S(1)} %get-tuple-element.88), channel_id=1, source_target_pairs={{0,1},{1,0},{2,3},{3,2},{4,5},{5,4},{6,7},{7,6},{8,9},{9,8},{10,11... | collective-permute-start | bytes 1179656 | tf_op jit(solution)/shard_map/ppermute | solution.py:346
  89.0 19.0 %collective-permute-start.17 = (f32[2,192,256]{2,1,0:T(8,128)S(1)}, f32[2,192,256]{2,1,0:T(8,128)S(1)}, u32[]{:S(2)}, u32[]{:S(2)}) collective-permute-start(f32[2,192,256]{2,1,0:T(8,128)S(1)} %get-tuple-element.89), channel_id=1, source_target_pairs={{0,1},{1,0},{2,3},{3,2},{4,5},{5,4},{6,7},{7,6},{8,9},{9,8},{10,11... | collective-permute-start | bytes 1179656 | tf_op jit(solution)/shard_map/ppermute | solution.py:346
  107.4 6.4 %collective-permute-start.18 = (f32[2,96,256]{2,1,0:T(8,128)S(1)}, f32[2,96,256]{2,1,0:T(8,128)S(1)}, u32[]{:S(2)}, u32[]{:S(2)}) collective-permute-start(f32[2,96,256]{2,1,0:T(8,128)S(1)} %get-tuple-element.94), channel_id=1, source_target_pairs={{0,1},{1,0},{2,3},{3,2},{4,5},{5,4},{6,7},{7,6},{8,9},{9,8},{10,11... | collective-permute-start | bytes 589832 | tf_op jit(solution)/shard_map/ppermute | solution.py:346
  107.5 6.3 %collective-permute-start.19 = (f32[2,96,256]{2,1,0:T(8,128)S(1)}, f32[2,96,256]{2,1,0:T(8,128)S(1)}, u32[]{:S(2)}, u32[]{:S(2)}) collective-permute-start(f32[2,96,256]{2,1,0:T(8,128)S(1)} %get-tuple-element.95), channel_id=1, source_target_pairs={{0,1},{1,0},{2,3},{3,2},{4,5},{5,4},{6,7},{7,6},{8,9},{9,8},{10,11... | collective-permute-start | bytes 589832 | tf_op jit(solution)/shard_map/ppermute | solution.py:346
  108.0 18.2 %collective-permute-start.9 = (f32[2,192,256]{2,1,0:T(8,128)S(1)}, f32[2,192,256]{2,1,0:T(8,128)S(1)}, u32[]{:S(2)}, u32[]{:S(2)}) collective-permute-start(f32[2,192,256]{2,1,0:T(8,128)S(1)} %get-tuple-element.73.refs_1_), channel_id=1, source_target_pairs={{0,1},{1,0},{2,3},{3,2},{4,5},{5,4},{6,7},{7,6},{8,9},{9,8},{10,11... | collective-permute-start | bytes 1179656 | tf_op jit(solution)/shard_map/ppermute | solution.py:366
  108.2 42.0 %collective-permute-start.22 = (f32[2,2,192,256]{3,2,1,0:T(8,128)S(1)}, f32[2,2,192,256]{3,2,1,0:T(8,128)S(1)}, u32[]{:S(2)}, u32[]{:S(2)}) collective-permute-start(f32[2,2,192,256]{3,2,1,0:T(8,128)S(1)} %add.32.sums_ref), channel_id=1, source_target_pairs={{0,2},{1,3},{2,0},{3,1},{4,6},{5,7},{6,4},{7,5},{8,10},{9,11},{10,... | collective-permute-start | bytes 2359304 | tf_op jit(solution)/shard_map/ppermute | solution.py:359
  125.5 1.5 collective-permute-start.20
  125.6 6.9 %collective-permute-start.8 = (f32[2,192,256]{2,1,0:T(8,128)S(1)}, f32[2,192,256]{2,1,0:T(8,128)S(1)}, u32[]{:S(2)}, u32[]{:S(2)}) collective-permute-start(f32[2,192,256]{2,1,0:T(8,128)S(1)} %get-tuple-element.72.refs_0_), channel_id=1, source_target_pairs={{0,1},{1,0},{2,3},{3,2},{4,5},{5,4},{6,7},{7,6},{8,9},{9,8},{10,11... | collective-permute-start | bytes 1179656 | tf_op jit(solution)/shard_map/ppermute | solution.py:366
  126.1 1.8 %collective-permute-start.21 = (f32[2,96,256]{2,1,0:T(8,128)S(1)}, f32[2,96,256]{2,1,0:T(8,128)S(1)}, u32[]{:S(2)}, u32[]{:S(2)}) collective-permute-start(f32[2,96,256]{2,1,0:T(8,128)S(1)} %get-tuple-element.101), channel_id=1, source_target_pairs={{0,1},{1,0},{2,3},{3,2},{4,5},{5,4},{6,7},{7,6},{8,9},{9,8},{10,11... | collective-permute-start | bytes 589832 | tf_op jit(solution)/shard_map/ppermute | solution.py:346
  126.2 9.9 %collective-permute-start.11 = (f32[2,192,256]{2,1,0:T(8,128)S(1)}, f32[2,192,256]{2,1,0:T(8,128)S(1)}, u32[]{:S(2)}, u32[]{:S(2)}) collective-permute-start(f32[2,192,256]{2,1,0:T(8,128)S(1)} %get-tuple-element.82.refs_3_), channel_id=1, source_target_pairs={{0,1},{1,0},{2,3},{3,2},{4,5},{5,4},{6,7},{7,6},{8,9},{9,8},{10,11... | collective-permute-start | bytes 1179656 | tf_op jit(solution)/shard_map/ppermute | solution.py:366
  127.0 9.1 %collective-permute-start.10 = (f32[2,192,256]{2,1,0:T(8,128)S(1)}, f32[2,192,256]{2,1,0:T(8,128)S(1)}, u32[]{:S(2)}, u32[]{:S(2)}) collective-permute-start(f32[2,192,256]{2,1,0:T(8,128)S(1)} %get-tuple-element.81.refs_2_), channel_id=1, source_target_pairs={{0,1},{1,0},{2,3},{3,2},{4,5},{5,4},{6,7},{7,6},{8,9},{9,8},{10,11... | collective-permute-start | bytes 1179656 | tf_op jit(solution)/shard_map/ppermute | solution.py:366
  127.9 23.6 %collective-permute-start.23 = (f32[2,2,96,256]{3,2,1,0:T(8,128)S(1)}, f32[2,2,96,256]{3,2,1,0:T(8,128)S(1)}, u32[]{:S(2)}, u32[]{:S(2)}) collective-permute-start(f32[2,2,96,256]{3,2,1,0:T(8,128)S(1)} %add.33.sums_ref), channel_id=1, source_target_pairs={{0,2},{1,3},{2,0},{3,1},{4,6},{5,7},{6,4},{7,5},{8,10},{9,11},{10,... | collective-permute-start | bytes 1179656 | tf_op jit(solution)/shard_map/ppermute | solution.py:359
  132.5 20.3 %collective-permute-start.24 = (f32[2,2,96,256]{3,2,1,0:T(8,128)S(1)}, f32[2,2,96,256]{3,2,1,0:T(8,128)S(1)}, u32[]{:S(2)}, u32[]{:S(2)}) collective-permute-start(f32[2,2,96,256]{3,2,1,0:T(8,128)S(1)} %add.34.sums_ref), channel_id=1, source_target_pairs={{0,2},{1,3},{2,0},{3,1},{4,6},{5,7},{6,4},{7,5},{8,10},{9,11},{10,... | collective-permute-start | bytes 1179656 | tf_op jit(solution)/shard_map/ppermute | solution.py:359
  150.9 3.1 %collective-permute-start.25 = (f32[2,192,256]{2,1,0:T(8,128)S(1)}, f32[2,192,256]{2,1,0:T(8,128)S(1)}, u32[]{:S(2)}, u32[]{:S(2)}) collective-permute-start(f32[2,192,256]{2,1,0:T(8,128)S(1)} %get-tuple-element.109.refs_0_), channel_id=1, source_target_pairs={{0,1},{1,0},{2,3},{3,2},{4,5},{5,4},{6,7},{7,6},{8,9},{9,8},{10,11... | collective-permute-start | bytes 1179656 | tf_op jit(solution)/shard_map/ppermute | solution.py:366
  151.0 3.0 %collective-permute-start.26 = (f32[2,192,256]{2,1,0:T(8,128)S(1)}, f32[2,192,256]{2,1,0:T(8,128)S(1)}, u32[]{:S(2)}, u32[]{:S(2)}) collective-permute-start(f32[2,192,256]{2,1,0:T(8,128)S(1)} %get-tuple-element.110.refs_1_), channel_id=1, source_target_pairs={{0,1},{1,0},{2,3},{3,2},{4,5},{5,4},{6,7},{7,6},{8,9},{9,8},{10,11... | collective-permute-start | bytes 1179656 | tf_op jit(solution)/shard_map/ppermute | solution.py:366
  152.2 1.5 collective-permute-start.27
  152.4 1.7 collective-permute-start.28
  153.5 1.5 collective-permute-start.29
  153.7 1.5 collective-permute-start.30
  (1 other events, 6.2 us)

commit v5 on v4

--- a/solution.py
+++ b/solution.py
@@ -246,7 +246,7 @@
 
 def finish(mine, other, noise, stack, prior, share, unit, scalars, scale, sizes):
     across, rows, pairs = sizes
-    tiles = 3 if pairs % 384 == 0 else 1
+    tiles = 2 if pairs % 256 == 0 else 1
     turned = (share.shape[0], share.shape[2], share.shape[1])
     in_specs = [pl.BlockSpec((1, *part.shape[1:]), lambda t, x, p, s: (x, 0, 0)) for part in (*mine, *other)]
     in_specs += [

time: 178 us -> 178 us (level)
  no operation moved by 1% of the time
where the time goes in v5:
time: 178 us
  Pallas kernels  85.6 us (48%)
  waiting for transfers between devices  58.1 us (33%)
  starting transfers between devices  18.9 us (11%)
  local copies, waits for them, and re-layouts  14 us (8%)
    ppermute x6, waiting for transfers between devices, hop(): lax.ppermute(after(held[step - 1, start], *token), 'field', ring)  55.6 us
    pallas_call x10, Pallas kernels, bias_of(): pl.pallas_call(functools.partial(bias_kernel, len(parts)), out_shape=[jax...  36.1 us
    pallas_call x1, Pallas kernels, finish(): pl.pallas_call(functools.partial(finish_kernel, len(mine), len(unit), uni...  22.2 us
    pallas_call x1, Pallas kernels, begin(): pl.pallas_call(functools.partial(begin_kernel, len(mine), unit), out_shap...  14.1 us
    ppermute x5, starting transfers between devices, across_chips(): lax.ppermute(total, 'pair', [(i, i ^ reach) for i in range(pair_size)])  7.38 us
    unnamed x4, local copies, waits for them, and re-layouts  6.37 us
    ppermute x6, starting transfers between devices, hop(): lax.ppermute(after(held[step - 1, start], *token), 'field', ring)  6.34 us
    pallas_call x1, Pallas kernels, split_green(): pl.pallas_call(split_green_kernel, out_shape=[pltpu.VMEM((channels, acros...  6.2 us
  transfers between devices with their start and end apart: 31, of which 10 were waited for; matrix products, arithmetic and copies ran while one was open for 3% of the time, Pallas kernels for 36%

profile of v5, /device:TPU:0, one launch (start us, length us, event | category | flops | bytes accessed | tf_op | source)
XLA Modules:
  0.0 177.5 jit_solution(17824267510632773977)
XLA Ops:
  0.6 2.1 %slice.6 = f32[96,2304]{1,0:T(8,128)} slice(f32[192,2304]{1,0:T(8,128)} %refs_0_.2), slice={[0:96], [0:2304]} | slice | bytes 1769472 | tf_op jit(solution)/shard_map/slice | solution.py:308
  2.8 3.0 %collective-permute-start.3 = (f32[96,2304]{1,0:T(8,128)}, f32[96,2304]{1,0:T(8,128)}, u32[]{:S(2)}, u32[]{:S(2)}) collective-permute-start(f32[96,2304]{1,0:T(8,128)} %slice.6), channel_id=1, source_target_pairs={{0,4},{4,8},{8,12},{12,0},{1,5},{5,9},{9,13},{13,1},{2,6},{6,10},{... | collective-permute-start | bytes 2654216 | tf_op jit(solution)/shard_map/ppermute | solution.py:323
  5.8 2.1 %slice.7 = f32[96,2304]{1,0:T(8,128)} slice(f32[192,2304]{1,0:T(8,128)} %refs_0_.2), slice={[96:192], [0:2304]} | slice | bytes 1769472 | tf_op jit(solution)/shard_map/slice | solution.py:308
  7.9 1.6 collective-permute-start.4
  10.4 2.4 %copy.11 = f32[768,1024]{1,0:T(8,128)S(1)} copy(f32[768,1024]{0,1:T(8,128)} %bitcast.25) | data formatting | bytes 6291456 | tf_op jit(solution)/shard_map/transpose | solution.py:331
  12.9 6.4 %copy-done.1 = f32[2,1024,2304]{2,1,0:T(8,128)S(1)} copy-done((f32[2,1024,2304]{2,1,0:T(8,128)S(1)}, f32[2,1024,2304]{2,1,0:T(8,128)}, u32[]{:S(2)}) %copy-start.1) | copy-done | bytes 18874392
  19.3 6.2 %split_green.1 = (bf16[2,2,256,2304]{3,2,1,0:T(8,128)(2,1)S(1)}, bf16[2,2,256,2304]{3,2,1,0:T(8,128)(2,1)S(1)}, bf16[2,2,256,2304]{3,2,1,0:T(8,128)(2,1)S(1)}, bf16[2,2,256,2304]{3,2,1,0:T(8,128)(2,1)S(1)}) custom-call(s32[6]{0:T(128)S(1)} %stack.34.s_ref, f32[2,2,2,256,2304]{4,3,2,1,0:T(8,128)S(1)} %bitcast.19), custom_call_target="tpu_custom_call" | custom-call | flops 1 | bytes 1 | tf_op jit(solution)/shard_map/split_green/pallas_call | solution.py:48
  25.5 3.5 %bias.10 = (f32[2,192,256]{2,1,0:T(8,128)S(1)}, f32[2,192,256]{2,1,0:T(8,128)S(1)}) custom-call(bf16[2,2,256,2304]{3,2,1,0:T(8,128)(2,1)S(1)} %get-tuple-element.65.high_ref, bf16[2,2,256,2304]{3,2,1,0:T(8,128)(2,1)S(1)} %get-tuple-element.66.low_ref, f32[192,2304]{1,0:T(8,128)S(1)} %copy-done), custom_call_target="tpu_custom_call" | custom-call | flops 1 | bytes 1 | tf_op jit(solution)/shard_map/bias/pallas_call | solution.py:78
  29.6 3.5 %bias.11 = (f32[2,192,256]{2,1,0:T(8,128)S(1)}, f32[2,192,256]{2,1,0:T(8,128)S(1)}) custom-call(bf16[2,2,256,2304]{3,2,1,0:T(8,128)(2,1)S(1)} %get-tuple-element.63.high_ref, bf16[2,2,256,2304]{3,2,1,0:T(8,128)(2,1)S(1)} %get-tuple-element.64.low_ref, f32[192,2304]{1,0:T(8,128)S(1)} %copy-done), custom_call_target="tpu_custom_call" | custom-call | flops 1 | bytes 1 | tf_op jit(solution)/shard_map/bias/pallas_call | solution.py:78
  33.1 1.6 collective-permute-start.13
  34.8 12.7 %collective-permute-done.4.refs_1_.refs_2_ = f32[96,2304]{1,0:T(8,128)} collective-permute-done((f32[96,2304]{1,0:T(8,128)}, f32[96,2304]{1,0:T(8,128)}, u32[]{:S(2)}, u32[]{:S(2)}) %collective-permute-start.4) | collective-permute-done | bytes 884768 | tf_op jit(solution)/shard_map/ppermute | solution.py:323
  47.6 1.7 collective-permute-start.2
  49.3 4.9 %bias.12 = (f32[2,192,256]{2,1,0:T(8,128)S(1)}, f32[2,192,256]{2,1,0:T(8,128)S(1)}) custom-call(bf16[2,2,256,2304]{3,2,1,0:T(8,128)(2,1)S(1)} %get-tuple-element.65.high_ref, bf16[2,2,256,2304]{3,2,1,0:T(8,128)(2,1)S(1)} %get-tuple-element.66.low_ref, f32[96,2304]{1,0:T(8,128)} %collective-permute-done.3.refs_0_.refs_1_, ...), custom_call_target="tpu_custom_call" | custom-call | flops 1 | bytes 1 | tf_op jit(solution)/shard_map/bias/pallas_call | solution.py:78
  54.8 4.9 %bias.13 = (f32[2,192,256]{2,1,0:T(8,128)S(1)}, f32[2,192,256]{2,1,0:T(8,128)S(1)}) custom-call(bf16[2,2,256,2304]{3,2,1,0:T(8,128)(2,1)S(1)} %get-tuple-element.63.high_ref, bf16[2,2,256,2304]{3,2,1,0:T(8,128)(2,1)S(1)} %get-tuple-element.64.low_ref, f32[96,2304]{1,0:T(8,128)} %collective-permute-done.3.refs_0_.refs_1_, ...), custom_call_target="tpu_custom_call" | custom-call | flops 1 | bytes 1 | tf_op jit(solution)/shard_map/bias/pallas_call | solution.py:78
  59.8 6.6 %collective-permute-done.13.refs_0_ = f32[96,2304]{1,0:T(8,128)S(1)} collective-permute-done((f32[96,2304]{1,0:T(8,128)}, f32[96,2304]{1,0:T(8,128)S(1)}, u32[]{:S(2)}, u32[]{:S(2)}) %collective-permute-start.13) | collective-permute-done | bytes 884768 | tf_op jit(solution)/shard_map/ppermute | solution.py:323
  66.5 1.8 %collective-permute-start.7 = (f32[2,2,192,256]{3,2,1,0:T(8,128)S(1)}, f32[2,2,192,256]{3,2,1,0:T(8,128)S(1)}, u32[]{:S(2)}, u32[]{:S(2)}) collective-permute-start(f32[2,2,192,256]{3,2,1,0:T(8,128)S(1)} %add.31.sums_ref), channel_id=1, source_target_pairs={{0,2},{1,3},{2,0},{3,1},{4,6},{5,7},{6,4},{7,5},{8,10},{9,11},{10,... | collective-permute-start | bytes 2359304 | tf_op jit(solution)/shard_map/ppermute | solution.py:359
  69.1 16.3 %collective-permute-done.12.refs_1_ = f32[96,2304]{1,0:T(8,128)S(1)} collective-permute-done((f32[96,2304]{1,0:T(8,128)}, f32[96,2304]{1,0:T(8,128)S(1)}, u32[]{:S(2)}, u32[]{:S(2)}) %collective-permute-start.12) | collective-permute-done | bytes 884768 | tf_op jit(solution)/shard_map/ppermute | solution.py:323
  85.4 3.5 %bias.14 = (f32[2,192,256]{2,1,0:T(8,128)S(1)}, f32[2,192,256]{2,1,0:T(8,128)S(1)}) custom-call(bf16[2,2,256,2304]{3,2,1,0:T(8,128)(2,1)S(1)} %get-tuple-element.65.high_ref, bf16[2,2,256,2304]{3,2,1,0:T(8,128)(2,1)S(1)} %get-tuple-element.66.low_ref, f32[96,2304]{1,0:T(8,128)S(1)} %collective-permute-done.13.refs_0_, ...), custom_call_target="tpu_custom_call" | custom-call | flops 1 | bytes 1 | tf_op jit(solution)/shard_map/bias/pallas_call | solution.py:78
  89.5 3.5 %bias.15 = (f32[2,192,256]{2,1,0:T(8,128)S(1)}, f32[2,192,256]{2,1,0:T(8,128)S(1)}) custom-call(bf16[2,2,256,2304]{3,2,1,0:T(8,128)(2,1)S(1)} %get-tuple-element.63.high_ref, bf16[2,2,256,2304]{3,2,1,0:T(8,128)(2,1)S(1)} %get-tuple-element.64.low_ref, f32[96,2304]{1,0:T(8,128)S(1)} %collective-permute-done.13.refs_0_, ...), custom_call_target="tpu_custom_call" | custom-call | flops 1 | bytes 1 | tf_op jit(solution)/shard_map/bias/pallas_call | solution.py:78
  93.0 11.3 %collective-permute-done.15.refs_0_.refs_2_ = f32[96,2304]{1,0:T(8,128)S(1)} collective-permute-done((f32[96,2304]{1,0:T(8,128)S(1)}, f32[96,2304]{1,0:T(8,128)S(1)}, u32[]{:S(2)}, u32[]{:S(2)}) %collective-permute-start.15) | collective-permute-done | bytes 884768 | tf_op jit(solution)/shard_map/ppermute | solution.py:323
  104.3 3.1 %bias.16 = (f32[2,96,256]{2,1,0:T(8,128)S(1)}, f32[2,96,256]{2,1,0:T(8,128)S(1)}) custom-call(bf16[2,2,256,2304]{3,2,1,0:T(8,128)(2,1)S(1)} %get-tuple-element.65.high_ref, bf16[2,2,256,2304]{3,2,1,0:T(8,128)(2,1)S(1)} %get-tuple-element.66.low_ref, f32[96,2304]{1,0:T(8,128)S(1)} %collective-permute-done.15.refs_0_.refs_2_), custom_call_target="tpu_custom_call" | custom-call | flops 1 | bytes 1 | tf_op jit(solution)/shard_map/bias/pallas_call | solution.py:78
  108.2 1.8 %collective-permute-start.22 = (f32[2,2,192,256]{3,2,1,0:T(8,128)S(1)}, f32[2,2,192,256]{3,2,1,0:T(8,128)S(1)}, u32[]{:S(2)}, u32[]{:S(2)}) collective-permute-start(f32[2,2,192,256]{3,2,1,0:T(8,128)S(1)} %add.32.sums_ref), channel_id=1, source_target_pairs={{0,2},{1,3},{2,0},{3,1},{4,6},{5,7},{6,4},{7,5},{8,10},{9,11},{10,... | collective-permute-start | bytes 2359304 | tf_op jit(solution)/shard_map/ppermute | solution.py:359
  110.7 3.1 %bias.17 = (f32[2,96,256]{2,1,0:T(8,128)S(1)}, f32[2,96,256]{2,1,0:T(8,128)S(1)}) custom-call(bf16[2,2,256,2304]{3,2,1,0:T(8,128)(2,1)S(1)} %get-tuple-element.63.high_ref, bf16[2,2,256,2304]{3,2,1,0:T(8,128)(2,1)S(1)} %get-tuple-element.64.low_ref, f32[96,2304]{1,0:T(8,128)S(1)} %collective-permute-done.15.refs_0_.refs_2_), custom_call_target="tpu_custom_call" | custom-call | flops 1 | bytes 1 | tf_op jit(solution)/shard_map/bias/pallas_call | solution.py:78
  113.9 8.6 %collective-permute-done.14.refs_0_.refs_3_ = f32[96,2304]{1,0:T(8,128)S(1)} collective-permute-done((f32[96,2304]{1,0:T(8,128)S(1)}, f32[96,2304]{1,0:T(8,128)S(1)}, u32[]{:S(2)}, u32[]{:S(2)}) %collective-permute-start.14) | collective-permute-done | bytes 884768 | tf_op jit(solution)/shard_map/ppermute | solution.py:323
  122.5 3.1 %bias.18 = (f32[2,96,256]{2,1,0:T(8,128)S(1)}, f32[2,96,256]{2,1,0:T(8,128)S(1)}) custom-call(bf16[2,2,256,2304]{3,2,1,0:T(8,128)(2,1)S(1)} %get-tuple-element.65.high_ref, bf16[2,2,256,2304]{3,2,1,0:T(8,128)(2,1)S(1)} %get-tuple-element.66.low_ref, f32[96,2304]{1,0:T(8,128)S(1)} %collective-permute-done.14.refs_0_.refs_3_), custom_call_target="tpu_custom_call" | custom-call | flops 1 | bytes 1 | tf_op jit(solution)/shard_map/bias/pallas_call | solution.py:78
  127.9 1.5 collective-permute-start.23
  129.4 3.1 %bias.19 = (f32[2,96,256]{2,1,0:T(8,128)S(1)}, f32[2,96,256]{2,1,0:T(8,128)S(1)}) custom-call(bf16[2,2,256,2304]{3,2,1,0:T(8,128)(2,1)S(1)} %get-tuple-element.63.high_ref, bf16[2,2,256,2304]{3,2,1,0:T(8,128)(2,1)S(1)} %get-tuple-element.64.low_ref, f32[96,2304]{1,0:T(8,128)S(1)} %collective-permute-done.14.refs_0_.refs_3_), custom_call_target="tpu_custom_call" | custom-call | flops 1 | bytes 1 | tf_op jit(solution)/shard_map/bias/pallas_call | solution.py:78
  133.1 0.9 stack_cholesky.3.refs_16_
  134.0 2.1 %stack_cholesky.2.refs_11_ = bf16[1152,2304]{1,0:T(8,128)(2,1)S(1)} custom-call(f32[192,2304]{1,0:T(8,128)S(1)} %copy-done, f32[96,2304]{1,0:T(8,128)} %collective-permute-done.3.refs_0_.refs_1_, f32[96,2304]{1,0:T(8,128)} %collective-permute-done.4.refs_1_.refs_2_), custom_call_target="tpu_custom_call" | custom-call | flops 1 | bytes 1 | tf_op jit(solution)/shard_map/stack_cholesky/pallas_call | solution.py:182
  136.1 14.1 %begin.1.refs_17_ = f32[2,2,512,2304]{3,2,1,0:T(8,128)S(1)} custom-call(s32[6]{0:T(128)S(1)} %stack.34.s_ref, f32[2,192,256]{2,1,0:T(8,128)S(1)} %get-tuple-element.72.refs_0_, f32[2,192,256]{2,1,0:T(8,128)S(1)} %get-tuple-element.73.refs_1_, f32[2,192,256]{2,1,0:T(8,128)S(1)} %get-tuple-element.81.refs_2_, f32[2,192,256]{2,1,0:T(8,128)S(1)} %get-tuple-element.82.refs_3_, ...), custom_call_target="tpu_custom_call" | custom-call | flops 1 | bytes 1 | tf_op jit(solution)/shard_map/begin/pallas_call | solution.py:210
  154.1 0.9 collective-permute-done.29.refs_10_
  155.3 22.2 %finish.1 = (f32[2,2,256,2,2304]{4,3,2,1,0:T(2,128)}, f32[2,256,768]{2,1,0:T(8,128)}) custom-call(s32[6]{0:T(128)S(1)} %stack.34.s_ref, f32[2,192,256]{2,1,0:T(8,128)S(1)} %get-tuple-element.109.refs_0_, f32[2,192,256]{2,1,0:T(8,128)S(1)} %get-tuple-element.110.refs_1_, f32[2,96,256]{2,1,0:T(8,128)S(1)} %get-tuple-element.112.refs_2_, ...), custom_call_target="tpu_custom_call" | custom-call | flops 1 | bytes 1 | tf_op jit(solution)/shard_map/finish/pallas_call | solution.py:256
  (64 shorter events, 12.4 us)
Async XLA Ops:
  2.8 30.3 %collective-permute-start.3 = (f32[96,2304]{1,0:T(8,128)}, f32[96,2304]{1,0:T(8,128)}, u32[]{:S(2)}, u32[]{:S(2)}) collective-permute-start(f32[96,2304]{1,0:T(8,128)} %slice.6), channel_id=1, source_target_pairs={{0,4},{4,8},{8,12},{12,0},{1,5},{5,9},{9,13},{13,1},{2,6},{6,10},{... | collective-permute-start | bytes 2654216 | tf_op jit(solution)/shard_map/ppermute | solution.py:323
  7.9 39.6 %collective-permute-start.4 = (f32[96,2304]{1,0:T(8,128)}, f32[96,2304]{1,0:T(8,128)}, u32[]{:S(2)}, u32[]{:S(2)}) collective-permute-start(f32[96,2304]{1,0:T(8,128)} %slice.7), channel_id=1, source_target_pairs={{0,4},{4,8},{8,12},{12,0},{1,5},{5,9},{9,13},{13,1},{2,6},{6,10},{... | collective-permute-start | bytes 2654216 | tf_op jit(solution)/shard_map/ppermute | solution.py:323
  12.9 6.4 %copy-start.1 = (f32[2,1024,2304]{2,1,0:T(8,128)S(1)}, f32[2,1024,2304]{2,1,0:T(8,128)}, u32[]{:S(2)}) copy-start(f32[2,1024,2304]{2,1,0:T(8,128)} %param.5) | copy-start | bytes 56623108
  29.0 5.7 %collective-permute-start = (f32[2,192,256]{2,1,0:T(8,128)S(1)}, f32[2,192,256]{2,1,0:T(8,128)S(1)}, u32[]{:S(2)}, u32[]{:S(2)}) collective-permute-start(f32[2,192,256]{2,1,0:T(8,128)S(1)} %get-tuple-element.67), channel_id=1, source_target_pairs={{0,1},{1,0},{2,3},{3,2},{4,5},{5,4},{6,7},{7,6},{8,9},{9,8},{10,11... | collective-permute-start | bytes 1179656 | tf_op jit(solution)/shard_map/ppermute | solution.py:346
  29.1 5.7 %collective-permute-start.1 = (f32[2,192,256]{2,1,0:T(8,128)S(1)}, f32[2,192,256]{2,1,0:T(8,128)S(1)}, u32[]{:S(2)}, u32[]{:S(2)}) collective-permute-start(f32[2,192,256]{2,1,0:T(8,128)S(1)} %get-tuple-element.68), channel_id=1, source_target_pairs={{0,1},{1,0},{2,3},{3,2},{4,5},{5,4},{6,7},{7,6},{8,9},{9,8},{10,11... | collective-permute-start | bytes 1179656 | tf_op jit(solution)/shard_map/ppermute | solution.py:346
  33.1 33.3 %collective-permute-start.13 = (f32[96,2304]{1,0:T(8,128)}, f32[96,2304]{1,0:T(8,128)S(1)}, u32[]{:S(2)}, u32[]{:S(2)}) collective-permute-start(f32[96,2304]{1,0:T(8,128)} %collective-permute-done.3.refs_0_.refs_1_), channel_id=1, source_target_pairs={{0,4},{4,8},{8,12},{12,0},{1,5},{5,9},{9,13},{13,1},{2,6},{6,10},{... | collective-permute-start | bytes 2654216 | tf_op jit(solution)/shard_map/ppermute | solution.py:323
  47.6 37.8 %collective-permute-start.12 = (f32[96,2304]{1,0:T(8,128)}, f32[96,2304]{1,0:T(8,128)S(1)}, u32[]{:S(2)}, u32[]{:S(2)}) collective-permute-start(f32[96,2304]{1,0:T(8,128)} %collective-permute-done.4.refs_1_.refs_2_), channel_id=1, source_target_pairs={{0,4},{4,8},{8,12},{12,0},{1,5},{5,9},{9,13},{13,1},{2,6},{6,10},{... | collective-permute-start | bytes 2654216 | tf_op jit(solution)/shard_map/ppermute | solution.py:323
  47.6 20.7 %collective-permute-start.2 = (f32[2,2,192,256]{3,2,1,0:T(8,128)S(1)}, f32[2,2,192,256]{3,2,1,0:T(8,128)S(1)}, u32[]{:S(2)}, u32[]{:S(2)}) collective-permute-start(f32[2,2,192,256]{3,2,1,0:T(8,128)S(1)} %add.30.sums_ref), channel_id=1, source_target_pairs={{0,2},{1,3},{2,0},{3,1},{4,6},{5,7},{6,4},{7,5},{8,10},{9,11},{10,... | collective-permute-start | bytes 2359304 | tf_op jit(solution)/shard_map/ppermute | solution.py:359
  54.3 12.2 %collective-permute-start.5 = (f32[2,192,256]{2,1,0:T(8,128)S(1)}, f32[2,192,256]{2,1,0:T(8,128)S(1)}, u32[]{:S(2)}, u32[]{:S(2)}) collective-permute-start(f32[2,192,256]{2,1,0:T(8,128)S(1)} %get-tuple-element.75), channel_id=1, source_target_pairs={{0,1},{1,0},{2,3},{3,2},{4,5},{5,4},{6,7},{7,6},{8,9},{9,8},{10,11... | collective-permute-start | bytes 1179656 | tf_op jit(solution)/shard_map/ppermute | solution.py:346
  54.3 12.1 %collective-permute-start.6 = (f32[2,192,256]{2,1,0:T(8,128)S(1)}, f32[2,192,256]{2,1,0:T(8,128)S(1)}, u32[]{:S(2)}, u32[]{:S(2)}) collective-permute-start(f32[2,192,256]{2,1,0:T(8,128)S(1)} %get-tuple-element.76), channel_id=1, source_target_pairs={{0,1},{1,0},{2,3},{3,2},{4,5},{5,4},{6,7},{7,6},{8,9},{9,8},{10,11... | collective-permute-start | bytes 1179656 | tf_op jit(solution)/shard_map/ppermute | solution.py:346
  66.4 37.9 %collective-permute-start.15 = (f32[96,2304]{1,0:T(8,128)S(1)}, f32[96,2304]{1,0:T(8,128)S(1)}, u32[]{:S(2)}, u32[]{:S(2)}) collective-permute-start(f32[96,2304]{1,0:T(8,128)S(1)} %collective-permute-done.13.refs_0_), channel_id=1, source_target_pairs={{0,4},{4,8},{8,12},{12,0},{1,5},{5,9},{9,13},{13,1},{2,6},{6,10},{... | collective-permute-start | bytes 2654216 | tf_op jit(solution)/shard_map/ppermute | solution.py:323
  66.5 41.6 %collective-permute-start.7 = (f32[2,2,192,256]{3,2,1,0:T(8,128)S(1)}, f32[2,2,192,256]{3,2,1,0:T(8,128)S(1)}, u32[]{:S(2)}, u32[]{:S(2)}) collective-permute-start(f32[2,2,192,256]{3,2,1,0:T(8,128)S(1)} %add.31.sums_ref), channel_id=1, source_target_pairs={{0,2},{1,3},{2,0},{3,1},{4,6},{5,7},{6,4},{7,5},{8,10},{9,11},{10,... | collective-permute-start | bytes 2359304 | tf_op jit(solution)/shard_map/ppermute | solution.py:359
  85.4 37.1 %collective-permute-start.14 = (f32[96,2304]{1,0:T(8,128)S(1)}, f32[96,2304]{1,0:T(8,128)S(1)}, u32[]{:S(2)}, u32[]{:S(2)}) collective-permute-start(f32[96,2304]{1,0:T(8,128)S(1)} %collective-permute-done.12.refs_1_), channel_id=1, source_target_pairs={{0,4},{4,8},{8,12},{12,0},{1,5},{5,9},{9,13},{13,1},{2,6},{6,10},{... | collective-permute-start | bytes 2654216 | tf_op jit(solution)/shard_map/ppermute | solution.py:323
  88.9 18.5 %collective-permute-start.16 = (f32[2,192,256]{2,1,0:T(8,128)S(1)}, f32[2,192,256]{2,1,0:T(8,128)S(1)}, u32[]{:S(2)}, u32[]{:S(2)}) collective-permute-start(f32[2,192,256]{2,1,0:T(8,128)S(1)} %get-tuple-element.88), channel_id=1, source_target_pairs={{0,1},{1,0},{2,3},{3,2},{4,5},{5,4},{6,7},{7,6},{8,9},{9,8},{10,11... | collective-permute-start | bytes 1179656 | tf_op jit(solution)/shard_map/ppermute | solution.py:346
  89.0 19.0 %collective-permute-start.17 = (f32[2,192,256]{2,1,0:T(8,128)S(1)}, f32[2,192,256]{2,1,0:T(8,128)S(1)}, u32[]{:S(2)}, u32[]{:S(2)}) collective-permute-start(f32[2,192,256]{2,1,0:T(8,128)S(1)} %get-tuple-element.89), channel_id=1, source_target_pairs={{0,1},{1,0},{2,3},{3,2},{4,5},{5,4},{6,7},{7,6},{8,9},{9,8},{10,11... | collective-permute-start | bytes 1179656 | tf_op jit(solution)/shard_map/ppermute | solution.py:346
  107.4 6.4 %collective-permute-start.18 = (f32[2,96,256]{2,1,0:T(8,128)S(1)}, f32[2,96,256]{2,1,0:T(8,128)S(1)}, u32[]{:S(2)}, u32[]{:S(2)}) collective-permute-start(f32[2,96,256]{2,1,0:T(8,128)S(1)} %get-tuple-element.94), channel_id=1, source_target_pairs={{0,1},{1,0},{2,3},{3,2},{4,5},{5,4},{6,7},{7,6},{8,9},{9,8},{10,11... | collective-permute-start | bytes 589832 | tf_op jit(solution)/shard_map/ppermute | solution.py:346
  107.5 6.3 %collective-permute-start.19 = (f32[2,96,256]{2,1,0:T(8,128)S(1)}, f32[2,96,256]{2,1,0:T(8,128)S(1)}, u32[]{:S(2)}, u32[]{:S(2)}) collective-permute-start(f32[2,96,256]{2,1,0:T(8,128)S(1)} %get-tuple-element.95), channel_id=1, source_target_pairs={{0,1},{1,0},{2,3},{3,2},{4,5},{5,4},{6,7},{7,6},{8,9},{9,8},{10,11... | collective-permute-start | bytes 589832 | tf_op jit(solution)/shard_map/ppermute | solution.py:346
  108.0 18.2 %collective-permute-start.9 = (f32[2,192,256]{2,1,0:T(8,128)S(1)}, f32[2,192,256]{2,1,0:T(8,128)S(1)}, u32[]{:S(2)}, u32[]{:S(2)}) collective-permute-start(f32[2,192,256]{2,1,0:T(8,128)S(1)} %get-tuple-element.73.refs_1_), channel_id=1, source_target_pairs={{0,1},{1,0},{2,3},{3,2},{4,5},{5,4},{6,7},{7,6},{8,9},{9,8},{10,11... | collective-permute-start | bytes 1179656 | tf_op jit(solution)/shard_map/ppermute | solution.py:366
  108.2 42.0 %collective-permute-start.22 = (f32[2,2,192,256]{3,2,1,0:T(8,128)S(1)}, f32[2,2,192,256]{3,2,1,0:T(8,128)S(1)}, u32[]{:S(2)}, u32[]{:S(2)}) collective-permute-start(f32[2,2,192,256]{3,2,1,0:T(8,128)S(1)} %add.32.sums_ref), channel_id=1, source_target_pairs={{0,2},{1,3},{2,0},{3,1},{4,6},{5,7},{6,4},{7,5},{8,10},{9,11},{10,... | collective-permute-start | bytes 2359304 | tf_op jit(solution)/shard_map/ppermute | solution.py:359
  125.5 1.5 collective-permute-start.20
  125.6 6.9 %collective-permute-start.8 = (f32[2,192,256]{2,1,0:T(8,128)S(1)}, f32[2,192,256]{2,1,0:T(8,128)S(1)}, u32[]{:S(2)}, u32[]{:S(2)}) collective-permute-start(f32[2,192,256]{2,1,0:T(8,128)S(1)} %get-tuple-element.72.refs_0_), channel_id=1, source_target_pairs={{0,1},{1,0},{2,3},{3,2},{4,5},{5,4},{6,7},{7,6},{8,9},{9,8},{10,11... | collective-permute-start | bytes 1179656 | tf_op jit(solution)/shard_map/ppermute | solution.py:366
  126.1 1.8 collective-permute-start.21
  126.2 9.9 %collective-permute-start.11 = (f32[2,192,256]{2,1,0:T(8,128)S(1)}, f32[2,192,256]{2,1,0:T(8,128)S(1)}, u32[]{:S(2)}, u32[]{:S(2)}) collective-permute-start(f32[2,192,256]{2,1,0:T(8,128)S(1)} %get-tuple-element.82.refs_3_), channel_id=1, source_target_pairs={{0,1},{1,0},{2,3},{3,2},{4,5},{5,4},{6,7},{7,6},{8,9},{9,8},{10,11... | collective-permute-start | bytes 1179656 | tf_op jit(solution)/shard_map/ppermute | solution.py:366
  127.0 9.1 %collective-permute-start.10 = (f32[2,192,256]{2,1,0:T(8,128)S(1)}, f32[2,192,256]{2,1,0:T(8,128)S(1)}, u32[]{:S(2)}, u32[]{:S(2)}) collective-permute-start(f32[2,192,256]{2,1,0:T(8,128)S(1)} %get-tuple-element.81.refs_2_), channel_id=1, source_target_pairs={{0,1},{1,0},{2,3},{3,2},{4,5},{5,4},{6,7},{7,6},{8,9},{9,8},{10,11... | collective-permute-start | bytes 1179656 | tf_op jit(solution)/shard_map/ppermute | solution.py:366
  127.9 23.6 %collective-permute-start.23 = (f32[2,2,96,256]{3,2,1,0:T(8,128)S(1)}, f32[2,2,96,256]{3,2,1,0:T(8,128)S(1)}, u32[]{:S(2)}, u32[]{:S(2)}) collective-permute-start(f32[2,2,96,256]{3,2,1,0:T(8,128)S(1)} %add.33.sums_ref), channel_id=1, source_target_pairs={{0,2},{1,3},{2,0},{3,1},{4,6},{5,7},{6,4},{7,5},{8,10},{9,11},{10,... | collective-permute-start | bytes 1179656 | tf_op jit(solution)/shard_map/ppermute | solution.py:359
  132.5 20.3 %collective-permute-start.24 = (f32[2,2,96,256]{3,2,1,0:T(8,128)S(1)}, f32[2,2,96,256]{3,2,1,0:T(8,128)S(1)}, u32[]{:S(2)}, u32[]{:S(2)}) collective-permute-start(f32[2,2,96,256]{3,2,1,0:T(8,128)S(1)} %add.34.sums_ref), channel_id=1, source_target_pairs={{0,2},{1,3},{2,0},{3,1},{4,6},{5,7},{6,4},{7,5},{8,10},{9,11},{10,... | collective-permute-start | bytes 1179656 | tf_op jit(solution)/shard_map/ppermute | solution.py:359
  150.9 3.1 %collective-permute-start.25 = (f32[2,192,256]{2,1,0:T(8,128)S(1)}, f32[2,192,256]{2,1,0:T(8,128)S(1)}, u32[]{:S(2)}, u32[]{:S(2)}) collective-permute-start(f32[2,192,256]{2,1,0:T(8,128)S(1)} %get-tuple-element.109.refs_0_), channel_id=1, source_target_pairs={{0,1},{1,0},{2,3},{3,2},{4,5},{5,4},{6,7},{7,6},{8,9},{9,8},{10,11... | collective-permute-start | bytes 1179656 | tf_op jit(solution)/shard_map/ppermute | solution.py:366
  151.0 3.0 %collective-permute-start.26 = (f32[2,192,256]{2,1,0:T(8,128)S(1)}, f32[2,192,256]{2,1,0:T(8,128)S(1)}, u32[]{:S(2)}, u32[]{:S(2)}) collective-permute-start(f32[2,192,256]{2,1,0:T(8,128)S(1)} %get-tuple-element.110.refs_1_), channel_id=1, source_target_pairs={{0,1},{1,0},{2,3},{3,2},{4,5},{5,4},{6,7},{7,6},{8,9},{9,8},{10,11... | collective-permute-start | bytes 1179656 | tf_op jit(solution)/shard_map/ppermute | solution.py:366
  152.2 1.5 collective-permute-start.27
  152.4 1.7 collective-permute-start.28
  153.5 1.5 collective-permute-start.29
  153.7 1.5 collective-permute-start.30
  (1 other events, 6.2 us)
